TPU v7x, 32 devices: a whole 2x2x4 slice. The times are simulated.
32 devices in a mesh: grp: 4 (over y, x), key: 8 (over z, core).
Axes of the slice: x: 2, y: 2, z: 4, core: 2. Of those that a mesh axis runs over, the one named last changes fastest.
Arguments:
- tokens: bfloat16 [8, 2048, 1024], P('grp', 'key'), may hold values from -6 to 6
- token_docs: int32 [8, 2048], P('grp', 'key'), may hold values from 0 to 7, as said below
- memory_docs: int32 [8, 2048], P('grp', 'key'), may hold values from 0 to 3
- memory_resets: int32 [8], P('grp'), may hold values 0 or 1
- memory_keys: bfloat16 [8, 2048, 1024], P('grp', 'key'), may hold values from -6 to 6
- memory_values: bfloat16 [8, 2048, 1024], P('grp', 'key'), may hold values from -6 to 6
- attn_gain1: bfloat16 [1024], P(('grp', 'key')), may hold values from 0.5 to 1.5
- query_weight1: bfloat16 [1024, 1024], P(('grp', 'key')), may hold values from -0.1875 to 0.1875
- key_weight1: bfloat16 [1024, 1024], P(('grp', 'key')), may hold values from -0.1875 to 0.1875
- value_weight1: bfloat16 [1024, 1024], P(('grp', 'key')), may hold values from -0.1875 to 0.1875
- out_weight1: bfloat16 [1024, 1024], P(('grp', 'key')), may hold values from -0.75 to 0.75
- ffn_gain1: bfloat16 [1024], P(('grp', 'key')), may hold values from 0.5 to 1.5
- gate_weight1: bfloat16 [1024, 2816], P(('grp', 'key')), may hold values from -0.1875 to 0.1875
- up_weight1: bfloat16 [1024, 2816], P(('grp', 'key')), may hold values from -0.1875 to 0.1875
- down_weight1: bfloat16 [2816, 1024], P(('grp', 'key')), may hold values from -0.109375 to 0.109375
- attn_gain2: bfloat16 [1024], P(('grp', 'key')), may hold values from 0.5 to 1.5
- second_query_weight: bfloat16 [1024, 1024], P(('grp', 'key')), may hold values from -0.1875 to 0.1875
- key_weight2: bfloat16 [1024, 1024], P(('grp', 'key')), may hold values from -0.1875 to 0.1875
- value_weight2: bfloat16 [1024, 1024], P(('grp', 'key')), may hold values from -0.1875 to 0.1875
- out_weight2: bfloat16 [1024, 1024], P(('grp', 'key')), may hold values from -0.75 to 0.75
- ffn_gain2: bfloat16 [1024], P(('grp', 'key')), may hold values from 0.5 to 1.5
- gate_weight2: bfloat16 [1024, 2816], P(('grp', 'key')), may hold values from -0.1875 to 0.1875
- up_weight2: bfloat16 [1024, 2816], P(('grp', 'key')), may hold values from -0.1875 to 0.1875
- down_weight2: bfloat16 [2816, 1024], P(('grp', 'key')), may hold values from -0.109375 to 0.109375
- cotangent: bfloat16 [8, 2048, 1024], P('grp', 'key'), may hold values from -6 to 6
Outputs:
- output: bfloat16 [8, 2048, 1024], P('grp', 'key')
- grad_tokens: float32 [8, 2048, 1024], P('grp', 'key')
- grad_attn_gain1: float32 [1024], P(('grp', 'key'))
- grad_query_weight1: float32 [1024, 1024], P(('grp', 'key'))
- grad_key_weight1: float32 [1024, 1024], P(('grp', 'key'))
- grad_value_weight1: float32 [1024, 1024], P(('grp', 'key'))
- grad_out_weight1: float32 [1024, 1024], P(('grp', 'key'))
- grad_ffn_gain1: float32 [1024], P(('grp', 'key'))
- grad_gate_weight1: float32 [1024, 2816], P(('grp', 'key'))
- grad_up_weight1: float32 [1024, 2816], P(('grp', 'key'))
- grad_down_weight1: float32 [2816, 1024], P(('grp', 'key'))
- grad_attn_gain2: float32 [1024], P(('grp', 'key'))
- grad_query_weight2: float32 [1024, 1024], P(('grp', 'key'))
- grad_key_weight2: float32 [1024, 1024], P(('grp', 'key'))
- grad_value_weight2: float32 [1024, 1024], P(('grp', 'key'))
- grad_out_weight2: float32 [1024, 1024], P(('grp', 'key'))
- grad_ffn_gain2: float32 [1024], P(('grp', 'key'))
- grad_gate_weight2: float32 [1024, 2816], P(('grp', 'key'))
- grad_up_weight2: float32 [1024, 2816], P(('grp', 'key'))
- grad_down_weight2: float32 [2816, 1024], P(('grp', 'key'))
Inputs may be any that keep to these rules, and one draw needn't show every extreme that they name: `token_docs`: in every segment the numbers start at 0 and rise by 0 or 1 from one token to the next; among each group's 2 consecutive segments, one holds a single document, and every other segment holds exactly 8 documents.
All inputs are finite; a program needn't handle non-finite values. No bound on the sum of `memory_resets` on one device may be relied on, other than what follows from the above.
Results may differ from a plain program's by a relative error of at most 0.03.
Values may be sent and summed in bfloat16 or wider, within the bound.
A program may use at most 512 MiB of HBM per device.

v0:
```python
import jax
import jax.numpy as jnp
from jax import lax
from jax.sharding import PartitionSpec as P

HEADS = 8


EPS = 1e-05
NEG = -1e30


def norm_forward(values, gain_vec):
    inverse = lax.rsqrt(jnp.mean(values * values, axis=-1, keepdims=True) + EPS)
    return (values * inverse * gain_vec, inverse)


def norm_backward(values, gain_vec, inverse, grad_normed):
    grad_gain = jnp.sum(grad_normed * values * inverse, axis=(0, 1))
    scaled = grad_normed * gain_vec
    grad_values = inverse * scaled - values * inverse**3 * jnp.mean(
        scaled * values, axis=-1, keepdims=True
    )
    return (grad_values, grad_gain)


def project(input_operand, weight_matrix):
    return jnp.dot(input_operand, weight_matrix, preferred_element_type=jnp.float32)


def project_back(gradient_row_block, weight_matrix):
    return jnp.einsum(
        "tzu,ku->tzk", gradient_row_block, weight_matrix, preferred_element_type=jnp.float32
    )


def outer_sum(input_arrays, gradient_reduced_precision):
    return jnp.einsum(
        "zhp,zhv->pv", input_arrays, gradient_reduced_precision, preferred_element_type=jnp.float32
    )


def split_heads(rows):
    return rows.reshape(rows.shape[0], rows.shape[1], HEADS, rows.shape[2] // HEADS)


def fetch_weights(shards):
    return (
        lax.all_gather(shards[0], ("grp", "key"), axis=0, tiled=True),
        lax.all_gather(shards[1], ("grp", "key"), axis=0, tiled=True),
        lax.all_gather(shards[2], ("grp", "key"), axis=0, tiled=True),
        lax.all_gather(shards[3], ("grp", "key"), axis=0, tiled=True),
        lax.all_gather(shards[4], ("grp", "key"), axis=0, tiled=True),
        lax.all_gather(shards[5], ("grp", "key"), axis=0, tiled=True),
        lax.all_gather(shards[6], ("grp", "key"), axis=0, tiled=True),
        lax.all_gather(shards[7], ("grp", "key"), axis=0, tiled=True),
        lax.all_gather(shards[8], ("grp", "key"), axis=0, tiled=True),
    )


def refetch_weights(shards):
    return (
        lax.all_gather(shards[0], ("grp", "key"), axis=0, tiled=True),
        lax.all_gather(shards[1], ("grp", "key"), axis=0, tiled=True),
        lax.all_gather(shards[2], ("grp", "key"), axis=0, tiled=True),
        lax.all_gather(shards[3], ("grp", "key"), axis=0, tiled=True),
        lax.all_gather(shards[4], ("grp", "key"), axis=0, tiled=True),
        lax.all_gather(shards[5], ("grp", "key"), axis=0, tiled=True),
        lax.all_gather(shards[6], ("grp", "key"), axis=0, tiled=True),
        lax.all_gather(shards[7], ("grp", "key"), axis=0, tiled=True),
        lax.all_gather(shards[8], ("grp", "key"), axis=0, tiled=True),
    )


def reduce_gradient_sums(terms):
    return (
        lax.psum_scatter(terms[0], ("grp", "key"), scatter_dimension=0, tiled=True),
        lax.psum_scatter(terms[1], ("grp", "key"), scatter_dimension=0, tiled=True),
        lax.psum_scatter(terms[2], ("grp", "key"), scatter_dimension=0, tiled=True),
        lax.psum_scatter(terms[3], ("grp", "key"), scatter_dimension=0, tiled=True),
        lax.psum_scatter(terms[4], ("grp", "key"), scatter_dimension=0, tiled=True),
        lax.psum_scatter(terms[5], ("grp", "key"), scatter_dimension=0, tiled=True),
        lax.psum_scatter(terms[6], ("grp", "key"), scatter_dimension=0, tiled=True),
        lax.psum_scatter(terms[7], ("grp", "key"), scatter_dimension=0, tiled=True),
        lax.psum_scatter(terms[8], ("grp", "key"), scatter_dimension=0, tiled=True),
    )


def head_scores(query_all, key_block, allowed):
    head_size = query_all.shape[2] // HEADS
    raw_scores = jnp.einsum(
        "sqhd,skhd->shqk",
        split_heads(query_all),
        split_heads(key_block),
        preferred_element_type=jnp.float32,
    ) * head_size ** (-0.5)
    return jnp.where(allowed[:, None], raw_scores, NEG)


def attend_forward(query_all, key_block, value_block, allowed):
    scores = head_scores(query_all, key_block, allowed)
    row_top = lax.pmax(jnp.max(scores, axis=3).astype(jnp.bfloat16), "key").astype(jnp.float32)
    exp_scores = jnp.where(allowed[:, None], jnp.exp(scores - row_top[..., None]), 0.0)
    row_total = lax.psum(jnp.sum(exp_scores, axis=3).astype(jnp.bfloat16), "key").astype(
        jnp.float32
    )
    probability = exp_scores / row_total[..., None]
    partial_value = jnp.einsum(
        "shqk,skhd->sqhd",
        probability.astype(jnp.bfloat16),
        split_heads(value_block),
        preferred_element_type=jnp.float32,
    )
    partial_value = partial_value.reshape(query_all.shape)
    attended = lax.psum_scatter(
        partial_value.astype(jnp.bfloat16), "key", scatter_dimension=1, tiled=True
    ).astype(jnp.float32)
    return (attended, row_top, row_total)


def layer_forward(stream, full_weights, allowed, extra_keys, extra_values):
    gain_a, query_w, key_w, value_w, out_w, gain_b, gate_w, up_w, down_w = full_weights
    normed, first_inverse_factor = norm_forward(stream, gain_a.astype(jnp.float32))
    normed_low = normed.astype(jnp.bfloat16)
    query_low = project(normed_low, query_w).astype(jnp.bfloat16)
    key_low = project(normed_low, key_w).astype(jnp.bfloat16)
    value_low = project(normed_low, value_w).astype(jnp.bfloat16)
    query_all = lax.all_gather(query_low, "key", axis=1, tiled=True)
    if extra_keys is None:
        key_block = key_low
        value_block = value_low
    else:
        key_block = jnp.concatenate((key_low, extra_keys), axis=1)
        value_block = jnp.concatenate((value_low, extra_values), axis=1)
    attended, row_top, row_total = attend_forward(query_all, key_block, value_block, allowed)
    attended_low = attended.astype(jnp.bfloat16)
    mixed_stream = stream + project(attended_low, out_w)
    normed_ff, inverse_b = norm_forward(mixed_stream, gain_b.astype(jnp.float32))
    normed_ff_low = normed_ff.astype(jnp.bfloat16)
    gate_value = project(normed_ff_low, gate_w)
    up_value = project(normed_ff_low, up_w)
    activated_low = (gate_value * jax.nn.sigmoid(gate_value) * up_value).astype(jnp.bfloat16)
    result = mixed_stream + project(activated_low, down_w)
    kept_state = (
        stream,
        first_inverse_factor,
        normed_low,
        key_block,
        value_block,
        query_all,
        row_top,
        row_total,
        attended_low,
        mixed_stream,
        inverse_b,
        normed_ff_low,
        gate_value,
        up_value,
        activated_low,
    )
    return (result, kept_state)


def layer_backward(grad_result, full_weights, kept_state, allowed):
    gain_a, query_w, key_w, value_w, out_w, gain_b, gate_w, up_w, down_w = full_weights
    (
        stream,
        first_inverse_factor,
        normed_low,
        key_block,
        value_block,
        query_all,
        row_top,
        row_total,
        attended_low,
        mixed_stream,
        inverse_b,
        normed_ff_low,
        gate_value,
        up_value,
        activated_low,
    ) = kept_state
    own_rows = stream.shape[1]
    branch_low = grad_result.astype(jnp.bfloat16)
    grad_down = outer_sum(activated_low, branch_low)
    grad_act = project_back(branch_low, down_w)
    sigmoid_gate = jax.nn.sigmoid(gate_value)
    grad_gate = (
        grad_act * up_value * sigmoid_gate * (1.0 + gate_value * (1.0 - sigmoid_gate))
    ).astype(jnp.bfloat16)
    grad_up_low = (grad_act * gate_value * sigmoid_gate).astype(jnp.bfloat16)
    grad_gate_w = outer_sum(normed_ff_low, grad_gate)
    grad_up_w = outer_sum(normed_ff_low, grad_up_low)
    grad_normed_ff = project_back(grad_gate, gate_w) + project_back(grad_up_low, up_w)
    grad_mixed_norm, grad_gain_b = norm_backward(
        mixed_stream, gain_b.astype(jnp.float32), inverse_b, grad_normed_ff
    )
    grad_mixed = grad_result + grad_mixed_norm
    attn_low = grad_mixed.astype(jnp.bfloat16)
    grad_out_w = outer_sum(attended_low, attn_low)
    grad_attended = project_back(attn_low, out_w).astype(jnp.bfloat16)
    grad_all = lax.all_gather(grad_attended, "key", axis=1, tiled=True)
    scores = head_scores(query_all, key_block, allowed)
    probability = (
        jnp.where(allowed[:, None], jnp.exp(scores - row_top[..., None]), 0.0)
        / row_total[..., None]
    )
    grad_heads = split_heads(grad_all)
    grad_probs = jnp.einsum(
        "sqhd,skhd->shqk", grad_heads, split_heads(value_block), preferred_element_type=jnp.float32
    )
    row_delta = lax.psum(
        jnp.sum(probability * grad_probs, axis=3).astype(jnp.bfloat16), "key"
    ).astype(jnp.float32)
    grad_scores = (probability * (grad_probs - row_delta[..., None])).astype(jnp.bfloat16)
    score_scale = (query_all.shape[2] // HEADS) ** (-0.5)
    query_part = (
        jnp.einsum(
            "shqk,skhd->sqhd",
            grad_scores,
            split_heads(key_block),
            preferred_element_type=jnp.float32,
        ).reshape(query_all.shape)
        * score_scale
    )
    grad_query = lax.psum_scatter(
        query_part.astype(jnp.bfloat16), "key", scatter_dimension=1, tiled=True
    )
    own_scores = grad_scores[..., :own_rows]
    grad_key = (
        jnp.einsum(
            "shqk,sqhd->skhd",
            own_scores,
            split_heads(query_all),
            preferred_element_type=jnp.float32,
        ).reshape(stream.shape)
        * score_scale
    ).astype(jnp.bfloat16)
    own_probs = probability.astype(jnp.bfloat16)[..., :own_rows]
    grad_value = (
        jnp.einsum("shqk,sqhd->skhd", own_probs, grad_heads, preferred_element_type=jnp.float32)
        .reshape(stream.shape)
        .astype(jnp.bfloat16)
    )
    grad_query_w = outer_sum(normed_low, grad_query)
    grad_key_w = outer_sum(normed_low, grad_key)
    grad_value_w = outer_sum(normed_low, grad_value)
    grad_normed = (
        project_back(grad_query, query_w)
        + project_back(grad_key, key_w)
        + project_back(grad_value, value_w)
    )
    grad_stream_norm, grad_gain_a = norm_backward(
        stream, gain_a.astype(jnp.float32), first_inverse_factor, grad_normed
    )
    grad_stream = grad_mixed + grad_stream_norm
    terms = (
        grad_gain_a,
        grad_query_w,
        grad_key_w,
        grad_value_w,
        grad_out_w,
        grad_gain_b,
        grad_gate_w,
        grad_up_w,
        grad_down,
    )
    return (grad_stream, terms)


def local(
    tokens,
    token_docs,
    memory_docs,
    memory_resets,
    memory_keys,
    memory_values,
    attn_gain1,
    query_weight1,
    key_weight1,
    value_weight1,
    out_weight1,
    ffn_gain1,
    gate_weight1,
    up_weight1,
    down_weight1,
    attn_gain2,
    second_query_weight,
    key_weight2,
    value_weight2,
    out_weight2,
    ffn_gain2,
    gate_weight2,
    up_weight2,
    down_weight2,
    cotangent,
):
    first_shards = (
        attn_gain1,
        query_weight1,
        key_weight1,
        value_weight1,
        out_weight1,
        ffn_gain1,
        gate_weight1,
        up_weight1,
        down_weight1,
    )
    second_shards = (
        attn_gain2,
        second_query_weight,
        key_weight2,
        value_weight2,
        out_weight2,
        ffn_gain2,
        gate_weight2,
        up_weight2,
        down_weight2,
    )
    docs_all = lax.all_gather(token_docs, "key", axis=1, tiled=True)
    own_rows = tokens.shape[1]
    query_place = jnp.arange(docs_all.shape[1], dtype=jnp.int32)
    key_place = lax.axis_index("key") * own_rows + jnp.arange(own_rows, dtype=jnp.int32)
    local_allowed = (key_place[None, None, :] <= query_place[None, :, None]) & (
        token_docs[:, None, :] == docs_all[:, :, None]
    )
    memory_allowed = (memory_docs[:, None, :] == docs_all[:, :, None]) & (
        memory_resets[:, None, None] == 0
    )
    both_allowed = jnp.concatenate((local_allowed, memory_allowed), axis=2)
    stream = tokens.astype(jnp.float32)
    first_full = fetch_weights(first_shards)
    middle, first_state = layer_forward(stream, first_full, local_allowed, None, None)
    second_full = fetch_weights(second_shards)
    result, second_state = layer_forward(
        middle, second_full, both_allowed, memory_keys, memory_values
    )
    second_full = refetch_weights(second_shards)
    grad_middle, second_terms = layer_backward(
        cotangent.astype(jnp.float32), second_full, second_state, both_allowed
    )
    second_grads = reduce_gradient_sums(second_terms)
    first_full = refetch_weights(first_shards)
    grad_stream, first_terms = layer_backward(grad_middle, first_full, first_state, local_allowed)
    first_grads = reduce_gradient_sums(first_terms)
    return (
        result.astype(jnp.bfloat16),
        grad_stream,
        first_grads[0],
        first_grads[1],
        first_grads[2],
        first_grads[3],
        first_grads[4],
        first_grads[5],
        first_grads[6],
        first_grads[7],
        first_grads[8],
        second_grads[0],
        second_grads[1],
        second_grads[2],
        second_grads[3],
        second_grads[4],
        second_grads[5],
        second_grads[6],
        second_grads[7],
        second_grads[8],
    )


def solution(mesh):
    in_specs = (
        P("grp", "key", None),
        P("grp", "key"),
        P("grp", "key"),
        P("grp"),
        P("grp", "key", None),
        P("grp", "key", None),
        P(("grp", "key")),
        P(("grp", "key"), None),
        P(("grp", "key"), None),
        P(("grp", "key"), None),
        P(("grp", "key"), None),
        P(("grp", "key")),
        P(("grp", "key"), None),
        P(("grp", "key"), None),
        P(("grp", "key"), None),
        P(("grp", "key")),
        P(("grp", "key"), None),
        P(("grp", "key"), None),
        P(("grp", "key"), None),
        P(("grp", "key"), None),
        P(("grp", "key")),
        P(("grp", "key"), None),
        P(("grp", "key"), None),
        P(("grp", "key"), None),
        P("grp", "key", None),
    )
    out_specs = (
        P("grp", "key", None),
        P("grp", "key", None),
        P(("grp", "key")),
        P(("grp", "key"), None),
        P(("grp", "key"), None),
        P(("grp", "key"), None),
        P(("grp", "key"), None),
        P(("grp", "key")),
        P(("grp", "key"), None),
        P(("grp", "key"), None),
        P(("grp", "key"), None),
        P(("grp", "key")),
        P(("grp", "key"), None),
        P(("grp", "key"), None),
        P(("grp", "key"), None),
        P(("grp", "key"), None),
        P(("grp", "key")),
        P(("grp", "key"), None),
        P(("grp", "key"), None),
        P(("grp", "key"), None),
    )
    return jax.shard_map(local, mesh=mesh, in_specs=in_specs, out_specs=out_specs, check_vma=False)
```

profile of v0, /device:TPU:1, one launch (start us, length us, event | category | flops | bytes accessed | tf_op | source)
XLA Modules:
  0.0 4383.5 jit_solution(6407500491144493390)
XLA Ops:
  133.8 77.8 %all-gather.23.cloned.1.call-done = bf16[2,2048,1024]{2,1,0:T(8,128)(2,1)} async-done(((bf16[2,256,1024]{2,1,0:T(8,128)(2,1)}), bf16[2,2048,1024]{2,1,0:T(8,128)(2,1)}) %all-gather.23.cloned.1.call-update) | async-done | bytes 8388624 | tf_op jit(solution)/shard_map/all_gather | solution.py:128
  465.3 88.2 %reduce-scatter.19.cloned.1.call-done = bf16[2,256,1024]{1,2,0:T(8,128)(2,1)} async-done(((bf16[2,2048,1024]{1,2,0:T(8,128)(2,1)}), bf16[2,256,1024]{1,2,0:T(8,128)(2,1)}) %reduce-scatter.19.cloned.1.call-update) | async-done | bytes 1048592 | tf_op jit(solution)/shard_map/reduce_scatter | solution.py:115
  559.6 65.1 %all-gather.29.cloned.1.call-done = bf16[1024,2816]{1,0:T(8,128)(2,1)} async-done(((bf16[32,2816]{1,0:T(8,128)(2,1)}), bf16[1024,2816]{1,0:T(8,128)(2,1)}) %all-gather.29.cloned.1.call-update) | async-done | bytes 5767184 | tf_op jit(solution)/shard_map/all_gather | solution.py:55
  633.3 60.4 %all-gather.31.cloned.1.call-done = bf16[1024,2816]{1,0:T(8,128)(2,1)} async-done(((bf16[32,2816]{1,0:T(8,128)(2,1)}), bf16[1024,2816]{1,0:T(8,128)(2,1)}) %all-gather.31.cloned.1.call-update) | async-done | bytes 5767184 | tf_op jit(solution)/shard_map/all_gather | solution.py:56
  705.2 57.8 %all-gather.33.cloned.1.call-done = bf16[2816,1024]{1,0:T(8,128)(2,1)} async-done(((bf16[88,1024]{1,0:T(8,128)(2,1)}), bf16[2816,1024]{1,0:T(8,128)(2,1)}) %all-gather.33.cloned.1.call-update) | async-done | bytes 5767184 | tf_op jit(solution)/shard_map/all_gather | solution.py:57
  770.7 50.5 %all-gather.37.cloned.1.call-done = bf16[1024,1024]{1,0:T(8,128)(2,1)} async-done(((bf16[32,1024]{1,0:T(8,128)(2,1)}), bf16[1024,1024]{1,0:T(8,128)(2,1)}) %all-gather.37.cloned.1.call-update) | async-done | bytes 2097168 | tf_op jit(solution)/shard_map/all_gather | solution.py:50
  826.7 52.9 %all-gather.41.cloned.1.call-done = bf16[1024,1024]{1,0:T(8,128)(2,1)} async-done(((bf16[32,1024]{1,0:T(8,128)(2,1)}), bf16[1024,1024]{1,0:T(8,128)(2,1)}) %all-gather.41.cloned.1.call-update) | async-done | bytes 2097168 | tf_op jit(solution)/shard_map/all_gather | solution.py:51
  888.3 73.7 %all-gather.39.cloned.1.call-done = bf16[2,2048,1024]{2,1,0:T(8,128)(2,1)} async-done(((bf16[2,256,1024]{2,1,0:T(8,128)(2,1)}), bf16[2,2048,1024]{2,1,0:T(8,128)(2,1)}) %all-gather.39.cloned.1.call-update) | async-done | bytes 8388624 | tf_op jit(solution)/shard_map/all_gather | solution.py:128
  1246.1 49.8 %all-gather.43.cloned.1.call-done = bf16[1024,1024]{1,0:T(8,128)(2,1)} async-done(((bf16[32,1024]{1,0:T(8,128)(2,1)}), bf16[1024,1024]{1,0:T(8,128)(2,1)}) %all-gather.43.cloned.1.call-update) | async-done | bytes 2097168 | tf_op jit(solution)/shard_map/all_gather | solution.py:53
  1295.9 88.1 %reduce-scatter.21.cloned.1.call-done = bf16[2,256,1024]{1,2,0:T(8,128)(2,1)} async-done(((bf16[2,2048,1024]{1,2,0:T(8,128)(2,1)}), bf16[2,256,1024]{1,2,0:T(8,128)(2,1)}) %reduce-scatter.21.cloned.1.call-update) | async-done | bytes 1048592 | tf_op jit(solution)/shard_map/reduce_scatter | solution.py:115
  1390.5 64.7 %all-gather.47.cloned.1.call-done = bf16[1024,2816]{1,0:T(8,128)(2,1)} async-done(((bf16[32,2816]{1,0:T(8,128)(2,1)}), bf16[1024,2816]{1,0:T(8,128)(2,1)}) %all-gather.47.cloned.1.call-update) | async-done | bytes 5767184 | tf_op jit(solution)/shard_map/all_gather | solution.py:56
  1463.7 60.5 %all-gather.45.cloned.1.call-done = bf16[1024,2816]{1,0:T(8,128)(2,1)} async-done(((bf16[32,2816]{1,0:T(8,128)(2,1)}), bf16[1024,2816]{1,0:T(8,128)(2,1)}) %all-gather.45.cloned.1.call-update) | async-done | bytes 5767184 | tf_op jit(solution)/shard_map/all_gather | solution.py:55
  1549.8 81.1 %all-gather.51.cloned.1.call-done = bf16[2,2048,1024]{2,1,0:T(8,128)(2,1)} async-done(((bf16[2,256,1024]{2,1,0:T(8,128)(2,1)}), bf16[2,2048,1024]{2,1,0:T(8,128)(2,1)}) %all-gather.51.cloned.1.call-update) | async-done | bytes 8388624 | tf_op jit(solution)/shard_map/all_gather | solution.py:202
  1642.8 59.1 %multiply_reduce_fusion = (bf16[2,8,2048]{2,1,0:T(8,128)(2,1)}, f32[2,8,2048,512]{2,3,1,0:T(8,128)}) fusion(f32[2,8,2048]{2,1,0:T(8,128)S(1)} %convert_element_type.240, f32[2,8,2048]{2,1,0:T(8,128)S(1)} %convert_element_type.238, f32[2,8,2048,512]{2,3,1,0:T(8,128)} %get-tuple-element.60, pred[2,2048,512]{1,2,0:T(8,128)(4,1)S(1)} %pad_add_fusion, ...), kind=kOutput, calls=%fused_computation.1 | convolution fusion | flops 4416569344 | bytes 147128320 | tf_op jit(solution)/shard_map/sqhd,skhd->shqk/dot_general | solution.py:209
  1701.9 50.2 %all-reduce.25.cloned.1.call-done = bf16[2,8,2048]{2,1,0:T(8,128)(2,1)} async-done(((bf16[2,8,2048]{2,1,0:T(8,128)(2,1)}), bf16[2,8,2048]{2,1,0:T(8,128)(2,1)}) %all-reduce.25.cloned.1.call-update) | async-done | bytes 65552 | tf_op jit(solution)/shard_map/psum | solution.py:212
  1753.0 53.4 %multiply_convert_fusion = bf16[2,8,2048,512]{2,3,1,0:T(8,128)(2,1)} fusion(f32[2,8,2048,512]{2,3,1,0:T(8,128)} %get-tuple-element.65, f32[2,8,2048]{2,1,0:T(8,128)S(1)} %convert_element_type.255, f32[2,8,2048]{2,1,0:T(8,128)S(1)} %convert_element_type.240, f32[2,8,2048]{2,1,0:T(8,128)S(1)} %convert_element_type.238, f32[2,8,2048,512]{2,3,1,0:T(8,128)} %get-tuple-element.60, ...), kind=kLoop, calls=%fused_computation | loop fusion | flops 134217728 | bytes 170262528 | tf_op jit(solution)/shard_map/convert_element_type | solution.py:215
  1863.1 60.7 %reduce-scatter.23.cloned.1.call-done = bf16[2,256,1024]{2,1,0:T(8,128)(2,1)} async-done(((bf16[2,2048,1024]{2,1,0:T(8,128)(2,1)}), bf16[2,256,1024]{2,1,0:T(8,128)(2,1)}) %reduce-scatter.23.cloned.1.call-update) | async-done | bytes 1048592 | tf_op jit(solution)/shard_map/reduce_scatter | solution.py:226
  1952.3 83.0 %all-gather.53.cloned.1.call-done = bf16[2,2048,1024]{2,1,0:T(8,128)(2,1)} async-done(((bf16[2,256,1024]{2,1,0:T(8,128)(2,1)}), bf16[2,2048,1024]{2,1,0:T(8,128)(2,1)}) %all-gather.53.cloned.1.call-update) | async-done | bytes 8388624 | tf_op jit(solution)/shard_map/all_gather | solution.py:202
  2078.3 50.3 %all-reduce.27.cloned.1.call-done = bf16[2,8,2048]{2,1,0:T(8,128)(2,1)} async-done(((bf16[2,8,2048]{2,1,0:T(8,128)(2,1)}), bf16[2,8,2048]{2,1,0:T(8,128)(2,1)}) %all-reduce.27.cloned.1.call-update) | async-done | bytes 65552 | tf_op jit(solution)/shard_map/psum | solution.py:212
  2411.4 142.4 %reduce-scatter.45.cloned.1.call-done = f32[32,1024]{1,0:T(8,128)} async-done(((f32[1024,1024]{1,0:T(8,128)}), f32[32,1024]{1,0:T(8,128)}) %reduce-scatter.45.cloned.1.call-update) | async-done | bytes 131088 | tf_op jit(solution)/shard_map/reduce_scatter | solution.py:80
  2553.8 161.1 %reduce-scatter.53.cloned.1.call-done = f32[88,1024]{1,0:T(8,128)} async-done(((f32[2816,1024]{1,0:T(8,128)}), f32[88,1024]{1,0:T(8,128)}) %reduce-scatter.53.cloned.1.call-update) | async-done | bytes 360464 | tf_op jit(solution)/shard_map/reduce_scatter | solution.py:85
  2715.0 161.0 %reduce-scatter.49.cloned.1.call-done = f32[32,2816]{1,0:T(8,128)} async-done(((f32[1024,2816]{1,0:T(8,128)}), f32[32,2816]{1,0:T(8,128)}) %reduce-scatter.49.cloned.1.call-update) | async-done | bytes 360464 | tf_op jit(solution)/shard_map/reduce_scatter | solution.py:83
  2876.0 161.0 %reduce-scatter.51.cloned.1.call-done = f32[32,2816]{1,0:T(8,128)} async-done(((f32[1024,2816]{1,0:T(8,128)}), f32[32,2816]{1,0:T(8,128)}) %reduce-scatter.51.cloned.1.call-update) | async-done | bytes 360464 | tf_op jit(solution)/shard_map/reduce_scatter | solution.py:84
  3036.9 142.9 %reduce-scatter.43.cloned.1.call-done = f32[32,1024]{1,0:T(8,128)} async-done(((f32[1024,1024]{1,0:T(8,128)}), f32[32,1024]{1,0:T(8,128)}) %reduce-scatter.43.cloned.1.call-update) | async-done | bytes 131088 | tf_op jit(solution)/shard_map/reduce_scatter | solution.py:79
  3179.9 142.7 %reduce-scatter.33.cloned.1.call-done = f32[32,1024]{1,0:T(8,128)} async-done(((f32[1024,1024]{1,0:T(8,128)}), f32[32,1024]{1,0:T(8,128)}) %reduce-scatter.33.cloned.1.call-update) | async-done | bytes 131088 | tf_op jit(solution)/shard_map/reduce_scatter | solution.py:81
  3322.5 142.2 %reduce-scatter.41.cloned.1.call-done = f32[32,1024]{1,0:T(8,128)} async-done(((f32[1024,1024]{1,0:T(8,128)}), f32[32,1024]{1,0:T(8,128)}) %reduce-scatter.41.cloned.1.call-update) | async-done | bytes 131088 | tf_op jit(solution)/shard_map/reduce_scatter | solution.py:78
  3464.7 161.3 %reduce-scatter.39.cloned.1.call-done = f32[88,1024]{1,0:T(8,128)} async-done(((f32[2816,1024]{1,0:T(8,128)}), f32[88,1024]{1,0:T(8,128)}) %reduce-scatter.39.cloned.1.call-update) | async-done | bytes 360464 | tf_op jit(solution)/shard_map/reduce_scatter | solution.py:85
  3626.1 162.2 %reduce-scatter.35.cloned.1.call-done = f32[32,2816]{1,0:T(8,128)} async-done(((f32[1024,2816]{1,0:T(8,128)}), f32[32,2816]{1,0:T(8,128)}) %reduce-scatter.35.cloned.1.call-update) | async-done | bytes 360464 | tf_op jit(solution)/shard_map/reduce_scatter | solution.py:83
  3788.2 161.3 %reduce-scatter.37.cloned.1.call-done = f32[32,2816]{1,0:T(8,128)} async-done(((f32[1024,2816]{1,0:T(8,128)}), f32[32,2816]{1,0:T(8,128)}) %reduce-scatter.37.cloned.1.call-update) | async-done | bytes 360464 | tf_op jit(solution)/shard_map/reduce_scatter | solution.py:84
  3949.5 142.7 %reduce-scatter.31.cloned.1.call-done = f32[32,1024]{1,0:T(8,128)} async-done(((f32[1024,1024]{1,0:T(8,128)}), f32[32,1024]{1,0:T(8,128)}) %reduce-scatter.31.cloned.1.call-update) | async-done | bytes 131088 | tf_op jit(solution)/shard_map/reduce_scatter | solution.py:80
  4092.2 142.4 %reduce-scatter.29.cloned.1.call-done = f32[32,1024]{1,0:T(8,128)} async-done(((f32[1024,1024]{1,0:T(8,128)}), f32[32,1024]{1,0:T(8,128)}) %reduce-scatter.29.cloned.1.call-update) | async-done | bytes 131088 | tf_op jit(solution)/shard_map/reduce_scatter | solution.py:79
  4234.7 142.1 %reduce-scatter.27.cloned.1.call-done = f32[32,1024]{1,0:T(8,128)} async-done(((f32[1024,1024]{1,0:T(8,128)}), f32[32,1024]{1,0:T(8,128)}) %reduce-scatter.27.cloned.1.call-update) | async-done | bytes 131088 | tf_op jit(solution)/shard_map/reduce_scatter | solution.py:78
  (364 shorter events, 1175.5 us)
Async XLA Ops:
  8.7 202.8 %all-gather.23.cloned.1.call-start = ((), (), s32[]{:S(2)}) async-start(), calls=%async_computation.20 | async-start | bytes 9437184 | tf_op jit(solution)/shard_map/all_gather | solution.py:128
  74.3 216.3 %all-reduce.17.cloned.1.call-start = ((), (), s32[]{:S(2)}) async-start(), calls=%async_computation.22 | async-start | bytes 131072 | tf_op jit(solution)/shard_map/pmax | solution.py:102
  307.8 245.7 %reduce-scatter.19.cloned.1.call-start = ((), (), s32[]{:S(2)}) async-start(), calls=%async_computation.24 | async-start | bytes 9437184 | tf_op jit(solution)/shard_map/reduce_scatter | solution.py:115
  424.3 200.4 %all-gather.29.cloned.1.call-start = ((), (), s32[]{:S(2)}) async-start(), calls=%async_computation.26 | async-start | bytes 5947392 | tf_op jit(solution)/shard_map/all_gather | solution.py:55
  425.0 268.7 %all-gather.31.cloned.1.call-start = ((), (), s32[]{:S(2)}) async-start(), calls=%async_computation.27 | async-start | bytes 5947392 | tf_op jit(solution)/shard_map/all_gather | solution.py:56
  425.6 337.3 %all-gather.33.cloned.1.call-start = ((), (), s32[]{:S(2)}) async-start(), calls=%async_computation.28 | async-start | bytes 5947392 | tf_op jit(solution)/shard_map/all_gather | solution.py:57
  426.3 394.9 %all-gather.37.cloned.1.call-start = ((), (), s32[]{:S(2)}) async-start(), calls=%async_computation.30 | async-start | bytes 2162688 | tf_op jit(solution)/shard_map/all_gather | solution.py:50
  426.9 452.7 %all-gather.41.cloned.1.call-start = ((), (), s32[]{:S(2)}) async-start(), calls=%async_computation.32 | async-start | bytes 2162688 | tf_op jit(solution)/shard_map/all_gather | solution.py:51
  427.7 534.3 %all-gather.39.cloned.1.call-start = ((), (), s32[]{:S(2)}) async-start(), calls=%async_computation.31 | async-start | bytes 9437184 | tf_op jit(solution)/shard_map/all_gather | solution.py:128
  825.1 227.1 %all-reduce.21.cloned.1.call-start = ((), (), s32[]{:S(2)}) async-start(), calls=%async_computation.33 | async-start | bytes 131072 | tf_op jit(solution)/shard_map/pmax | solution.py:102
  1076.2 219.7 %all-gather.43.cloned.1.call-start = ((), (), s32[]{:S(2)}) async-start(), calls=%async_computation.36 | async-start | bytes 2162688 | tf_op jit(solution)/shard_map/all_gather | solution.py:53
  1076.9 307.0 %reduce-scatter.21.cloned.1.call-start = ((), (), s32[]{:S(2)}) async-start(), calls=%async_computation.35 | async-start | bytes 9437184 | tf_op jit(solution)/shard_map/reduce_scatter | solution.py:115
  1218.2 236.9 %all-gather.47.cloned.1.call-start = ((), (), s32[]{:S(2)}) async-start(), calls=%async_computation.38 | async-start | bytes 5947392 | tf_op jit(solution)/shard_map/all_gather | solution.py:56
  1219.0 305.3 %all-gather.45.cloned.1.call-start = ((), (), s32[]{:S(2)}) async-start(), calls=%async_computation.37 | async-start | bytes 5947392 | tf_op jit(solution)/shard_map/all_gather | solution.py:55
  1219.7 411.2 %all-gather.51.cloned.1.call-start = ((), (), s32[]{:S(2)}) async-start(), calls=%async_computation.40 | async-start | bytes 9437184 | tf_op jit(solution)/shard_map/all_gather | solution.py:202
  1549.8 202.4 %all-reduce.25.cloned.1.call-start = ((), (), s32[]{:S(2)}) async-start(), calls=%async_computation.41 | async-start | bytes 131072 | tf_op jit(solution)/shard_map/psum | solution.py:212
  1701.9 221.8 %reduce-scatter.23.cloned.1.call-start = ((), (), s32[]{:S(2)}) async-start(), calls=%async_computation.42 | async-start | bytes 9437184 | tf_op jit(solution)/shard_map/reduce_scatter | solution.py:226
  2078.2 217.4 %reduce-scatter.25.cloned.1.call-start = ((), (), s32[]{:S(2)}) async-start(), calls=%async_computation.45 | async-start | bytes 9437184 | tf_op jit(solution)/shard_map/reduce_scatter | solution.py:226
  2181.6 229.8 %reduce-scatter.47.cloned.1.call-start = ((), (), s32[]{:S(2)}) async-start(), calls=%async_computation.56 | async-start | bytes 4325376 | tf_op jit(solution)/shard_map/reduce_scatter | solution.py:81
  2187.7 366.1 %reduce-scatter.45.cloned.1.call-start = ((), (), s32[]{:S(2)}) async-start(), calls=%async_computation.55 | async-start | bytes 4325376 | tf_op jit(solution)/shard_map/reduce_scatter | solution.py:80
  2193.0 522.0 %reduce-scatter.53.cloned.1.call-start = ((), (), s32[]{:S(2)}) async-start(), calls=%async_computation.59 | async-start | bytes 11894784 | tf_op jit(solution)/shard_map/reduce_scatter | solution.py:85
  2202.0 673.9 %reduce-scatter.49.cloned.1.call-start = ((), (), s32[]{:S(2)}) async-start(), calls=%async_computation.57 | async-start | bytes 11894784 | tf_op jit(solution)/shard_map/reduce_scatter | solution.py:83
  2211.0 826.0 %reduce-scatter.51.cloned.1.call-start = ((), (), s32[]{:S(2)}) async-start(), calls=%async_computation.58 | async-start | bytes 11894784 | tf_op jit(solution)/shard_map/reduce_scatter | solution.py:84
  2218.9 961.0 %reduce-scatter.43.cloned.1.call-start = ((), (), s32[]{:S(2)}) async-start(), calls=%async_computation.54 | async-start | bytes 4325376 | tf_op jit(solution)/shard_map/reduce_scatter | solution.py:79
  2223.4 1099.1 %reduce-scatter.33.cloned.1.call-start = ((), (), s32[]{:S(2)}) async-start(), calls=%async_computation.49 | async-start | bytes 4325376 | tf_op jit(solution)/shard_map/reduce_scatter | solution.py:81
  2229.5 1235.2 %reduce-scatter.41.cloned.1.call-start = ((), (), s32[]{:S(2)}) async-start(), calls=%async_computation.53 | async-start | bytes 4325376 | tf_op jit(solution)/shard_map/reduce_scatter | solution.py:78
  2234.6 1391.5 %reduce-scatter.39.cloned.1.call-start = ((), (), s32[]{:S(2)}) async-start(), calls=%async_computation.52 | async-start | bytes 11894784 | tf_op jit(solution)/shard_map/reduce_scatter | solution.py:85
  2242.5 1545.7 %reduce-scatter.35.cloned.1.call-start = ((), (), s32[]{:S(2)}) async-start(), calls=%async_computation.50 | async-start | bytes 11894784 | tf_op jit(solution)/shard_map/reduce_scatter | solution.py:83
  2251.6 1697.9 %reduce-scatter.37.cloned.1.call-start = ((), (), s32[]{:S(2)}) async-start(), calls=%async_computation.51 | async-start | bytes 11894784 | tf_op jit(solution)/shard_map/reduce_scatter | solution.py:84
  2259.6 1832.7 %reduce-scatter.31.cloned.1.call-start = ((), (), s32[]{:S(2)}) async-start(), calls=%async_computation.48 | async-start | bytes 4325376 | tf_op jit(solution)/shard_map/reduce_scatter | solution.py:80
  2280.4 1954.3 %reduce-scatter.29.cloned.1.call-start = ((), (), s32[]{:S(2)}) async-start(), calls=%async_computation.47 | async-start | bytes 4325376 | tf_op jit(solution)/shard_map/reduce_scatter | solution.py:79
  2295.3 2081.5 %reduce-scatter.27.cloned.1.call-start = ((), (), s32[]{:S(2)}) async-start(), calls=%async_computation.46 | async-start | bytes 4325376 | tf_op jit(solution)/shard_map/reduce_scatter | solution.py:78
  (87 other events, 5023.3 us)
Sparse Core Ops, SparseCore 0:
  11.0 59.0 all-gather.20
  130.6 80.8 all-gather.22
  293.9 57.4 all-gather.18
  407.8 57.5 all-gather.26
  467.6 85.8 reduce-scatter.18
  556.4 68.2 all-gather.28
  627.4 66.2 all-gather.30
  696.6 66.2 all-gather.32
  881.1 80.8 all-gather.38
  1055.5 57.4 all-gather.34
  1169.1 68.3 all-gather.48
  1298.0 85.8 reduce-scatter.20
  1386.8 68.2 all-gather.46
  1458.0 66.2 all-gather.44
  1549.9 80.9 all-gather.50
  1835.6 88.0 reduce-scatter.22
  1952.3 82.9 all-gather.52
  2181.7 88.0 reduce-scatter.24
  2272.7 138.7 reduce-scatter.46
  2414.1 139.6 reduce-scatter.44
  2556.7 158.1 reduce-scatter.52
  2717.9 158.0 reduce-scatter.48
  2878.7 158.1 reduce-scatter.50
  3039.8 140.0 reduce-scatter.42
  3182.7 139.7 reduce-scatter.32
  3325.2 139.4 reduce-scatter.40
  3467.5 158.5 reduce-scatter.38
  3628.9 159.2 reduce-scatter.34
  3791.0 158.5 reduce-scatter.36
  3952.4 139.8 reduce-scatter.30
  4095.1 139.5 reduce-scatter.28
  4237.5 139.2 reduce-scatter.26
  (10 shorter events, 522.5 us)
where the time goes:
time: 4400 us; the launch traced here: 4380 us
  waiting for transfers between devices  3520 us (80%)
  matrix products  470 us (11%)
  other arithmetic  176 us (4%)
  local copies, waits for them, and re-layouts  99.3 us (2%)
  blocking collectives  95.3 us (2%)
    reduce_scatter x2, waiting for transfers between devices, reduce_gradient_sums(): lax.psum_scatter(terms[6], ('grp', 'key'), scatter_dimension=0, tiled=True)  323 us
    reduce_scatter x2, waiting for transfers between devices, reduce_gradient_sums(): lax.psum_scatter(terms[8], ('grp', 'key'), scatter_dimension=0, tiled=True)  322 us
    reduce_scatter x2, waiting for transfers between devices, reduce_gradient_sums(): lax.psum_scatter(terms[7], ('grp', 'key'), scatter_dimension=0, tiled=True)  322 us
    reduce_scatter x2, waiting for transfers between devices, reduce_gradient_sums(): lax.psum_scatter(terms[2], ('grp', 'key'), scatter_dimension=0, tiled=True)  285 us
    reduce_scatter x2, waiting for transfers between devices, reduce_gradient_sums(): lax.psum_scatter(terms[3], ('grp', 'key'), scatter_dimension=0, tiled=True)  285 us
    reduce_scatter x2, waiting for transfers between devices, reduce_gradient_sums(): lax.psum_scatter(terms[1], ('grp', 'key'), scatter_dimension=0, tiled=True)  284 us
    reduce_scatter x2, waiting for transfers between devices, reduce_gradient_sums(): lax.psum_scatter(terms[4], ('grp', 'key'), scatter_dimension=0, tiled=True)  191 us
    reduce_scatter x2, waiting for transfers between devices, attend_forward(): lax.psum_scatter(partial_value.astype(jnp.bfloat16), 'key', scatter_dimen...  176 us
  transfers between devices with their start and end apart: 42, of which 41 were waited for; matrix products, arithmetic and copies ran while one was open for 8% of the time, Pallas kernels for 0%

commit v1 on v0

--- a/solution.py
+++ b/solution.py
@@ -1,6 +1,10 @@
+import functools
+
 import jax
 import jax.numpy as jnp
 from jax import lax
+from jax.experimental import pallas as pl
+from jax.experimental.pallas import tpu as pltpu
 from jax.sharding import PartitionSpec as P
 
 HEADS = 8
@@ -268,7 +272,7 @@
     return (grad_stream, terms)
 
 
-def local(
+def gathered_local(
     tokens,
     token_docs,
     memory_docs,
@@ -367,6 +371,988 @@
     )
 
 
+MESH = pl.DeviceIdType.MESH
+ANY = pl.BlockSpec(memory_space=pl.ANY)
+VMEM = pl.BlockSpec(memory_space=pltpu.VMEM)
+LOG2E = 1.4426950408889634
+BLOCK = 256
+LOCAL = 4
+HEAD = 128
+PAIR = 2 * HEAD
+BF = jnp.bfloat16
+F32 = jnp.float32
+
+
+SEND = pltpu.SemaphoreType.DMA
+
+
+def flip(value, change):
+    return lax.rem(value + change, 2)
+
+
+class Place:
+    def __init__(self):
+        self.grp = lax.axis_index("grp")
+        self.key = lax.axis_index("key")
+        self.y, self.x = self.grp // 2, lax.rem(self.grp, 2)
+        self.z, self.core = self.key // 2, lax.rem(self.key, 2)
+        self.rank = lax.rem(self.key, LOCAL)
+        self.seg = self.key // LOCAL
+
+    def chip(self, da, db, dz, core):
+        dx = da * (1 - core) + db * core
+        dy = da * core + db * (1 - core)
+        z = flip(self.z // 2, dz // 2) * 2 + flip(lax.rem(self.z, 2), dz % 2)
+        return flip(self.y, dy) * 2 + flip(self.x, dx), z
+
+    def device(self, da, db, dz):
+        grp, z = self.chip(da, db, dz, self.core)
+        return grp, z * 2 + self.core
+
+    def sibling(self):
+        return self.grp, self.z * 2 + 1 - self.core
+
+
+def remote(src, dst, send, recv, target):
+    return pltpu.make_async_remote_copy(
+        src_ref=src, dst_ref=dst, send_sem=send, recv_sem=recv,
+        device_id=target, device_id_type=MESH,
+    )
+
+
+def local(src, dst, sem):
+    return pltpu.make_async_copy(src, dst, sem)
+
+
+def span(index, size):
+    return pl.ds(pl.multiple_of(index * size, size), size)
+
+
+class RowBlocks:
+    def __init__(self, rows, width):
+        self.shape = (rows, width)
+
+    def whole(self, chips):
+        return (chips * 2 * self.shape[0], self.shape[1])
+
+    def at(self, ref, chip, core):
+        return ref.at[span((chip[0] * LOCAL + chip[1]) * 2 + core, self.shape[0]), :]
+
+
+class PairBlocks(RowBlocks):
+    def whole(self, chips):
+        return (chips * self.shape[0], 2 * self.shape[1])
+
+    def at(self, ref, chip, core):
+        rows, width = self.shape
+        return ref.at[span(chip[0] * LOCAL + chip[1], rows), span(core, width)]
+
+
+class ColumnBlocks(RowBlocks):
+    def __init__(self, rows, width, part):
+        self.shape = (rows, width)
+        self.part = part
+
+    def at(self, ref, chip, core):
+        rows, width = self.shape
+        return ref.at[
+            span((chip[0] * LOCAL + chip[1]) * 2 + core, rows), pl.ds(self.part * width, width)
+        ]
+
+
+class Swap:
+    def __init__(self, arrays, to_heads):
+        self.arrays = arrays
+        self.to_heads = to_heads
+        if to_heads:
+            rows, width = arrays[0].shape
+            self.parts = width // (LOCAL * PAIR)
+            self.outs = [jax.ShapeDtypeStruct((rows * LOCAL, PAIR), BF)] * self.parts
+        else:
+            rows = arrays[0].shape[0] // LOCAL
+            self.parts = len(arrays)
+            self.outs = [jax.ShapeDtypeStruct((rows, self.parts * LOCAL * PAIR), BF)]
+        self.rows = rows
+        self.scratch = [SEND((self.parts, LOCAL)), SEND((self.parts, LOCAL)), SEND((self.parts,))]
+        self.out_specs = [ANY] * len(self.outs)
+
+    def run(self, at, ins, outs, scratch):
+        send, recv, here = scratch
+
+        def copy(part, k):
+            target = lax.rem(at.rank + k, LOCAL)
+            if self.to_heads:
+                src = ins[0].at[:, span(part * LOCAL + target, PAIR)]
+                dst = outs[part].at[span(at.rank, self.rows), :]
+            else:
+                src = ins[part].at[span(target, self.rows), :]
+                dst = outs[0].at[:, span(part * LOCAL + at.rank, PAIR)]
+            if k == 0:
+                return local(src, dst, here.at[part])
+            device = (at.grp, at.seg * LOCAL + target)
+            return remote(src, dst, send.at[part, k], recv.at[part, k], device)
+
+        every = [(part, k) for part in range(self.parts) for k in (2, 3, 1, 0)]
+        for part, k in every:
+            copy(part, k).start()
+        yield
+        yield "last"
+        for part, k in every:
+            copy(part, k).wait()
+
+
+class Rows:
+    def __init__(self, array):
+        segs, rows, width = array.shape
+        self.arrays = [array]
+        self.rows = rows
+        self.outs = [jax.ShapeDtypeStruct((segs * rows, width), array.dtype)]
+        self.out_specs = [ANY]
+        self.scratch = [SEND((2,)), SEND((2,)), SEND(())]
+
+    def run(self, at, ins, outs, scratch):
+        (src,), (dst,) = ins, outs
+        send, recv, here = scratch
+        chunk = lax.rem(at.key, 2)
+
+        def part(index):
+            return dst.at[span(index, self.rows), :]
+
+        def out(seg):
+            target = seg * LOCAL + at.key // 2
+            return target, remote(
+                src.at[seg], part(chunk), send.at[seg], recv.at[chunk], (at.grp, target)
+            )
+
+        for seg in range(2):
+            target, copy = out(seg)
+            pl.when(target != at.key)(copy.start)
+            pl.when(target == at.key)(local(src.at[seg], part(chunk), here).start)
+        yield
+        yield "last"
+        for seg in range(2):
+            target, copy = out(seg)
+            pl.when(target != at.key)(copy.wait_send)
+        for index in range(2):
+            owner = 2 * at.rank + index
+            copy = remote(src.at[0], part(index), send.at[0], recv.at[index], (at.grp, owner))
+            pl.when(owner != at.key)(copy.wait_recv)
+            pl.when(owner == at.key)(local(src.at[0], part(index), here).wait)
+
+
+class Chunks:
+    def __init__(self, array):
+        rows, width = array.shape
+        self.arrays = [array]
+        self.rows = rows // 2
+        self.outs = [jax.ShapeDtypeStruct((2, rows // 2, width), array.dtype)]
+        self.out_specs = [ANY]
+        self.scratch = [SEND((2,)), SEND((2,)), SEND(())]
+
+    def run(self, at, ins, outs, scratch):
+        (src,), (dst,) = ins, outs
+        send, recv, here = scratch
+
+        def part(index):
+            return src.at[pl.ds(index * self.rows, self.rows), :]
+
+        def out(index):
+            target = 2 * at.rank + index
+            return target, remote(
+                part(index), dst.at[at.seg], send.at[index], recv.at[at.seg], (at.grp, target)
+            )
+
+        for index in range(2):
+            target, copy = out(index)
+            pl.when(target != at.key)(copy.start)
+            pl.when(target == at.key)(local(part(index), dst.at[at.seg], here).start)
+        yield
+        yield "last"
+        for index in range(2):
+            target, copy = out(index)
+            pl.when(target != at.key)(copy.wait_send)
+        for seg in range(2):
+            owner = seg * LOCAL + at.key // 2
+            copy = remote(part(0), dst.at[seg], send.at[0], recv.at[seg], (at.grp, owner))
+            pl.when(owner != at.key)(copy.wait_recv)
+            pl.when(owner == at.key)(local(part(0), dst.at[seg], here).wait)
+
+
+class Memory:
+    def __init__(self, array):
+        self.arrays = [array]
+        self.rows = array.shape[1]
+        self.outs = [jax.ShapeDtypeStruct((2 * LOCAL * self.rows, PAIR), BF)]
+        self.out_specs = [ANY]
+        self.scratch = [SEND((2 * LOCAL,)), SEND((2 * LOCAL,)), SEND(())]
+
+    def run(self, at, ins, outs, scratch):
+        send, recv, here = scratch
+
+        def copy(k):
+            target = lax.rem(at.key + k, 2 * LOCAL)
+            src = ins[0].at[target // LOCAL, :, span(lax.rem(target, LOCAL), PAIR)]
+            dst = outs[0].at[span(at.key, self.rows), :]
+            if k == 0:
+                return local(src, dst, here)
+            return remote(src, dst, send.at[k], recv.at[k], (at.grp, target))
+
+        for k in range(2 * LOCAL):
+            copy(k).start()
+        yield
+        yield "last"
+        for k in range(2 * LOCAL):
+            copy(k).wait()
+
+
+class Docs:
+    def __init__(self, array):
+        rows, self.width = array.shape
+        self.arrays = [array]
+        self.outs = [jax.ShapeDtypeStruct((rows, 2 * LOCAL * self.width), array.dtype)]
+        self.out_specs = [ANY]
+        self.scratch = [SEND((2 * LOCAL,)), SEND((2 * LOCAL,)), SEND(())]
+
+    def run(self, at, ins, outs, scratch):
+        send, recv, here = scratch
+
+        def copy(k):
+            target = lax.rem(at.key + k, 2 * LOCAL)
+            dst = outs[0].at[:, span(at.key, self.width)]
+            if k == 0:
+                return local(ins[0], dst, here)
+            return remote(ins[0], dst, send.at[k], recv.at[k], (at.grp, target))
+
+        for k in range(2 * LOCAL):
+            copy(k).start()
+        yield
+        yield "last"
+        for k in range(2 * LOCAL):
+            copy(k).wait()
+
+
+class Sibling:
+    def __init__(self, array):
+        self.arrays = [array]
+        self.outs = [jax.ShapeDtypeStruct(array.shape, array.dtype)]
+        self.out_specs = [ANY]
+        self.scratch = [SEND(()), SEND(())]
+
+    def run(self, at, ins, outs, scratch):
+        copy = remote(ins[0], outs[0], scratch[0], scratch[1], at.sibling())
+        copy.start()
+        yield
+        yield "last"
+        copy.wait()
+
+
+STEPS = [(da, db, dz) for db in range(2) for da in range(2) for dz in range(4)]
+
+
+class Gather:
+    def __init__(self, shard, blocks):
+        self.arrays = [shard]
+        self.blocks = blocks
+        self.outs = [jax.ShapeDtypeStruct(blocks.whole(4 * LOCAL), shard.dtype)]
+        self.out_specs = [ANY]
+        self.scratch = [SEND((32,)), SEND((32,)), SEND(())]
+
+    def run(self, at, ins, outs, scratch):
+        (shard,), (whole,) = ins, outs
+        send, recv, here = scratch
+        core = at.core
+
+        def spot(step, of=core):
+            return self.blocks.at(whole, at.chip(*step, of), of)
+
+        def copy(step, slot, target):
+            src = shard if step == (0, 0, 0) else spot(step)
+            return remote(src, spot(step), send.at[slot], recv.at[slot], target)
+
+        def along_z(dz):
+            return copy((0, 0, 0), dz, at.device(0, 0, dz))
+
+        def first(dz):
+            return copy((0, 0, dz), 4 + dz, at.device(1, 0, 0))
+
+        def second(da, dz):
+            return copy((da, 0, dz), 8 + 4 * da + dz, at.device(0, 1, 0))
+
+        def across(step):
+            return copy(step, 16 + STEPS.index(step), at.sibling())
+
+        def arrived(step, slot):
+            dst = spot(step)
+            remote(dst, dst, send.at[slot], recv.at[slot], at.sibling()).wait_recv()
+
+        mine = local(shard, spot((0, 0, 0)), here)
+        mine.start()
+        for dz in (3, 2, 1):
+            along_z(dz).start()
+        first(0).start()
+        second(0, 0).start()
+        across((0, 0, 0)).start()
+        yield
+        for dz in (1, 2, 3):
+            arrived((0, 0, dz), dz)
+            first(dz).start()
+            second(0, dz).start()
+            across((0, 0, dz)).start()
+        yield
+        for dz in range(4):
+            arrived((1, 0, dz), 4 + dz)
+            second(1, dz).start()
+            across((1, 0, dz)).start()
+        yield
+        for da in range(2):
+            for dz in range(4):
+                arrived((da, 1, dz), 8 + 4 * da + dz)
+                across((da, 1, dz)).start()
+        yield "last"
+        for step in STEPS:
+            dst = spot(step, 1 - core)
+            slot = 16 + STEPS.index(step)
+            remote(dst, dst, send.at[slot], recv.at[slot], at.sibling()).wait_recv()
+        for dz in (1, 2, 3):
+            along_z(dz).wait_send()
+        for dz in range(4):
+            first(dz).wait_send()
+            for da in range(2):
+                second(da, dz).wait_send()
+        for step in STEPS:
+            across(step).wait_send()
+        mine.wait()
+
+
+def add_into(dst, parts, tile):
+    rows, width = dst.shape
+
+    @pl.loop(0, width // tile)
+    def _(t):
+        cut = pl.ds(pl.multiple_of(t * tile, tile), tile)
+        total = parts[0][:, cut].astype(F32)
+        for part in parts[1:]:
+            total += part[:, cut].astype(F32)
+        dst[:, cut] = total.astype(dst.dtype)
+
+
+class Scatter:
+    def __init__(self, whole, blocks, lag=0):
+        self.arrays = [whole]
+        self.blocks = blocks
+        self.lag = lag
+        shape = blocks.shape
+        self.pair = isinstance(blocks, PairBlocks)
+        self.tile = 256 if shape[1] % 256 == 0 else 128
+        out = (shape[0] // 2, 2 * shape[1]) if self.pair else shape
+        self.outs = [jax.ShapeDtypeStruct(out, F32)]
+        self.out_specs = [VMEM]
+        dma = SEND
+        self.scratch = [
+            pltpu.VMEM((16,) + shape, BF),
+            pltpu.VMEM((16,) + shape, BF),
+            pltpu.VMEM((8,) + shape, BF),
+            pltpu.VMEM((4,) + shape, BF),
+            pltpu.VMEM((4,) + shape, BF),
+            dma((16,)),
+            dma((32,)),
+            dma((32,)),
+        ]
+        if self.pair:
+            self.scratch += [pltpu.VMEM(shape, F32), dma((2,))]
+
+    def run(self, at, ins, outs, scratch):
+        (whole,), (out,) = ins, outs
+        own, near, from_b, from_a, from_z, load, send, recv = scratch[:8]
+        core = at.core
+        order = list(reversed(STEPS))
+
+        def fetch(slot):
+            src = self.blocks.at(whole, at.chip(*STEPS[slot], core), core)
+            return local(src, own.at[slot], load.at[slot])
+
+        def across(slot):
+            src = self.blocks.at(whole, at.chip(*STEPS[slot], 1 - core), 1 - core)
+            return remote(src, near.at[slot], send.at[slot], recv.at[slot], at.sibling())
+
+        def second(da, dz):
+            slot = STEPS.index((da, 1, dz))
+            spot = 4 * da + dz
+            return remote(
+                own.at[slot], from_b.at[spot], send.at[16 + spot], recv.at[16 + spot],
+                at.device(0, 1, 0),
+            )
+
+        def first(dz):
+            slot = STEPS.index((1, 0, dz))
+            return remote(
+                own.at[slot], from_a.at[dz], send.at[24 + dz], recv.at[24 + dz], at.device(1, 0, 0)
+            )
+
+        def along_z(dz):
+            slot = STEPS.index((0, 0, dz))
+            return remote(
+                own.at[slot], from_z.at[dz], send.at[28 + dz], recv.at[28 + dz], at.device(0, 0, dz)
+            )
+
+        for step in order:
+            slot = STEPS.index(step)
+            across(slot).start()
+            fetch(slot).start()
+        for _ in range(1 + self.lag):
+            yield
+
+        def settle(step, more, dst=None):
+            slot = STEPS.index(step)
+            fetch(slot).wait()
+            across(slot).wait_recv()
+            parts = [own.at[slot], near.at[slot]] + more
+            add_into(own.at[slot] if dst is None else dst, parts, self.tile)
+
+        for da in (1, 0):
+            for dz in (3, 2, 1, 0):
+                settle((da, 1, dz), [])
+                second(da, dz).start()
+        yield
+        for dz in (3, 2, 1, 0):
+            second(1, dz).wait_recv()
+            settle((1, 0, dz), [from_b.at[4 + dz]])
+            first(dz).start()
+        yield
+        for dz in (3, 2, 1):
+            second(0, dz).wait_recv()
+            first(dz).wait_recv()
+            settle((0, 0, dz), [from_b.at[dz], from_a.at[dz]])
+            along_z(dz).start()
+        yield
+        second(0, 0).wait_recv()
+        first(0).wait_recv()
+        for dz in (1, 2, 3):
+            along_z(dz).wait_recv()
+        total = scratch[8] if self.pair else out
+        more = [from_b.at[0], from_a.at[0]] + [from_z.at[dz] for dz in (1, 2, 3)]
+        settle((0, 0, 0), more, total)
+        if self.pair:
+            rows, width = self.blocks.shape
+            half = rows // 2
+            columns = span(core, width)
+            swap = remote(
+                total.at[span(1 - core, half), :], out.at[:, columns],
+                scratch[9].at[0], scratch[9].at[1], at.sibling(),
+            )
+            swap.start()
+            out[:, columns] = total[span(core, half), :]
+        yield "last"
+        if self.pair:
+            swap.wait()
+        for slot in range(16):
+            across(slot).wait_send()
+        for dz in range(4):
+            for da in range(2):
+                second(da, dz).wait_send()
+            first(dz).wait_send()
+            if dz:
+                along_z(dz).wait_send()
+
+
+def exchange(name, collective, parts, vmem=4):
+    sizes = [(len(p.arrays), len(p.outs), len(p.scratch)) for p in parts]
+    n_in = sum(size[0] for size in sizes)
+    n_out = sum(size[1] for size in sizes)
+
+    def kernel(*refs):
+        at = Place()
+        barrier = pltpu.get_barrier_semaphore()
+        near = [(at.grp, lax.rem(at.key + k, 2 * LOCAL)) for k in range(1, 2 * LOCAL)]
+        near += [at.device(1, 0, 0), at.device(0, 1, 0)]
+        for device in near:
+            pl.semaphore_signal(barrier, inc=1, device_id=device, device_id_type=MESH)
+        pl.semaphore_wait(barrier, len(near))
+        ins, outs, scratch = refs[:n_in], refs[n_in : n_in + n_out], refs[n_in + n_out :]
+        live = []
+        sums = any(isinstance(part, Scatter) for part in parts)
+        for part, (i, o, s) in zip(parts, sizes):
+            live.append(part.run(at, ins[:i], outs[:o], scratch[:s]))
+            ins, outs, scratch = ins[i:], outs[o:], scratch[s:]
+        for stage in live:
+            next(stage)
+        ending = []
+        while live:
+            for stage in list(reversed(live) if sums else live):
+                if next(stage) == "last":
+                    live.remove(stage)
+                    ending.append(stage)
+        for stage in ending:
+            for _ in stage:
+                pass
+
+    outs = pl.pallas_call(
+        kernel,
+        name=name,
+        out_shape=[o for p in parts for o in p.outs],
+        in_specs=[ANY] * n_in,
+        out_specs=[o for p in parts for o in p.out_specs],
+        scratch_shapes=[s for p in parts for s in p.scratch],
+        compiler_params=pltpu.CompilerParams(
+            collective_id=collective, has_side_effects=True, vmem_limit_bytes=vmem * 2**20
+        ),
+    )(*[a for p in parts for a in p.arrays])
+    outs = list(outs)
+    return [[outs.pop(0) for _ in p.outs] for p in parts]
+
+
+def dot_nt(a, b):
+    return lax.dot_general(a, b, (((1,), (1,)), ((), ())), preferred_element_type=F32)
+
+
+def dot_nn(a, b):
+    return lax.dot_general(a, b, (((1,), (0,)), ((), ())), preferred_element_type=F32)
+
+
+def heads(index):
+    return pl.ds(index * HEAD, HEAD)
+
+
+def block_rows(j):
+    return pl.ds(pl.multiple_of(j * BLOCK, BLOCK), BLOCK)
+
+
+def transpose_blocks(src, dst):
+    @pl.loop(0, src.shape[0] // BLOCK)
+    def _(j):
+        dst[j] = src[block_rows(j), :].astype(F32).T.astype(BF)
+
+
+def visible(bounds, low, high, j):
+    at = lax.broadcasted_iota(jnp.int32, (BLOCK, BLOCK), 0)
+    start = j * BLOCK
+    return (at >= bounds[low : low + 1, :] - start) & (at < bounds[high : high + 1, :] - start)
+
+
+def attend_kernel(with_memory, local_from, mem_from, mem_to, *refs):
+    if with_memory:
+        q, k, v, bounds, mk, mv, out, stat, vt, mvt, acc, top, total = refs
+    else:
+        q, k, v, bounds, out, stat, vt, acc, top, total = refs
+    i = pl.program_id(0)
+    scale = HEAD ** (-0.5) * LOG2E
+
+    @pl.when(i == 0)
+    def _():
+        transpose_blocks(v, vt)
+        if with_memory:
+            transpose_blocks(mv, mvt)
+
+    acc[...] = jnp.zeros_like(acc)
+    top[...] = jnp.full_like(top, NEG)
+    total[...] = jnp.zeros_like(total)
+
+    def run(keys, values_t, low, high):
+        def body(j, _):
+            seen = visible(bounds, low, high, j)
+            for h in range(2):
+                scores = dot_nt(keys[block_rows(j), heads(h)], q[:, heads(h)]) * scale
+                scores = jnp.where(seen, scores, NEG)
+                old = top[h : h + 1, :]
+                new = jnp.maximum(old, jnp.max(scores, axis=0, keepdims=True))
+                probs = jnp.exp2(scores - new)
+                shrink = jnp.exp2(old - new)
+                top[h : h + 1, :] = new
+                total[h : h + 1, :] = total[h : h + 1, :] * shrink + jnp.sum(
+                    probs, axis=0, keepdims=True
+                )
+                acc[heads(h), :] = acc[heads(h), :] * shrink + dot_nn(
+                    values_t[j, heads(h), :], probs.astype(BF)
+                )
+            return 0
+
+        return body
+
+    lax.fori_loop(local_from[i], i + 1, run(k, vt, 0, 1), 0)
+    if with_memory:
+        lax.fori_loop(mem_from[i], mem_to[i], run(mk, mvt, 2, 3), 0)
+    for h in range(2):
+        share = total[h : h + 1, :]
+        out[:, heads(h)] = (acc[heads(h), :] / share).T.astype(BF)
+        stat[h : h + 1, :] = top[h : h + 1, :] + jnp.log2(share)
+    stat[2:, :] = jnp.zeros_like(stat[2:, :])
+
+
+def attend(q, k, v, memory, bounds, ranges):
+    rows = q.shape[0]
+    blocks = rows // BLOCK
+    row_block = pl.BlockSpec((BLOCK, PAIR), lambda i, *_: (i, 0))
+    lane_block = pl.BlockSpec((8, BLOCK), lambda i, *_: (0, i))
+    operands = [q, k, v, bounds]
+    in_specs = [row_block, VMEM, VMEM, lane_block]
+    scratch = [pltpu.VMEM((blocks, PAIR, BLOCK), BF)]
+    if memory is not None:
+        operands += [memory[0], memory[1]]
+        in_specs += [VMEM, VMEM]
+        scratch += [pltpu.VMEM((memory[1].shape[0] // BLOCK, PAIR, BLOCK), BF)]
+    return pl.pallas_call(
+        functools.partial(attend_kernel, memory is not None),
+        name="attend",
+        grid_spec=pltpu.PrefetchScalarGridSpec(
+            num_scalar_prefetch=3,
+            grid=(blocks,),
+            in_specs=in_specs,
+            out_specs=(row_block, lane_block),
+            scratch_shapes=scratch
+            + [
+                pltpu.VMEM((PAIR, BLOCK), F32),
+                pltpu.VMEM((8, BLOCK), F32),
+                pltpu.VMEM((8, BLOCK), F32),
+            ],
+        ),
+        out_shape=(
+            jax.ShapeDtypeStruct((rows, PAIR), BF),
+            jax.ShapeDtypeStruct((8, rows), F32),
+        ),
+        compiler_params=pltpu.CompilerParams(vmem_limit_bytes=48 * 2**20),
+    )(*ranges, *operands)
+
+
+def attend_back_kernel(with_memory, local_from, mem_from, mem_to, *refs):
+    if with_memory:
+        (q, go, o, stat, bounds, k, v, mk, mv, gq, gk, gv, kt, mkt, delta, gq_t, gk_sum, gv_sum) = refs
+    else:
+        (q, go, o, stat, bounds, k, v, gq, gk, gv, kt, delta, gq_t, gk_sum, gv_sum) = refs
+    i = pl.program_id(0)
+    unit = HEAD ** (-0.5)
+    scale = unit * LOG2E
+
+    @pl.when(i == 0)
+    def _():
+        transpose_blocks(k, kt)
+        gk_sum[...] = jnp.zeros_like(gk_sum)
+        gv_sum[...] = jnp.zeros_like(gv_sum)
+        if with_memory:
+            transpose_blocks(mk, mkt)
+
+    for h in range(2):
+        both = go[:, heads(h)].astype(F32) * o[:, heads(h)].astype(F32)
+        delta[h : h + 1, :] = jnp.sum(both.T, axis=0, keepdims=True)
+    gq_t[...] = jnp.zeros_like(gq_t)
+
+    def run(keys, values, keys_t, low, high, own):
+        def body(j, _):
+            seen = visible(bounds, low, high, j)
+            for h in range(2):
+                query, grad = q[:, heads(h)], go[:, heads(h)]
+                scores = dot_nt(keys[block_rows(j), heads(h)], query) * scale
+                probs = jnp.where(seen, jnp.exp2(scores - stat[h : h + 1, :]), 0.0)
+                grad_probs = dot_nt(values[block_rows(j), heads(h)], grad)
+                grad_scores = (probs * (grad_probs - delta[h : h + 1, :])).astype(BF)
+                gq_t[heads(h), :] += dot_nn(keys_t[j, heads(h), :], grad_scores)
+                if own:
+                    gv_sum[block_rows(j), heads(h)] += dot_nn(probs.astype(BF), grad)
+                    gk_sum[block_rows(j), heads(h)] += dot_nn(grad_scores, query)
+            return 0
+
+        return body
+
+    lax.fori_loop(local_from[i], i + 1, run(k, v, kt, 0, 1, True), 0)
+    if with_memory:
+        lax.fori_loop(mem_from[i], mem_to[i], run(mk, mv, mkt, 2, 3, False), 0)
+    gq[...] = (gq_t[...] * unit).T.astype(BF)
+
+    @pl.when(i == pl.num_programs(0) - 1)
+    def _():
+        gk[...] = (gk_sum[...] * unit).astype(BF)
+        gv[...] = gv_sum[...].astype(BF)
+
+
+def attend_back(q, k, v, memory, bounds, ranges, out, stat, grad):
+    rows = q.shape[0]
+    blocks = rows // BLOCK
+    row_block = pl.BlockSpec((BLOCK, PAIR), lambda i, *_: (i, 0))
+    lane_block = pl.BlockSpec((8, BLOCK), lambda i, *_: (0, i))
+    operands = [q, grad, out, stat, bounds, k, v]
+    in_specs = [row_block, row_block, row_block, lane_block, lane_block, VMEM, VMEM]
+    scratch = [pltpu.VMEM((blocks, PAIR, BLOCK), BF)]
+    if memory is not None:
+        operands += [memory[0], memory[1]]
+        in_specs += [VMEM, VMEM]
+        scratch += [pltpu.VMEM((memory[0].shape[0] // BLOCK, PAIR, BLOCK), BF)]
+    whole = jax.ShapeDtypeStruct((rows, PAIR), BF)
+    return pl.pallas_call(
+        functools.partial(attend_back_kernel, memory is not None),
+        name="attend_back",
+        grid_spec=pltpu.PrefetchScalarGridSpec(
+            num_scalar_prefetch=3,
+            grid=(blocks,),
+            in_specs=in_specs,
+            out_specs=(row_block, VMEM, VMEM),
+            scratch_shapes=scratch
+            + [
+                pltpu.VMEM((8, BLOCK), F32),
+                pltpu.VMEM((PAIR, BLOCK), F32),
+                pltpu.VMEM((rows, PAIR), F32),
+                pltpu.VMEM((rows, PAIR), F32),
+            ],
+        ),
+        out_shape=(whole, whole, whole),
+        compiler_params=pltpu.CompilerParams(vmem_limit_bytes=48 * 2**20),
+    )(*ranges, *operands)
+
+
+def count(compared):
+    return jnp.sum(compared.astype(jnp.int32), axis=1)
+
+
+def mask_ranges(docs, mem_docs, reset):
+    rows = docs.shape[0]
+    entries = mem_docs.shape[0]
+    at = jnp.arange(rows, dtype=jnp.int32)
+    start = count(docs[None, :] < docs[:, None])
+    mem_low = count(mem_docs[None, :] < docs[:, None])
+    mem_high = count(mem_docs[None, :] <= docs[:, None])
+    mem_low = jnp.where(reset == 0, mem_low, 0)
+    mem_high = jnp.where(reset == 0, mem_high, 0)
+    zero = jnp.zeros_like(start)
+    bounds = jnp.stack((start, at + 1, mem_low, mem_high, zero, zero, zero, zero))
+
+    def per_block(values):
+        return values.reshape(rows // BLOCK, BLOCK)
+
+    local_from = jnp.min(per_block(start), axis=1) // BLOCK
+    some = mem_high > mem_low
+    first = jnp.min(per_block(jnp.where(some, mem_low, entries)), axis=1)
+    last = jnp.max(per_block(jnp.where(some, mem_high, 0)), axis=1)
+    mem_from = first // BLOCK
+    mem_to = jnp.maximum((last + BLOCK - 1) // BLOCK, mem_from)
+    return bounds, (local_from, mem_from, mem_to)
+
+
+def sort_memory(memory, mem_docs):
+    entries = mem_docs.shape[0]
+    at = jnp.arange(entries, dtype=jnp.int32)
+    before = (mem_docs[None, :] < mem_docs[:, None]) | (
+        (mem_docs[None, :] == mem_docs[:, None]) & (at[None, :] < at[:, None])
+    )
+    rank = count(before)
+    moved = (rank[None, :] == at[:, None]).astype(BF)
+    return tuple(
+        jnp.dot(moved, memory[index], preferred_element_type=F32).astype(BF) for index in range(2)
+    )
+
+
+def columns(matrix, sizes):
+    pieces, at = [], 0
+    for size in sizes:
+        pieces.append(matrix[:, at : at + size])
+        at += size
+    return pieces
+
+
+def dot_tn(a, b):
+    return lax.dot_general(a, b, (((0,), (0,)), ((), ())), preferred_element_type=F32)
+
+
+def norm_rows(values, gain):
+    inverse = lax.rsqrt(jnp.mean(values * values, axis=-1, keepdims=True) + EPS)
+    return (values * inverse * gain).astype(BF), inverse
+
+
+def norm_rows_back(values, gain, inverse, grad):
+    grad_gain = jnp.sum(grad * values * inverse, axis=0)
+    scaled = grad * gain
+    mean = jnp.mean(scaled * values, axis=-1, keepdims=True)
+    return inverse * scaled - values * inverse**3 * mean, grad_gain
+
+
+def layer(stream, qkv_w, gains, steps, memory, bounds, ranges):
+    gain_a, gain_b = gains
+    normed, inverse_a = norm_rows(stream, gain_a)
+    qkv = jnp.dot(normed, qkv_w, preferred_element_type=F32).astype(BF)
+    q, k, v = steps[0](qkv)
+    out, stat = attend(q, k, v, memory() if memory else None, bounds, ranges)
+    attended, out_w, gate_up_w, down_w = steps[1](out)
+    ff = down_w.shape[0]
+    mixed = stream + jnp.dot(attended, out_w, preferred_element_type=F32)
+    normed_ff, inverse_b = norm_rows(mixed, gain_b)
+    gate_up = jnp.dot(normed_ff, gate_up_w, preferred_element_type=F32)
+    gate, up = gate_up[:, :ff], gate_up[:, ff:]
+    activated = (gate * jax.nn.sigmoid(gate) * up).astype(BF)
+    result = mixed + jnp.dot(activated, down_w, preferred_element_type=F32)
+    weights = (gain_a, qkv_w, out_w, gain_b, gate_up_w, down_w)
+    kept = (stream, inverse_a, normed, q, k, v, out, stat, attended, mixed, inverse_b, normed_ff, gate, up, activated)
+    return result, weights, kept
+
+
+def ffn_back(grad_new, weights, kept):
+    gain_a, qkv_w, out_w, gain_b, gate_up_w, down_w = weights
+    attended, mixed, inverse_b, normed_ff, gate, up, activated = kept[8:]
+    branch = grad_new.astype(BF)
+    grad_down = dot_tn(activated, branch).astype(BF)
+    grad_act = dot_nt(branch, down_w)
+    sig = jax.nn.sigmoid(gate)
+    grad_gate = (grad_act * up * sig * (1.0 + gate * (1.0 - sig))).astype(BF)
+    grad_up = (grad_act * gate * sig).astype(BF)
+    grad_gate_up = jnp.concatenate((grad_gate, grad_up), axis=1)
+    grad_gate_up_w = dot_tn(normed_ff, grad_gate_up).astype(BF)
+    grad_normed_ff = dot_nt(grad_gate_up, gate_up_w)
+    back, grad_gain_b = norm_rows_back(mixed, gain_b, inverse_b, grad_normed_ff)
+    grad_mixed = grad_new + back
+    attn = grad_mixed.astype(BF)
+    grad_out_w = dot_tn(attended, attn).astype(BF)
+    grad_attended = dot_nt(attn, out_w).astype(BF)
+    return grad_mixed, grad_attended, grad_out_w, grad_gain_b, grad_gate_up_w, grad_down
+
+
+def projections_back(grad_mixed, grad_qkv, weights, kept):
+    gain_a, qkv_w = weights[:2]
+    stream, inverse_a, normed = kept[:3]
+    grad_qkv_w = dot_tn(normed, grad_qkv).astype(BF)
+    grad_normed = dot_nt(grad_qkv, qkv_w)
+    back, grad_gain_a = norm_rows_back(stream, gain_a, inverse_a, grad_normed)
+    return grad_mixed + back, grad_gain_a, grad_qkv_w
+
+
+def gain_columns(gains):
+    stacked = jnp.stack(gains, axis=1)
+    return jnp.pad(stacked, ((0, 0), (0, HEAD - len(gains))))
+
+
+def pair_rows(own, other, core):
+    rows, width = own.shape
+    both = jnp.where(core == 0, jnp.stack((own, other)), jnp.stack((other, own)))
+    return lax.dynamic_slice_in_dim(both.reshape(2 * rows, width), core * (width // 2), width // 2, 1)
+
+
+def head_local(
+    tokens, token_docs, memory_docs, memory_resets, memory_keys, memory_values,
+    attn_gain1, query_weight1, key_weight1, value_weight1, out_weight1,
+    ffn_gain1, gate_weight1, up_weight1, down_weight1,
+    attn_gain2, second_query_weight, key_weight2, value_weight2, out_weight2,
+    ffn_gain2, gate_weight2, up_weight2, down_weight2, cotangent,
+):
+    count, width = query_weight1.shape
+    ff = gate_weight1.shape[1]
+    each = down_weight1.shape[0]
+    core = lax.rem(lax.axis_index("key"), 2)
+    seg = lax.axis_index("key") // LOCAL
+    gains = gain_columns((attn_gain1, ffn_gain1, attn_gain2, ffn_gain2))
+    qkv1 = jnp.concatenate((query_weight1, key_weight1, value_weight1), axis=1)
+    qkv2 = jnp.concatenate((second_query_weight, key_weight2, value_weight2), axis=1)
+    gate_up1 = jnp.concatenate((gate_weight1, up_weight1), axis=1)
+    gate_up2 = jnp.concatenate((gate_weight2, up_weight2), axis=1)
+    downs = jnp.concatenate((down_weight1, down_weight2), axis=0)
+    docs = jnp.concatenate((token_docs, memory_docs), axis=0)
+    pairs = PairBlocks(2 * each, width // 2)
+
+    def own(matrix):
+        return RowBlocks(count, matrix.shape[1])
+
+    def gather(matrix):
+        return Gather(matrix, own(matrix))
+
+    (rows,), (docs,), (other,), (qkv1_w,), (gains,) = exchange(
+        "bring_tokens", 1,
+        [Rows(tokens), Docs(docs), Sibling(downs), gather(qkv1), gather(gains)],
+    )
+    down1 = pair_rows(down_weight1, other[:each], core)
+    down2 = pair_rows(down_weight2, other[each:], core)
+    own_docs = lax.dynamic_index_in_dim(docs, seg, 0, keepdims=False)
+    own_mem_docs = lax.dynamic_index_in_dim(docs, seg + 2, 0, keepdims=False)
+    reset = lax.dynamic_index_in_dim(memory_resets, seg, 0, keepdims=False)
+    bounds, ranges = mask_ranges(own_docs, own_mem_docs, reset)
+    gains = gains[:, :4].astype(F32)
+    held = {}
+
+    def heads1(qkv):
+        swapped, (held["out1"],), (held["gu1"],), (held["down1"],), (mk,), (mv,) = exchange(
+            "to_heads_1", 2,
+            [Swap([qkv], True), gather(out_weight1), gather(gate_up1), Gather(down1, pairs),
+             Memory(memory_keys), Memory(memory_values)],
+        )
+        held["memory"] = sort_memory((mk, mv), own_mem_docs)
+        return swapped
+
+    def rows1(out):
+        (attended,), (held["qkv2"],) = exchange(
+            "to_rows_1", 3, [Swap([out], False), gather(qkv2)]
+        )
+        return attended, held["out1"], held["gu1"], held["down1"]
+
+    def heads2(qkv):
+        swapped, (held["out2"],), (held["gu2"],) = exchange(
+            "to_heads_2", 4, [Swap([qkv], True), gather(out_weight2), gather(gate_up2)]
+        )
+        return swapped
+
+    def rows2(out):
+        (attended,), (down,), (held["cot"],) = exchange(
+            "to_rows_2", 5, [Swap([out], False), Gather(down2, pairs), Rows(cotangent)]
+        )
+        return attended, held["out2"], held["gu2"], down
+
+    middle, weights1, kept1 = layer(
+        rows.astype(F32), qkv1_w, (gains[:, 0], gains[:, 1]), (heads1, rows1), None, bounds, ranges
+    )
+    result, weights2, kept2 = layer(
+        middle, held["qkv2"], (gains[:, 2], gains[:, 3]), (heads2, rows2),
+        lambda: held["memory"], bounds, ranges,
+    )
+
+    def part(matrix, index, size):
+        return ColumnBlocks(count, size, index)
+
+    grad_mixed, grad_att, out_g2, gain_b2, gate_up_g2, down_g2 = ffn_back(
+        held["cot"].astype(F32), weights2, kept2
+    )
+    (grad_out,), (output,), (gate_s2,), (up_s2,) = exchange(
+        "back_to_heads_2", 6,
+        [Swap([grad_att], True), Chunks(result.astype(BF)),
+         Scatter(gate_up_g2, ColumnBlocks(count, ff, 0)),
+         Scatter(gate_up_g2, ColumnBlocks(count, ff, 1), 1)],
+        40,
+    )
+    q, k, v, out, stat = kept2[3:8]
+    grads = attend_back(q, k, v, held["memory"], bounds, ranges, out, stat, grad_out)
+    (grad_qkv,), (down_s2,), (out_s2,) = exchange(
+        "back_to_rows_2", 7,
+        [Swap(list(grads), False), Scatter(down_g2, pairs), Scatter(out_g2, own(out_g2), 1)],
+        40,
+    )
+    grad_middle, gain_a2, qkv_g2 = projections_back(grad_mixed, grad_qkv, weights2, kept2)
+
+    grad_mixed, grad_att, out_g1, gain_b1, gate_up_g1, down_g1 = ffn_back(
+        grad_middle, weights1, kept1
+    )
+    (grad_out,), (gate_s1,), (up_s1,), (qkv_s2,) = exchange(
+        "back_to_heads_1", 8,
+        [Swap([grad_att], True),
+         Scatter(gate_up_g1, ColumnBlocks(count, ff, 0)),
+         Scatter(gate_up_g1, ColumnBlocks(count, ff, 1), 1),
+         Scatter(qkv_g2, own(qkv_g2), 2)],
+        44,
+    )
+    q, k, v, out, stat = kept1[3:8]
+    grads = attend_back(q, k, v, None, bounds, ranges, out, stat, grad_out)
+    (grad_qkv,), (down_s1,), (out_s1,) = exchange(
+        "back_to_rows_1", 9,
+        [Swap(list(grads), False), Scatter(down_g1, pairs), Scatter(out_g1, own(out_g1), 1)],
+        40,
+    )
+    grad_rows, gain_a1, qkv_g1 = projections_back(grad_mixed, grad_qkv, weights1, kept1)
+    gain_grads = gain_columns((gain_a1, gain_b1, gain_a2, gain_b2)).astype(BF)
+    (grad_tokens,), (q_s1,), (k_s1,), (v_s1,), (gain_s,) = exchange(
+        "back_to_owners", 10,
+        [Chunks(grad_rows.astype(BF))]
+        + [Scatter(qkv_g1, ColumnBlocks(count, width, i), i) for i in range(3)]
+        + [Scatter(gain_grads, own(gain_grads), 2)],
+        40,
+    )
+    q_s2, k_s2, v_s2 = columns(qkv_s2, (width,) * 3)
+    return (
+        output, grad_tokens.astype(F32),
+        gain_s[:, 0], q_s1, k_s1, v_s1, out_s1, gain_s[:, 1], gate_s1, up_s1, down_s1,
+        gain_s[:, 2], q_s2, k_s2, v_s2, out_s2, gain_s[:, 3], gate_s2, up_s2, down_s2,
+    )
+
+
 def solution(mesh):
     in_specs = (
         P("grp", "key", None),
@@ -417,4 +1403,5 @@
         P(("grp", "key"), None),
         P(("grp", "key"), None),
     )
-    return jax.shard_map(local, mesh=mesh, in_specs=in_specs, out_specs=out_specs, check_vma=False)
+    body = head_local if mesh.shape["key"] == HEADS else gathered_local
+    return jax.shard_map(body, mesh=mesh, in_specs=in_specs, out_specs=out_specs, check_vma=False)

time: 4400 us -> 1190 us (0.27)
  waiting for transfers between devices: 3520 us -> 0 us
  Pallas kernels: 0 us -> 945 us
  matrix products: 470 us -> 163 us
  other arithmetic: 176 us -> 33.2 us
  blocking collectives: 95.3 us -> 0 us
  local copies, waits for them, and re-layouts: 99.3 us -> 36.5 us
    reduce_scatter x18 -> x0, waiting for transfers between devices: 2250 us -> none  [the longest x2 323 us: reduce_gradient_sums(): lax.psum_scatter(terms[6], ('grp', 'key'), scatter_dimension=0, tiled=True)]
    all_gather x18 -> x0, waiting for transfers between devices: 965 us -> none  [the longest x2 164 us: layer_backward(): grad_all = lax.all_gather(grad_attended, 'key', axis=1, tiled=True)]
    pallas_call x0 -> x14, Pallas kernels: none -> 945 us  [the longest x10 779 us: exchange(): pl.pallas_call(kernel, name=name, out_shape=[o for p in parts for o in p....]
    dot_general x54 -> x26, matrix products: 470 us -> 163 us  [the longest x8 62.6 us: dot_nt(): lax.dot_general(a, b, (((1,), (1,)), ((), ())), preferred_element_type=F32)]
    psum x4 -> x0, waiting for transfers between devices: 199 us -> none  [the longest x2 101 us: layer_backward(): lax.psum(jnp.sum(probability * grad_probs, axis=3).astype(jnp.bfloat16),...]
    convert_element_type x16 -> x4, other arithmetic: 124 us -> 7.38 us  [the longest x1 5.19 us: layer(): activated = (gate * jax.nn.sigmoid(gate) * up).astype(BF)]
    pmax x2 -> x0, waiting for transfers between devices: 99.5 us -> none  [attend_forward(): lax.pmax(jnp.max(scores, axis=3).astype(jnp.bfloat16), 'key')]
    unnamed x2 -> x0, blocking collectives: 82.5 us -> none
  transfers between devices with their start and end apart: 42 -> 0, of which waited for: 41 -> 0; matrix products, arithmetic and copies ran while one was open for 8% -> 0% of each run, Pallas kernels for 0% -> 0%
where the time goes in v1:
time: 1190 us; the launch traced here: 1180 us
  Pallas kernels  945 us (79%)
  matrix products  163 us (14%)
  local copies, waits for them, and re-layouts  36.5 us (3%)
  other arithmetic  33.2 us (3%)
    pallas_call x10, Pallas kernels, exchange(): pl.pallas_call(kernel, name=name, out_shape=[o for p in parts for o in p....  779 us
    pallas_call x2, Pallas kernels, attend_back(): pl.pallas_call(functools.partial(attend_back_kernel, memory is not None),...  85.5 us
    pallas_call x2, Pallas kernels, attend(): pl.pallas_call(functools.partial(attend_kernel, memory is not None), name...  80.6 us
    dot_general x8, matrix products, dot_nt(): lax.dot_general(a, b, (((1,), (1,)), ((), ())), preferred_element_type=F32)  62.6 us
    dot_general x8, matrix products, dot_tn(): lax.dot_general(a, b, (((0,), (0,)), ((), ())), preferred_element_type=F32)  46.2 us
    unnamed x158, local copies, waits for them, and re-layouts  29.4 us
    dot_general x2, matrix products, layer(): gate_up = jnp.dot(normed_ff, gate_up_w, preferred_element_type=F32)  25.4 us

profile of v1, /device:TPU:1, one launch (start us, length us, event | category | flops | bytes accessed | tf_op | source)
XLA Modules:
  0.0 1180.7 jit_solution(3453687952884566466)
XLA Ops:
  9.2 69.1 %bring_tokens.1 = (bf16[512,1024]{1,0:T(8,128)(2,1)S(1)}, s32[4,2048]{1,0:T(4,128)S(1)}, bf16[176,1024]{1,0:T(8,128)(2,1)S(1)}, bf16[1024,3072]{1,0:T(8,128)(2,1)S(1)}, bf16[1024,128]{1,0:T(8,128)(2,1)S(1)}) custom-call(bf16[2,256,1024]{2,1,0:T(8,128)(2,1)S(1)} %copy-done.11, s32[4,256]{1,0:T(4,128)S(1)} %pad_add_fusion.refs_1_, ...), custom_call_target="tpu_custom_call" | custom-call | tf_op jit(solution)/shard_map/bring_tokens/pallas_call | solution.py:889
  82.5 9.8 convert_reduce_fusion.2
  95.3 6.8 convolution_convert_fusion.7.refs_0_
  102.1 155.4 %to_heads_1.1 = (bf16[2048,256]{1,0:T(8,128)(2,1)S(1)}, bf16[2048,256]{1,0:T(8,128)(2,1)S(1)}, bf16[2048,256]{1,0:T(8,128)(2,1)S(1)}, bf16[1024,1024]{1,0:T(8,12...) custom-call(bf16[512,3072]{1,0:T(8,128)(2,1)S(1)} %convolution_conve, ...), custom_call_target="tpu_custom_call" | custom-call | tf_op jit(solution)/shard_map/to_heads_1/pallas_call | solution.py:889
  257.5 4.3 copy-done.32
  271.7 29.6 %attend.2 = (bf16[2048,256]{1,0:T(8,128)(2,1)S(1)}, f32[8,2048]{1,0:T(8,128)S(1)}) custom-call(s32[8]{0:T(128)S(1)} %get-tuple-element.178.local_from, s32[8]{0:T(128)S(1)} %get-tuple-element.147.mem_from, s32[8]{0:T(128)S(1)} %get-tuple-element.146.mem_to, bf16[2048,256]{1,0:T(8,128)(2,1)S(1)} %get-tuple-element.77.refs_0_, ...), custom_call_target="tpu_custom_call" | custom-call | tf_op jit(solution)/shard_map/attend/pallas_call | solution.py:993
  301.4 51.2 %to_rows_1.1 = (bf16[512,1024]{1,0:T(8,128)(2,1)S(1)}, bf16[1024,3072]{1,0:T(8,128)(2,1)S(1)}) custom-call(bf16[2048,256]{1,0:T(8,128)(2,1)S(1)} %get-tuple-element.80.refs_0_.refs_2_, bf16[32,3072]{1,0:T(8,128)(2,1)S(1)} %pad_maximum_fusion.10.refs_1_), custom_call_target="tpu_custom_call" | custom-call | tf_op jit(solution)/shard_map/to_rows_1/pallas_call | solution.py:889
  354.6 16.0 %fusion.36 = f32[512,5632]{1,0:T(8,128)} fusion(bf16[1024,5632]{1,0:T(8,128)(2,1)} %copy-done.32, f32[512,1024]{1,0:T(8,128)S(1)} %get-tuple-element.169, f32[1024]{0:T(1024)S(1)} %get-tuple-element.134, f32[512]{0:T(512)S(1)} %get-tuple-element.163), kind=kOutput, calls=%fused_computation.140 | convolution fusion | flops 5907152896 | bytes 25171968 | tf_op jit(solution)/shard_map/dot_general | solution.py:1175
  370.6 5.2 multiply_convert_fusion.5
  383.1 111.0 %to_heads_2.1 = (bf16[2048,256]{1,0:T(8,128)(2,1)S(1)}, bf16[2048,256]{1,0:T(8,128)(2,1)S(1)}, bf16[2048,256]{1,0:T(8,128)(2,1)S(1)}, bf16[1024,1024]{1,0:T(8,128)(2,1)S(1)}, bf16[1024,5632]{1,0:T(8,128)(2,1)S(1)}) custom-call(bf16[512,3072]{1,0:T(8,128)(2,1)S(1)} %convolution_convert_fusion.6.refs_0_, bf16[32,1024]{1,0:T(8,128)(2,1)S(1)} %copy-done.31, ...), custom_call_target="tpu_custom_call" | custom-call | tf_op jit(solution)/shard_map/to_heads_2/pallas_call | solution.py:889
  494.1 4.2 copy-done.33
  498.4 50.9 %attend.3 = (bf16[2048,256]{1,0:T(8,128)(2,1)S(1)}, f32[8,2048]{1,0:T(8,128)S(1)}) custom-call(s32[8]{0:T(128)S(1)} %get-tuple-element.178.local_from, s32[8]{0:T(128)S(1)} %get-tuple-element.147.mem_from, s32[8]{0:T(128)S(1)} %get-tuple-element.146.mem_to, bf16[2048,256]{1,0:T(8,128)(2,1)S(1)} %get-tuple-element.86.refs_0_, ...), custom_call_target="tpu_custom_call" | custom-call | tf_op jit(solution)/shard_map/attend/pallas_call | solution.py:993
  549.3 47.6 %to_rows_2.1 = (bf16[512,1024]{1,0:T(8,128)(2,1)S(1)}, bf16[2816,1024]{1,0:T(8,128)(2,1)S(1)}, bf16[512,1024]{1,0:T(8,128)(2,1)S(1)}) custom-call(bf16[2048,256]{1,0:T(8,128)(2,1)S(1)} %get-tuple-element.91.refs_0_.refs_2_, bf16[176,512]{1,0:T(8,128)(2,1)S(1)} %constant_dynamic-slice_fusion.refs_1_, bf16[2,256,1024]{2,1,0:T(8,128)(2,1)S(1)} %copy-done.12), custom_call_target="tpu_custom_call" | custom-call | tf_op jit(solution)/shard_map/to_rows_2/pallas_call | solution.py:889
  603.0 9.4 fusion.37
  612.4 9.9 multiply_convert_fusion.4
  625.5 13.0 %multiply_reduce_fusion = (bf16[1024]{0:T(1024)(128)(2,1)S(1)}, f32[512]{0:T(512)S(1)}, f32[512,1024]{1,0:T(8,128)}) fusion(f32[512,1024]{1,0:T(8,128)} %copy-done.53, f32[512]{0:T(512)S(1)} %get-tuple-element.167, f32[1024]{0:T(1024)S(1)} %get-tuple-element.132, bf16[1024,5632]{1,0:T(8,128)(2,1)} %copy-done.33, bf16[512,2816]{1,0:T(8,128)(2,1)} %get-tuple-element.151, ...), kind=kOutput, calls=%fused_computation.50 | convolution fusion | flops 5920258560 | bytes 21506048 | tf_op jit(solution)/shard_map/dot_general | solution.py:905
  644.7 5.1 convolution_convert_fusion.5.refs_3_
  649.8 11.8 convolution_convert_fusion.1.refs_2_.refs_3_
  661.6 73.4 %back_to_heads_2.1 = (bf16[2048,256]{1,0:T(8,128)(2,1)S(1)}, bf16[2,256,1024]{2,1,0:T(8,128)(2,1)S(1)}, f32[32,2816]{1,0:T(8,128)S(1)}, f32[32,2816]{1,0:T(8,128)S(1)}) custom-call(bf16[512,1024]{1,0:T(8,128)(2,1)S(1)} %convolution_convert_fusion.11.refs_0_, bf16[512,1024]{1,0:T(8,128)(2,1)S(1)} %add_convert_fusion.refs_1_, ...), custom_call_target="tpu_custom_call" | custom-call | tf_op jit(solution)/shard_map/back_to_heads_2/pallas_call | solution.py:889
  736.6 51.4 %attend_back.2 = (bf16[2048,256]{1,0:T(8,128)(2,1)S(1)}, bf16[2048,256]{1,0:T(8,128)(2,1)S(1)}, bf16[2048,256]{1,0:T(8,128)(2,1)S(1)}) custom-call(s32[8]{0:T(128)S(1)} %get-tuple-element.178.local_from, s32[8]{0:T(128)S(1)} %get-tuple-element.147.mem_from, s32[8]{0:T(128)S(1)} %get-tuple-element.146.mem_to, ...), custom_call_target="tpu_custom_call" | custom-call | tf_op jit(solution)/shard_map/attend_back/pallas_call | solution.py:1079
  788.0 55.7 %back_to_rows_2.1 = (bf16[512,3072]{1,0:T(8,128)(2,1)S(1)}, f32[88,1024]{1,0:T(8,128)S(1)}, f32[32,1024]{1,0:T(8,128)S(1)}) custom-call(bf16[2048,256]{1,0:T(8,128)(2,1)S(1)} %get-tuple-element.100.refs_0_, bf16[2048,256]{1,0:T(8,128)(2,1)S(1)} %get-tuple-element.101.refs_1_, bf16[2048,256]{1,0:T(8,128)(2,1)S(1)} %get-tuple-element.102.refs_2_, ...), custom_call_target="tpu_custom_call" | custom-call | tf_op jit(solution)/shard_map/back_to_rows_2/pallas_call | solution.py:889
  843.8 7.2 multiply_reduce_fusion.1
  851.7 9.6 multiply_convert_fusion.1
  861.3 13.1 %multiply_reduce_fusion.2 = (bf16[1024]{0:T(1024)(128)(2,1)S(1)}, f32[512]{0:T(512)S(1)}, f32[512,1024]{1,0:T(8,128)}) fusion(f32[512,1024]{1,0:T(8,128)S(1)} %copy-done.56, f32[512]{0:T(512)S(1)} %get-tuple-element.163, f32[1024]{0:T(1024)S(1)} %get-tuple-element.134, bf16[1024,5632]{1,0:T(8,128)(2,1)} %copy-done.32, ...), kind=kOutput, calls=%fused_computation.52 | convolution fusion | flops 5920258560 | bytes 21506048 | tf_op jit(solution)/shard_map/dot_general | solution.py:905
  879.9 5.0 convolution_convert_fusion.3.refs_3_
  890.6 11.8 %convolution_convert_fusion.refs_1_.refs_2_ = bf16[1024,5632]{1,0:T(8,128)(2,1)} fusion(bf16[512,2816]{1,0:T(8,128)(2,1)} %get-tuple-element.149, bf16[512,2816]{1,0:T(8,128)(2,1)} %get-tuple-element.148, f32[512,1024]{1,0:T(8,128)S(1)} %copy-done.57, f32[1024]{0:T(1024)S(1)} %get-tuple-element.134, f32[512]{0:T(512)S(1)} %get-tuple-element.163), kind=kOutput, calls=%fused_computation.10 | convolution fusion | flops 5924454400 | bytes 19404800 | tf_op jit(solution)/shard_map/dot_general | solution.py:1150
  902.4 109.4 %back_to_heads_1.1 = (bf16[2048,256]{1,0:T(8,128)(2,1)S(1)}, f32[32,2816]{1,0:T(8,128)S(1)}, f32[32,2816]{1,0:T(8,128)S(1)}, f32[32,3072]{1,0:T(8,128)S(1)}) custom-call(bf16[512,1024]{1,0:T(8,128)(2,1)S(1)} %convolution_convert_fusion.10.refs_0_, bf16[1024,5632]{1,0:T(8,128)(2,1)} %convolution_convert_fusion.refs_1_.refs_2_, ...), custom_call_target="tpu_custom_call" | custom-call | tf_op jit(solution)/shard_map/back_to_heads_1/pallas_call | solution.py:889
  1011.9 34.0 %attend_back.3 = (bf16[2048,256]{1,0:T(8,128)(2,1)S(1)}, bf16[2048,256]{1,0:T(8,128)(2,1)S(1)}, bf16[2048,256]{1,0:T(8,128)(2,1)S(1)}) custom-call(s32[8]{0:T(128)S(1)} %get-tuple-element.178.local_from, s32[8]{0:T(128)S(1)} %get-tuple-element.147.mem_from, s32[8]{0:T(128)S(1)} %get-tuple-element.146.mem_to, bf16[2048,256]{1,0:T(8,128)(2,1)S(1)} %copy-done.3, ...), custom_call_target="tpu_custom_call" | custom-call | tf_op jit(solution)/shard_map/attend_back/pallas_call | solution.py:1079
  1046.0 57.1 %back_to_rows_1.1 = (bf16[512,3072]{1,0:T(8,128)(2,1)S(1)}, f32[88,1024]{1,0:T(8,128)S(1)}, f32[32,1024]{1,0:T(8,128)S(1)}) custom-call(bf16[2048,256]{1,0:T(8,128)(2,1)S(1)} %get-tuple-element.106.refs_0_, bf16[2048,256]{1,0:T(8,128)(2,1)S(1)} %get-tuple-element.107.refs_1_, bf16[2048,256]{1,0:T(8,128)(2,1)S(1)} %get-tuple-element.108.refs_2_, ...), custom_call_target="tpu_custom_call" | custom-call | tf_op jit(solution)/shard_map/back_to_rows_1/pallas_call | solution.py:889
  1103.2 7.2 fusion.19
  1114.8 5.8 convolution_convert_fusion.2.refs_1_.refs_2_.refs_3_
  1120.6 48.9 %back_to_owners.1 = (bf16[2,256,1024]{2,1,0:T(8,128)(2,1)S(1)}, f32[32,1024]{1,0:T(8,128)S(1)}, f32[32,1024]{1,0:T(8,128)S(1)}, f32[32,1024]{1,0:T(8,128)S(1)}, f32[32,128]{1,0:T(8,128)S(1)}) custom-call(bf16[512,1024]{1,0:T(8,128)(2,1)S(1)} %fusion.16.refs_0_, bf16[1024,3072]{1,0:T(8,128)(2,1)S(1)} %convolution_convert_fusion.2.refs_1_.refs_2_.refs_3_, ...), custom_call_target="tpu_custom_call" | custom-call | tf_op jit(solution)/shard_map/back_to_owners/pallas_call | solution.py:889
  (221 shorter events, 77.9 us)
Async XLA Ops:
  0.7 8.5 copy-start.11
  81.5 271.0 %copy-start = (bf16[512,1024]{1,0:T(8,128)(2,1)}, bf16[512,1024]{1,0:T(8,128)(2,1)S(1)}, u32[]{:S(2)}) copy-start(bf16[512,1024]{1,0:T(8,128)(2,1)S(1)} %get-tuple-element.73) | copy-start | bytes 3145732
  81.5 12.6 %copy-start.29 = (bf16[1024,128]{1,0:T(8,128)(2,1)S(1)}, bf16[1024,128]{1,0:T(8,128)(2,1)}, u32[]{:S(2)}) copy-start(bf16[1024,128]{1,0:T(8,128)(2,1)} %copy-done.28) | copy-start | bytes 786436
  82.5 12.8 %copy-start.63 = (f32[512]{0:T(512)}, f32[512]{0:T(512)S(1)}, u32[]{:S(2)}) copy-start(f32[512]{0:T(512)S(1)} %get-tuple-element.161) | copy-start | bytes 6148
  264.4 7.3 copy-start.4
  264.4 7.3 copy-start.5
  264.4 88.2 %copy-start.41 = (bf16[1024,1024]{1,0:T(8,128)(2,1)}, bf16[1024,1024]{1,0:T(8,128)(2,1)S(1)}, u32[]{:S(2)}) copy-start(bf16[1024,1024]{1,0:T(8,128)(2,1)S(1)} %get-tuple-element.82) | copy-start | bytes 6291460
  267.6 230.8 %copy-start.8 = (bf16[2048,256]{1,0:T(8,128)(2,1)}, bf16[2048,256]{1,0:T(8,128)(2,1)S(1)}, u32[]{:S(2)}) copy-start(bf16[2048,256]{1,0:T(8,128)(2,1)S(1)} %fusion.8.refs_4_.refs_7_) | copy-start | bytes 3145732
  301.4 52.6 %copy-start.6 = (bf16[2048,256]{1,0:T(8,128)(2,1)}, bf16[2048,256]{1,0:T(8,128)(2,1)S(1)}, u32[]{:S(2)}) copy-start(bf16[2048,256]{1,0:T(8,128)(2,1)S(1)} %get-tuple-element.80.refs_0_.refs_2_) | copy-start | bytes 3145732
  352.6 26.5 %copy-start.36 = (bf16[1024,3072]{1,0:T(8,128)(2,1)}, bf16[1024,3072]{1,0:T(8,128)(2,1)S(1)}, u32[]{:S(2)}) copy-start(bf16[1024,3072]{1,0:T(8,128)(2,1)S(1)} %get-tuple-element.85) | copy-start | bytes 18874372
  352.6 23.2 %slice-start = ((s8[5767168]{0:T(1024)(128)(4,1)}), s8[4194304]{0:T(1024)(128)(4,1)S(1)}, s32[]{:S(2)}) async-start(s8[5767168]{0:T(1024)(128)(4,1)} %bitcast.50), calls=%async_computation | async-start | bytes 8388608
  354.0 21.8 %copy-start.55 = (f32[512,1024]{1,0:T(8,128)}, f32[512,1024]{1,0:T(8,128)S(1)}, u32[]{:S(2)}) copy-start(f32[512,1024]{1,0:T(8,128)S(1)} %get-tuple-element.169) | copy-start | bytes 6291460
  354.6 21.2 %slice-start.1 = ((s8[5767168]{0:T(1024)(128)(4,1)}), s8[1572864]{0:T(1024)(128)(4,1)S(1)}, s32[]{:S(2)}) async-start(s8[5767168]{0:T(1024)(128)(4,1)} %bitcast.50), calls=%async_computation.1 | async-start | bytes 3145728
  498.3 98.6 %copy-start.9 = (bf16[2048,256]{1,0:T(8,128)(2,1)}, bf16[2048,256]{1,0:T(8,128)(2,1)S(1)}, u32[]{:S(2)}) copy-start(bf16[2048,256]{1,0:T(8,128)(2,1)S(1)} %get-tuple-element.87.refs_1_.refs_5_) | copy-start | bytes 3145732
  498.3 98.6 %copy-start.10 = (bf16[2048,256]{1,0:T(8,128)(2,1)}, bf16[2048,256]{1,0:T(8,128)(2,1)S(1)}, u32[]{:S(2)}) copy-start(bf16[2048,256]{1,0:T(8,128)(2,1)S(1)} %get-tuple-element.88.refs_2_.refs_6_) | copy-start | bytes 3145732
  498.3 98.6 %copy-start.43 = (bf16[1024,1024]{1,0:T(8,128)(2,1)}, bf16[1024,1024]{1,0:T(8,128)(2,1)S(1)}, u32[]{:S(2)}) copy-start(bf16[1024,1024]{1,0:T(8,128)(2,1)S(1)} %get-tuple-element.94) | copy-start | bytes 6291460
  498.3 51.0 %copy-start.12 = (bf16[2,256,1024]{2,1,0:T(8,128)(2,1)S(1)}, bf16[2,256,1024]{2,1,0:T(8,128)(2,1)}, u32[]{:S(2)}) copy-start(bf16[2,256,1024]{2,1,0:T(8,128)(2,1)} %refs_2_.1) | copy-start | bytes 3145732
  549.3 51.1 %copy-start.7 = (bf16[2048,256]{1,0:T(8,128)(2,1)}, bf16[2048,256]{1,0:T(8,128)(2,1)S(1)}, u32[]{:S(2)}) copy-start(bf16[2048,256]{1,0:T(8,128)(2,1)S(1)} %get-tuple-element.91.refs_0_.refs_2_) | copy-start | bytes 3145732
  600.4 21.9 %copy-start.53 = (f32[512,1024]{1,0:T(8,128)}, f32[512,1024]{1,0:T(8,128)S(1)}, u32[]{:S(2)}) copy-start(f32[512,1024]{1,0:T(8,128)S(1)} %get-tuple-element.173) | copy-start | bytes 6291460
  788.0 55.8 %copy-start.59 = (f32[512,1024]{1,0:T(8,128)S(1)}, f32[512,1024]{1,0:T(8,128)}, u32[]{:S(2)}) copy-start(f32[512,1024]{1,0:T(8,128)} %copy-done.58) | copy-start | bytes 6291460
  788.0 63.6 %slice-start.2 = ((s8[5767168]{0:T(1024)(128)(4,1)}), s8[4194304]{0:T(1024)(128)(4,1)S(1)}, s32[]{:S(2)}) async-start(s8[5767168]{0:T(1024)(128)(4,1)} %bitcast.52), calls=%async_computation.2 | async-start | bytes 8388608
  843.8 7.8 slice-start.3
  851.6 9.6 copy-start.56
  861.3 13.1 %copy-start.66 = (f32[512]{0:T(512)S(1)}, f32[512]{0:T(512)}, u32[]{:S(2)}) copy-start(f32[512]{0:T(512)} %get-tuple-element.162) | copy-start | bytes 6148
  877.4 11.6 copy-start.49
  902.4 109.5 %copy-start.3 = (bf16[2048,256]{1,0:T(8,128)(2,1)S(1)}, bf16[2048,256]{1,0:T(8,128)(2,1)}, u32[]{:S(2)}) copy-start(bf16[2048,256]{1,0:T(8,128)(2,1)} %copy-done.2) | copy-start | bytes 3145732
  1011.8 91.2 %copy-start.15 = (f32[32,3072]{1,0:T(8,128)}, f32[32,3072]{1,0:T(8,128)S(1)}, u32[]{:S(2)}) copy-start(f32[32,3072]{1,0:T(8,128)S(1)} %get-tuple-element.119) | copy-start | bytes 1179652
  1011.9 91.2 %copy-start.22 = (f32[32,2816]{1,0:T(8,128)}, f32[32,2816]{1,0:T(8,128)S(1)}, u32[]{:S(2)}) copy-start(f32[32,2816]{1,0:T(8,128)S(1)} %get-tuple-element.210) | copy-start | bytes 1081348
  1011.9 91.2 %copy-start.24 = (f32[32,2816]{1,0:T(8,128)}, f32[32,2816]{1,0:T(8,128)S(1)}, u32[]{:S(2)}) copy-start(f32[32,2816]{1,0:T(8,128)S(1)} %get-tuple-element.209) | copy-start | bytes 1081348
  1045.9 57.2 %copy-start.1 = (bf16[512,1024]{1,0:T(8,128)(2,1)S(1)}, bf16[512,1024]{1,0:T(8,128)(2,1)}, u32[]{:S(2)}) copy-start(bf16[512,1024]{1,0:T(8,128)(2,1)} %copy-done) | copy-start | bytes 3145732
  1045.9 57.2 %copy-start.62 = (f32[1024]{0:T(1024)S(1)}, f32[1024]{0:T(1024)}, u32[]{:S(2)}) copy-start(f32[1024]{0:T(1024)} %copy-done.61) | copy-start | bytes 12292
  1046.0 57.2 %copy-start.64 = (f32[512]{0:T(512)S(1)}, f32[512]{0:T(512)}, u32[]{:S(2)}) copy-start(f32[512]{0:T(512)} %copy-done.63) | copy-start | bytes 6148
  (41 other events, 188.7 us)

commit v2 on v1

--- a/solution.py
+++ b/solution.py
@@ -375,7 +375,8 @@
 ANY = pl.BlockSpec(memory_space=pl.ANY)
 VMEM = pl.BlockSpec(memory_space=pltpu.VMEM)
 LOG2E = 1.4426950408889634
-BLOCK = 256
+BLOCK = 512
+QUERIES = 512
 LOCAL = 4
 HEAD = 128
 PAIR = 2 * HEAD
@@ -402,7 +403,7 @@
     def chip(self, da, db, dz, core):
         dx = da * (1 - core) + db * core
         dy = da * core + db * (1 - core)
-        z = flip(self.z // 2, dz // 2) * 2 + flip(lax.rem(self.z, 2), dz % 2)
+        z = flip(self.z // 2, dz // 2) * 2 + flip(lax.rem(self.z, 2), lax.rem(dz, 2))
         return flip(self.y, dy) * 2 + flip(self.x, dx), z
 
     def device(self, da, db, dz):
@@ -655,7 +656,7 @@
         self.blocks = blocks
         self.outs = [jax.ShapeDtypeStruct(blocks.whole(4 * LOCAL), shard.dtype)]
         self.out_specs = [ANY]
-        self.scratch = [SEND((32,)), SEND((32,)), SEND(())]
+        self.scratch = [SEND((36,)), SEND((36,)), SEND(())]
 
     def run(self, at, ins, outs, scratch):
         (shard,), (whole,) = ins, outs
@@ -666,55 +667,74 @@
             return self.blocks.at(whole, at.chip(*step, of), of)
 
         def copy(step, slot, target):
-            src = shard if step == (0, 0, 0) else spot(step)
+            mine = isinstance(step[2], int) and step == (0, 0, 0)
+            src = shard if mine else spot(step)
             return remote(src, spot(step), send.at[slot], recv.at[slot], target)
 
-        def along_z(dz):
-            return copy((0, 0, 0), dz, at.device(0, 0, dz))
+        def cross(step):
+            da, db, dz = step
+            return 20 + 8 * db + 4 * da + dz
 
         def first(dz):
-            return copy((0, 0, dz), 4 + dz, at.device(1, 0, 0))
+            return copy((0, 0, dz), 8 + dz, at.device(1, 0, 0))
 
         def second(da, dz):
-            return copy((da, 0, dz), 8 + 4 * da + dz, at.device(0, 1, 0))
+            return copy((da, 0, dz), 12 + 4 * da + dz, at.device(0, 1, 0))
 
         def across(step):
-            return copy(step, 16 + STEPS.index(step), at.sibling())
+            return copy(step, cross(step), at.sibling())
 
         def arrived(step, slot):
             dst = spot(step)
             remote(dst, dst, send.at[slot], recv.at[slot], at.sibling()).wait_recv()
 
+        inner = flip(at.z // 2, lax.rem(at.z, 2))
+        near, turns = at.device(0, 0, 1), (1, 2 + inner, 3 - inner)
+        far = at.device(0, 0, 3)
+        inside = pl.when(inner == 1)
+
+        def along_z(index):
+            if index == 0:
+                return remote(shard, spot((0, 0, 0)), send.at[0], recv.at[1], near)
+            if index == 1:
+                return remote(shard, spot((0, 0, 0)), send.at[1], recv.at[3], far)
+            step, slot, device = {
+                2: ((0, 0, 1), 2, far), 3: ((0, 0, 3), 2, near), 4: ((0, 0, 2), 3, near)
+            }[index]
+            return remote(spot(step), spot(step), send.at[index], recv.at[slot], device)
+
         mine = local(shard, spot((0, 0, 0)), here)
         mine.start()
-        for dz in (3, 2, 1):
-            along_z(dz).start()
+        along_z(0).start()
+        inside(along_z(1).start)
         first(0).start()
         second(0, 0).start()
         across((0, 0, 0)).start()
         yield
-        for dz in (1, 2, 3):
+        for turn, dz in enumerate(turns):
             arrived((0, 0, dz), dz)
+            inside(along_z((2, 3, 4)[turn]).start)
             first(dz).start()
             second(0, dz).start()
             across((0, 0, dz)).start()
         yield
-        for dz in range(4):
-            arrived((1, 0, dz), 4 + dz)
+        for dz in (0,) + turns:
+            arrived((1, 0, dz), 8 + dz)
             second(1, dz).start()
             across((1, 0, dz)).start()
         yield
         for da in range(2):
-            for dz in range(4):
-                arrived((da, 1, dz), 8 + 4 * da + dz)
+            for dz in (0,) + turns:
+                arrived((da, 1, dz), 12 + 4 * da + dz)
                 across((da, 1, dz)).start()
         yield "last"
         for step in STEPS:
             dst = spot(step, 1 - core)
-            slot = 16 + STEPS.index(step)
+            slot = cross(step)
             remote(dst, dst, send.at[slot], recv.at[slot], at.sibling()).wait_recv()
-        for dz in (1, 2, 3):
-            along_z(dz).wait_send()
+        along_z(0).wait_send()
+        for index in range(1, 5):
+            inside(along_z(index).wait_send)
         for dz in range(4):
             first(dz).wait_send()
             for da in range(2):
@@ -736,11 +756,141 @@
         dst[:, cut] = total.astype(dst.dtype)
 
 
+class Assemble:
+    def __init__(self, groups, blocks):
+        self.arrays = list(groups)
+        self.blocks = blocks
+        self.outs = [jax.ShapeDtypeStruct(b.whole(4 * LOCAL), groups[0].dtype) for b in blocks]
+        self.out_specs = [ANY] * len(blocks)
+        n = len(blocks)
+        self.scratch = [SEND((n, 16)), SEND((n, 16)), SEND((n, 16))]
+
+    def run(self, at, ins, outs, scratch):
+        send, recv, here = scratch
+
+        def each():
+            begin = 0
+            for index, blocks in enumerate(self.blocks):
+                for slot in range(16):
+                    yield index, slot, pl.ds(begin, blocks.shape[1])
+                begin += blocks.shape[1]
+
+        def spot(index, slot, core):
+            return self.blocks[index].at(outs[index], at.chip(*STEPS[slot], core), core)
+
+        def copies(index, slot, cut):
+            src = ins[slot // 4].at[slot % 4, :, cut]
+            dst = spot(index, slot, at.core)
+            return remote(
+                src, dst, send.at[index, slot], recv.at[index, slot], at.sibling()
+            ), local(src, dst, here.at[index, slot])
+
+        for spec in each():
+            for copy in copies(*spec):
+                copy.start()
+        yield
+        yield "last"
+        for index, slot, cut in each():
+            across, own = copies(index, slot, cut)
+            across.wait_send()
+            own.wait()
+            dst = spot(index, slot, 1 - at.core)
+            remote(dst, dst, send.at[index, slot], recv.at[index, slot], at.sibling()).wait_recv()
+
+
+PACK = 16
+
+
+class CoreSums:
+    def __init__(self, *wholes):
+        self.arrays = [whole for whole, _ in wholes]
+        self.blocks = [blocks for _, blocks in wholes]
+        shapes = [blocks.shape for blocks in self.blocks]
+        self.width = sum(rows // PACK * width for rows, width in shapes)
+        self.outs = [jax.ShapeDtypeStruct((n, PACK, self.width), BF) for n in (4, 4, 8)]
+        self.out_specs = [ANY] * 3
+        n = len(shapes)
+        self.scratch = [pltpu.VMEM((16,) + shape, BF) for shape in shapes] * 2
+        self.scratch += [pltpu.VMEM((16, PACK, self.width), BF)]
+        self.scratch += [SEND((n, 16)), SEND((n, 16)), SEND((n, 16)), SEND((16,))]
+
+    def run(self, at, ins, outs, scratch):
+        n = len(ins)
+        own, near, packed = scratch[:n], scratch[n : 2 * n], scratch[2 * n]
+        load, send, recv, store = scratch[2 * n + 1 :]
+
+        def chip(slot, core):
+            return at.chip(lax.rem(slot // 4, 2), slot // 8, lax.rem(slot, 4), core)
+
+        def fetch(index, slot):
+            src = self.blocks[index].at(ins[index], chip(slot, at.core), at.core)
+            return local(src, own[index].at[slot], load.at[index, slot])
+
+        def across(index, slot):
+            other = 1 - at.core
+            src = self.blocks[index].at(ins[index], chip(slot, other), other)
+            return remote(
+                src, near[index].at[slot], send.at[index, slot], recv.at[index, slot], at.sibling()
+            )
+
+        def keep(slot, group, first):
+            return local(packed.at[slot], outs[group].at[slot - first], store.at[slot])
+
+        @pl.loop(0, 16)
+        def _(turn):
+            for index in range(n):
+                across(index, 15 - turn).start()
+                fetch(index, 15 - turn).start()
+
+        yield
+        groups = ((2, 8, 8), (1, 4, 4), (0, 0, 4))
+        for group, first, count in groups:
+
+            @pl.loop(0, count)
+            def _(turn):
+                slot = first + count - 1 - turn
+                begin = 0
+                for index in range(n):
+                    fetch(index, slot).wait()
+                    across(index, slot).wait_recv()
+                    rows, width = self.blocks[index].shape
+                    for part in range(rows // PACK):
+                        cut = pl.ds(part * PACK, PACK)
+                        add_into(
+                            packed.at[slot, :, pl.ds(begin, width)],
+                            [own[index].at[slot, cut, :], near[index].at[slot, cut, :]],
+                            512,
+                        )
+                        begin += width
+                keep(slot, group, first).start()
+
+            yield
+        yield "last"
+        for group, first, count in groups:
+
+            @pl.loop(0, count)
+            def _(turn):
+                slot = first + count - 1 - turn
+                for index in range(n):
+                    across(index, slot).wait_send()
+                keep(slot, group, first).wait()
+
+
+def unpack(total, shapes):
+    blocks, begin = [], 0
+    for rows, width in shapes:
+        parts = rows // PACK
+        cut = total[:, begin : begin + parts * width].reshape(PACK, parts, width)
+        blocks.append(cut.transpose(1, 0, 2).reshape(rows, width))
+        begin += parts * width
+    return blocks
+
+
 class Scatter:
-    def __init__(self, whole, blocks, lag=0):
+    def __init__(self, whole, blocks, turn=0):
         self.arrays = [whole]
         self.blocks = blocks
-        self.lag = lag
+        self.turn = turn
         shape = blocks.shape
         self.pair = isinstance(blocks, PairBlocks)
         self.tile = 256 if shape[1] % 256 == 0 else 128
@@ -799,7 +949,7 @@
             slot = STEPS.index(step)
             across(slot).start()
             fetch(slot).start()
-        for _ in range(1 + self.lag):
+        for _ in range(1 + self.turn):
             yield
 
         def settle(step, more, dst=None):
@@ -855,6 +1005,17 @@
                 along_z(dz).wait_send()
 
 
+def later(part, steps=2):
+    part.wait = steps
+    return part
+
+
+def staged(part, *refs):
+    for _ in range(getattr(part, "wait", 0)):
+        yield
+    yield from part.run(*refs)
+
+
 def exchange(name, collective, parts, vmem=4):
     sizes = [(len(p.arrays), len(p.outs), len(p.scratch)) for p in parts]
     n_in = sum(size[0] for size in sizes)
@@ -872,7 +1033,7 @@
         live = []
         sums = any(isinstance(part, Scatter) for part in parts)
         for part, (i, o, s) in zip(parts, sizes):
-            live.append(part.run(at, ins[:i], outs[:o], scratch[:s]))
+            live.append(staged(part, at, ins[:i], outs[:o], scratch[:s]))
             ins, outs, scratch = ins[i:], outs[o:], scratch[s:]
         for stage in live:
             next(stage)
@@ -901,6 +1062,86 @@
     return [[outs.pop(0) for _ in p.outs] for p in parts]
 
 
+def hop(values, change):
+    pairs = []
+    for y in range(2):
+        for x in range(2):
+            for z in range(LOCAL):
+                for core in range(2):
+                    to = [y, x, z, core]
+                    if change in ("a", "b"):
+                        to[1 if (change == "a") == (core == 0) else 0] ^= 1
+                    elif change == "core":
+                        to[3] ^= 1
+                    else:
+                        to[2] ^= change
+                    number = [((v[0] * 2 + v[1]) * LOCAL + v[2]) * 2 + v[3] for v in ([y, x, z, core], to)]
+                    pairs.append(tuple(number))
+    return lax.ppermute(values, ("grp", "key"), pairs)
+
+
+def column_hop(values, pairs):
+    size = 2 * LOCAL
+    every = [(g * size + s, g * size + t) for g in range(4) for s, t in pairs]
+    return lax.ppermute(values, ("grp", "key"), every)
+
+
+def join(value, others):
+    return lax.optimization_barrier((value, others))
+
+
+def gather_column(shard):
+    return jnp.stack([shard] + [hop(shard, dz) for dz in (1, 2, 3)])
+
+
+def add(*terms):
+    return sum(term.astype(F32) for term in terms)
+
+
+def scatter_second(sums):
+    here, first, second = sums
+    return here, first, hop(second, "b")
+
+
+def scatter_first(sums):
+    here, first, got = sums
+    return here, got, hop(add(first, got[4:]).astype(BF), "a")
+
+
+def scatter_z(sums):
+    here, got, more = sums
+    total = add(here, got[:4], more)
+    low = total[1:].astype(BF)
+    return [total[0]] + [hop(low[dz - 1], dz) for dz in (1, 2, 3)]
+
+
+def scatter_end(sums):
+    return add(*sums)
+
+
+def rows_hops(chunks):
+    odd = lax.rem(lax.axis_index("key"), 2) == 1
+    size = 2 * LOCAL
+    same = [(j, j // 2 + LOCAL * (j % 2)) for j in range(size)]
+    cross = [(j, j // 2 + LOCAL * (1 - j % 2)) for j in range(size)]
+    one = column_hop(jnp.where(odd, chunks[1], chunks[0]), same)
+    two = column_hop(jnp.where(odd, chunks[0], chunks[1]), cross)
+    upper = lax.axis_index("key") >= LOCAL
+    return jnp.concatenate((jnp.where(upper, two, one), jnp.where(upper, one, two)))
+
+
+def chunk_hops(rows):
+    half = rows.shape[0] // 2
+    odd = lax.rem(lax.axis_index("key"), 2) == 1
+    upper = lax.axis_index("key") >= LOCAL
+    size = 2 * LOCAL
+    same = [(j // 2 + LOCAL * (j % 2), j) for j in range(size)]
+    cross = [(j // 2 + LOCAL * (1 - j % 2), j) for j in range(size)]
+    one = column_hop(jnp.where(upper, rows[half:], rows[:half]), same)
+    two = column_hop(jnp.where(upper, rows[:half], rows[half:]), cross)
+    return jnp.stack((jnp.where(odd, two, one), jnp.where(odd, one, two)))
+
+
 def dot_nt(a, b):
     return lax.dot_general(a, b, (((1,), (1,)), ((), ())), preferred_element_type=F32)
 
@@ -924,18 +1165,36 @@
 
 
 def visible(bounds, low, high, j):
-    at = lax.broadcasted_iota(jnp.int32, (BLOCK, BLOCK), 0)
+    at = lax.broadcasted_iota(jnp.int32, (BLOCK, QUERIES), 0)
     start = j * BLOCK
     return (at >= bounds[low : low + 1, :] - start) & (at < bounds[high : high + 1, :] - start)
 
 
-def attend_kernel(with_memory, local_from, mem_from, mem_to, *refs):
+def fold(values):
+    return values.reshape(values.shape[0] // 8, 8, values.shape[1])
+
+
+def each_block(ranges, i, with_memory, local_body, memory_body):
+    begin, full, diagonal, end = (ranges[i, k] for k in range(4))
+    lax.fori_loop(begin, full, local_body(True), 0)
+    lax.fori_loop(full, diagonal, local_body(False), 0)
+    lax.fori_loop(diagonal, end, local_body(True), 0)
     if with_memory:
-        q, k, v, bounds, mk, mv, out, stat, vt, mvt, acc, top, total = refs
+        begin, full, rest, end = (ranges[i, k] for k in range(4, 8))
+        lax.fori_loop(begin, full, memory_body(True), 0)
+        lax.fori_loop(full, rest, memory_body(False), 0)
+        lax.fori_loop(rest, end, memory_body(True), 0)
+
+
+def attend_kernel(with_memory, ranges, *refs):
+    if with_memory:
+        q, k, v, bounds, mk, mv, out, stat, vt, mvt, scores, acc, top, total = refs
     else:
-        q, k, v, bounds, out, stat, vt, acc, top, total = refs
+        q, k, v, bounds, out, stat, vt, scores, acc, top, total = refs
+        mk = mvt = None
     i = pl.program_id(0)
     scale = HEAD ** (-0.5) * LOG2E
+    blocks = vt.shape[0]
 
     @pl.when(i == 0)
     def _():
@@ -947,62 +1206,75 @@
     top[...] = jnp.full_like(top, NEG)
     total[...] = jnp.zeros_like(total)
 
-    def run(keys, values_t, low, high):
-        def body(j, _):
-            seen = visible(bounds, low, high, j)
-            for h in range(2):
-                scores = dot_nt(keys[block_rows(j), heads(h)], q[:, heads(h)]) * scale
-                scores = jnp.where(seen, scores, NEG)
-                old = top[h : h + 1, :]
-                new = jnp.maximum(old, jnp.max(scores, axis=0, keepdims=True))
-                probs = jnp.exp2(scores - new)
-                shrink = jnp.exp2(old - new)
-                top[h : h + 1, :] = new
-                total[h : h + 1, :] = total[h : h + 1, :] * shrink + jnp.sum(
-                    probs, axis=0, keepdims=True
-                )
-                acc[heads(h), :] = acc[heads(h), :] * shrink + dot_nn(
-                    values_t[j, heads(h), :], probs.astype(BF)
-                )
-            return 0
-
-        return body
-
-    lax.fori_loop(local_from[i], i + 1, run(k, vt, 0, 1), 0)
+    def scan(keys, first, low):
+        def run(masked):
+            def body(j, _):
+                for h in range(2):
+                    part = dot_nt(keys[block_rows(j), heads(h)], q[:, heads(h)])
+                    if masked:
+                        part = jnp.where(visible(bounds, low, low + 1, j), part, NEG)
+                    scores[h, first + j] = part
+                    top[h] = jnp.maximum(top[h], jnp.max(fold(part), axis=0))
+                return 0
+
+            return body
+
+        return run
+
+    each_block(ranges, i, with_memory, scan(k, 0, 0), scan(mk, blocks, 2))
+    tops = [jnp.max(top[h], axis=0, keepdims=True) * scale for h in range(2)]
+
+    def take(values_t, first):
+        def run(masked):
+            def body(j, _):
+                for h in range(2):
+                    probs = jnp.exp2(scores[h, first + j] * scale - tops[h])
+                    total[h] += jnp.sum(fold(probs), axis=0)
+                    acc[heads(h), :] += dot_nn(values_t[j, heads(h), :], probs.astype(BF))
+                return 0
+
+            return body
+
+        return run
+
+    lax.fori_loop(ranges[i, 0], ranges[i, 3], take(vt, 0)(False), 0)
     if with_memory:
-        lax.fori_loop(mem_from[i], mem_to[i], run(mk, mvt, 2, 3), 0)
+        lax.fori_loop(ranges[i, 4], ranges[i, 7], take(mvt, blocks)(False), 0)
     for h in range(2):
-        share = total[h : h + 1, :]
+        share = jnp.sum(total[h], axis=0, keepdims=True)
         out[:, heads(h)] = (acc[heads(h), :] / share).T.astype(BF)
-        stat[h : h + 1, :] = top[h : h + 1, :] + jnp.log2(share)
+        stat[h : h + 1, :] = tops[h] + jnp.log2(share)
     stat[2:, :] = jnp.zeros_like(stat[2:, :])
 
 
 def attend(q, k, v, memory, bounds, ranges):
     rows = q.shape[0]
     blocks = rows // BLOCK
-    row_block = pl.BlockSpec((BLOCK, PAIR), lambda i, *_: (i, 0))
-    lane_block = pl.BlockSpec((8, BLOCK), lambda i, *_: (0, i))
+    row_block = pl.BlockSpec((QUERIES, PAIR), lambda i, *_: (i, 0))
+    lane_block = pl.BlockSpec((8, QUERIES), lambda i, *_: (0, i))
     operands = [q, k, v, bounds]
     in_specs = [row_block, VMEM, VMEM, lane_block]
     scratch = [pltpu.VMEM((blocks, PAIR, BLOCK), BF)]
     if memory is not None:
         operands += [memory[0], memory[1]]
         in_specs += [VMEM, VMEM]
-        scratch += [pltpu.VMEM((memory[1].shape[0] // BLOCK, PAIR, BLOCK), BF)]
+        more = memory[1].shape[0] // BLOCK
+        scratch += [pltpu.VMEM((more, PAIR, BLOCK), BF)]
+        blocks += more
     return pl.pallas_call(
         functools.partial(attend_kernel, memory is not None),
         name="attend",
         grid_spec=pltpu.PrefetchScalarGridSpec(
-            num_scalar_prefetch=3,
-            grid=(blocks,),
+            num_scalar_prefetch=1,
+            grid=(rows // QUERIES,),
             in_specs=in_specs,
             out_specs=(row_block, lane_block),
             scratch_shapes=scratch
             + [
-                pltpu.VMEM((PAIR, BLOCK), F32),
-                pltpu.VMEM((8, BLOCK), F32),
-                pltpu.VMEM((8, BLOCK), F32),
+                pltpu.VMEM((2, blocks, BLOCK, QUERIES), F32),
+                pltpu.VMEM((PAIR, QUERIES), F32),
+                pltpu.VMEM((2, 8, QUERIES), F32),
+                pltpu.VMEM((2, 8, QUERIES), F32),
             ],
         ),
         out_shape=(
@@ -1010,14 +1282,15 @@
             jax.ShapeDtypeStruct((8, rows), F32),
         ),
         compiler_params=pltpu.CompilerParams(vmem_limit_bytes=48 * 2**20),
-    )(*ranges, *operands)
-
-
-def attend_back_kernel(with_memory, local_from, mem_from, mem_to, *refs):
+    )(ranges, *operands)
+
+
+def attend_back_kernel(with_memory, ranges, *refs):
     if with_memory:
         (q, go, o, stat, bounds, k, v, mk, mv, gq, gk, gv, kt, mkt, delta, gq_t, gk_sum, gv_sum) = refs
     else:
         (q, go, o, stat, bounds, k, v, gq, gk, gv, kt, delta, gq_t, gk_sum, gv_sum) = refs
+        mk = mv = mkt = None
     i = pl.program_id(0)
     unit = HEAD ** (-0.5)
     scale = unit * LOG2E
@@ -1035,26 +1308,28 @@
         delta[h : h + 1, :] = jnp.sum(both.T, axis=0, keepdims=True)
     gq_t[...] = jnp.zeros_like(gq_t)
 
-    def run(keys, values, keys_t, low, high, own):
-        def body(j, _):
-            seen = visible(bounds, low, high, j)
-            for h in range(2):
-                query, grad = q[:, heads(h)], go[:, heads(h)]
-                scores = dot_nt(keys[block_rows(j), heads(h)], query) * scale
-                probs = jnp.where(seen, jnp.exp2(scores - stat[h : h + 1, :]), 0.0)
-                grad_probs = dot_nt(values[block_rows(j), heads(h)], grad)
-                grad_scores = (probs * (grad_probs - delta[h : h + 1, :])).astype(BF)
-                gq_t[heads(h), :] += dot_nn(keys_t[j, heads(h), :], grad_scores)
-                if own:
-                    gv_sum[block_rows(j), heads(h)] += dot_nn(probs.astype(BF), grad)
-                    gk_sum[block_rows(j), heads(h)] += dot_nn(grad_scores, query)
-            return 0
-
-        return body
-
-    lax.fori_loop(local_from[i], i + 1, run(k, v, kt, 0, 1, True), 0)
-    if with_memory:
-        lax.fori_loop(mem_from[i], mem_to[i], run(mk, mv, mkt, 2, 3, False), 0)
+    def step(keys, values, keys_t, low, own):
+        def run(masked):
+            def body(j, _):
+                for h in range(2):
+                    query, grad = q[:, heads(h)], go[:, heads(h)]
+                    scores = dot_nt(keys[block_rows(j), heads(h)], query) * scale
+                    probs = jnp.exp2(scores - stat[h : h + 1, :])
+                    if masked:
+                        probs = jnp.where(visible(bounds, low, low + 1, j), probs, 0.0)
+                    grad_probs = dot_nt(values[block_rows(j), heads(h)], grad)
+                    grad_scores = (probs * (grad_probs - delta[h : h + 1, :])).astype(BF)
+                    gq_t[heads(h), :] += dot_nn(keys_t[j, heads(h), :], grad_scores)
+                    if own:
+                        gv_sum[block_rows(j), heads(h)] += dot_nn(probs.astype(BF), grad)
+                        gk_sum[block_rows(j), heads(h)] += dot_nn(grad_scores, query)
+                return 0
+
+            return body
+
+        return run
+
+    each_block(ranges, i, with_memory, step(k, v, kt, 0, True), step(mk, mv, mkt, 2, False))
     gq[...] = (gq_t[...] * unit).T.astype(BF)
 
     @pl.when(i == pl.num_programs(0) - 1)
@@ -1066,8 +1341,8 @@
 def attend_back(q, k, v, memory, bounds, ranges, out, stat, grad):
     rows = q.shape[0]
     blocks = rows // BLOCK
-    row_block = pl.BlockSpec((BLOCK, PAIR), lambda i, *_: (i, 0))
-    lane_block = pl.BlockSpec((8, BLOCK), lambda i, *_: (0, i))
+    row_block = pl.BlockSpec((QUERIES, PAIR), lambda i, *_: (i, 0))
+    lane_block = pl.BlockSpec((8, QUERIES), lambda i, *_: (0, i))
     operands = [q, grad, out, stat, bounds, k, v]
     in_specs = [row_block, row_block, row_block, lane_block, lane_block, VMEM, VMEM]
     scratch = [pltpu.VMEM((blocks, PAIR, BLOCK), BF)]
@@ -1080,59 +1355,83 @@
         functools.partial(attend_back_kernel, memory is not None),
         name="attend_back",
         grid_spec=pltpu.PrefetchScalarGridSpec(
-            num_scalar_prefetch=3,
-            grid=(blocks,),
+            num_scalar_prefetch=1,
+            grid=(rows // QUERIES,),
             in_specs=in_specs,
             out_specs=(row_block, VMEM, VMEM),
             scratch_shapes=scratch
             + [
-                pltpu.VMEM((8, BLOCK), F32),
-                pltpu.VMEM((PAIR, BLOCK), F32),
+                pltpu.VMEM((8, QUERIES), F32),
+                pltpu.VMEM((PAIR, QUERIES), F32),
                 pltpu.VMEM((rows, PAIR), F32),
                 pltpu.VMEM((rows, PAIR), F32),
             ],
         ),
         out_shape=(whole, whole, whole),
         compiler_params=pltpu.CompilerParams(vmem_limit_bytes=48 * 2**20),
-    )(*ranges, *operands)
-
-
-def count(compared):
-    return jnp.sum(compared.astype(jnp.int32), axis=1)
+    )(ranges, *operands)
+
+
+NUMBERS = 8
+
+
+def members(docs):
+    number = jnp.arange(NUMBERS, dtype=jnp.int32)
+    return (docs[None, :] == number[:, None]).astype(jnp.int32)
+
+
+def before(counts):
+    at = jnp.arange(counts.shape[-1])
+    earlier = at[:, None] < at[None, :]
+    return jnp.sum(jnp.where(earlier, counts[..., :, None], 0), axis=-2)
+
+
+def pick(which, table):
+    return jnp.sum(which * table[:, None], axis=0)
 
 
 def mask_ranges(docs, mem_docs, reset):
     rows = docs.shape[0]
-    entries = mem_docs.shape[0]
     at = jnp.arange(rows, dtype=jnp.int32)
-    start = count(docs[None, :] < docs[:, None])
-    mem_low = count(mem_docs[None, :] < docs[:, None])
-    mem_high = count(mem_docs[None, :] <= docs[:, None])
-    mem_low = jnp.where(reset == 0, mem_low, 0)
-    mem_high = jnp.where(reset == 0, mem_high, 0)
+    own, other = members(docs), members(mem_docs)
+    start = pick(own, before(jnp.sum(own, axis=1)))
+    counts = jnp.where(reset == 0, jnp.sum(other, axis=1), 0)
+    mem_low = pick(own, before(counts))
+    mem_high = mem_low + pick(own, counts)
     zero = jnp.zeros_like(start)
     bounds = jnp.stack((start, at + 1, mem_low, mem_high, zero, zero, zero, zero))
 
     def per_block(values):
-        return values.reshape(rows // BLOCK, BLOCK)
-
-    local_from = jnp.min(per_block(start), axis=1) // BLOCK
+        return values.reshape(rows // QUERIES, QUERIES)
+
+    def up(values):
+        return (values + BLOCK - 1) // BLOCK
+
+    step = QUERIES // BLOCK
+    diagonal = jnp.arange(rows // QUERIES, dtype=jnp.int32) * step
+    first = jnp.min(per_block(start), axis=1) // BLOCK
+    full = jnp.clip(up(jnp.max(per_block(start), axis=1)), first, diagonal)
     some = mem_high > mem_low
-    first = jnp.min(per_block(jnp.where(some, mem_low, entries)), axis=1)
-    last = jnp.max(per_block(jnp.where(some, mem_high, 0)), axis=1)
-    mem_from = first // BLOCK
-    mem_to = jnp.maximum((last + BLOCK - 1) // BLOCK, mem_from)
-    return bounds, (local_from, mem_from, mem_to)
+    mem_first = jnp.min(per_block(jnp.where(some, mem_low, mem_docs.shape[0])), axis=1) // BLOCK
+    mem_end = jnp.maximum(up(jnp.max(per_block(mem_high), axis=1)), mem_first)
+    mem_full = jnp.clip(up(jnp.max(per_block(mem_low), axis=1)), mem_first, mem_end)
+    mem_rest = jnp.clip(jnp.min(per_block(mem_high), axis=1) // BLOCK, mem_full, mem_end)
+    columns = (first, full, diagonal, diagonal + step, mem_first, mem_full, mem_rest, mem_end)
+    return bounds, jnp.stack(columns, axis=1)
 
 
 def sort_memory(memory, mem_docs):
     entries = mem_docs.shape[0]
-    at = jnp.arange(entries, dtype=jnp.int32)
-    before = (mem_docs[None, :] < mem_docs[:, None]) | (
-        (mem_docs[None, :] == mem_docs[:, None]) & (at[None, :] < at[:, None])
-    )
-    rank = count(before)
-    moved = (rank[None, :] == at[:, None]).astype(BF)
+    which = members(mem_docs)
+    lanes = which.reshape(-1, HEAD)
+    at = jnp.arange(HEAD)
+    earlier = (at[:, None] < at[None, :]).astype(BF)
+    inside = jnp.dot(lanes.astype(BF), earlier, preferred_element_type=F32).astype(jnp.int32)
+    totals = jnp.sum(lanes, axis=1).reshape(NUMBERS, -1)
+    first = before(jnp.sum(totals, axis=1))[:, None] + before(totals)
+    rank = inside.reshape(NUMBERS, -1, HEAD) + first[:, :, None]
+    rank = jnp.sum(which * rank.reshape(NUMBERS, entries), axis=0)
+    moved = (rank[None, :] == jnp.arange(entries, dtype=jnp.int32)[:, None]).astype(BF)
     return tuple(
         jnp.dot(moved, memory[index], preferred_element_type=F32).astype(BF) for index in range(2)
     )
@@ -1250,7 +1549,7 @@
 
     (rows,), (docs,), (other,), (qkv1_w,), (gains,) = exchange(
         "bring_tokens", 1,
-        [Rows(tokens), Docs(docs), Sibling(downs), gather(qkv1), gather(gains)],
+        [later(Rows(tokens)), Docs(docs), Sibling(downs), gather(qkv1), gather(gains)],
     )
     down1 = pair_rows(down_weight1, other[:each], core)
     down2 = pair_rows(down_weight2, other[each:], core)
@@ -1261,83 +1560,112 @@
     gains = gains[:, :4].astype(F32)
     held = {}
 
+    hops = {}
+    rest2 = jnp.concatenate((gate_up2, out_weight2), axis=1)
+
     def heads1(qkv):
-        swapped, (held["out1"],), (held["gu1"],), (held["down1"],), (mk,), (mv,) = exchange(
+        swapped, (mk,), (mv,), (held["gu1"],), (held["down1"],), (held["out1"],), (held["qkv2"],) = exchange(
             "to_heads_1", 2,
-            [Swap([qkv], True), gather(out_weight1), gather(gate_up1), Gather(down1, pairs),
-             Memory(memory_keys), Memory(memory_values)],
+            [later(Swap([qkv], True)), later(Memory(memory_keys), 3), later(Memory(memory_values), 3),
+             gather(gate_up1), Gather(down1, pairs), gather(out_weight1), gather(qkv2)],
         )
-        held["memory"] = sort_memory((mk, mv), own_mem_docs)
+        held["memory"] = mk, mv
+        swapped, shards = join(swapped, (rest2, down2))
+        hops["rest"] = [gather_column(shard) for shard in shards]
         return swapped
 
     def rows1(out):
-        (attended,), (held["qkv2"],) = exchange(
-            "to_rows_1", 3, [Swap([out], False), gather(qkv2)]
+        ((attended,),) = exchange("to_rows_1", 3, [Swap([out], False)])
+        return attended, held["out1"], held["gu1"], held["down1"]
+
+    def heads2(qkv):
+        held["memory"] = sort_memory(held["memory"], own_mem_docs)
+        (swapped,) = exchange("to_heads_2", 4, [Swap([qkv], True)])
+        swapped, firsts = join(swapped, [group[1] for group in hops["rest"]])
+        hops["rest"] = [
+            (group[0], first, group[2], hop(first, "b"))
+            for group, first in zip(hops["rest"], firsts)
+        ]
+        return swapped
+
+    def rows2(out):
+        out, (rest, down) = join(out, hops["rest"])
+        (attended,), (gate_up_w, out_w), (down_w,) = exchange(
+            "to_rows_2", 5,
+            [Swap([out], False), Assemble(rest, [RowBlocks(count, 2 * ff), RowBlocks(count, width)]),
+             Assemble(down, [pairs])],
         )
-        return attended, held["out1"], held["gu1"], held["down1"]
-
-    def heads2(qkv):
-        swapped, (held["out2"],), (held["gu2"],) = exchange(
-            "to_heads_2", 4, [Swap([qkv], True), gather(out_weight2), gather(gate_up2)]
-        )
-        return swapped
-
-    def rows2(out):
-        (attended,), (down,), (held["cot"],) = exchange(
-            "to_rows_2", 5, [Swap([out], False), Gather(down2, pairs), Rows(cotangent)]
-        )
-        return attended, held["out2"], held["gu2"], down
+        attended, cot = join(attended, cotangent)
+        hops["cot"] = rows_hops(cot)
+        return attended, out_w, gate_up_w, down_w
 
     middle, weights1, kept1 = layer(
         rows.astype(F32), qkv1_w, (gains[:, 0], gains[:, 1]), (heads1, rows1), None, bounds, ranges
     )
+    middle, rest = join(middle, hops["rest"])
+    hops["rest"] = [(column, hop(column, "a"), hop(column, "b")) for column in rest]
+    qkv2_w = held["qkv2"]
     result, weights2, kept2 = layer(
-        middle, held["qkv2"], (gains[:, 2], gains[:, 3]), (heads2, rows2),
+        middle, qkv2_w, (gains[:, 2], gains[:, 3]), (heads2, rows2),
         lambda: held["memory"], bounds, ranges,
     )
-
-    def part(matrix, index, size):
-        return ColumnBlocks(count, size, index)
+    cot = hops["cot"]
+    output = chunk_hops(result.astype(BF))
+
+    def pair_sum(total):
+        half = lax.dynamic_slice_in_dim(total, core * each, each, 0)
+        other = hop(lax.dynamic_slice_in_dim(total, (1 - core) * each, each, 0), "core")
+        return jnp.where(
+            core == 0, jnp.concatenate((half, other), 1), jnp.concatenate((other, half), 1)
+        )
+
+    shapes = ((count, 2 * ff), (count, width), pairs.shape)
+
+    def feed_sums(out_g, gate_up_g, down_g):
+        return CoreSums((gate_up_g, own(gate_up_g)), (out_g, own(out_g)), (down_g, pairs))
 
     grad_mixed, grad_att, out_g2, gain_b2, gate_up_g2, down_g2 = ffn_back(
-        held["cot"].astype(F32), weights2, kept2
-    )
-    (grad_out,), (output,), (gate_s2,), (up_s2,) = exchange(
+        cot.astype(F32), weights2, kept2
+    )
+    (grad_out,), sums2 = exchange(
         "back_to_heads_2", 6,
-        [Swap([grad_att], True), Chunks(result.astype(BF)),
-         Scatter(gate_up_g2, ColumnBlocks(count, ff, 0)),
-         Scatter(gate_up_g2, ColumnBlocks(count, ff, 1), 1)],
-        40,
-    )
+        [Swap([grad_att], True), feed_sums(out_g2, gate_up_g2, down_g2)],
+        48,
+    )
+    sums2 = scatter_second(sums2)
     q, k, v, out, stat = kept2[3:8]
     grads = attend_back(q, k, v, held["memory"], bounds, ranges, out, stat, grad_out)
-    (grad_qkv,), (down_s2,), (out_s2,) = exchange(
-        "back_to_rows_2", 7,
-        [Swap(list(grads), False), Scatter(down_g2, pairs), Scatter(out_g2, own(out_g2), 1)],
-        40,
-    )
+    ((grad_qkv,),) = exchange("back_to_rows_2", 7, [Swap(list(grads), False)])
+    grad_qkv, (sums2, output) = join(grad_qkv, (sums2, output))
+    sums2 = scatter_first(sums2)
     grad_middle, gain_a2, qkv_g2 = projections_back(grad_mixed, grad_qkv, weights2, kept2)
+    (qkv_s2,) = exchange("projection_sums_2", 12, [CoreSums((qkv_g2, own(qkv_g2)))], 24)
+    grad_middle, (sums2, qkv_s2) = join(grad_middle, (sums2, qkv_s2))
+    sums2 = scatter_z(sums2)
+    qkv_s2 = scatter_second(qkv_s2)
 
     grad_mixed, grad_att, out_g1, gain_b1, gate_up_g1, down_g1 = ffn_back(
         grad_middle, weights1, kept1
     )
-    (grad_out,), (gate_s1,), (up_s1,), (qkv_s2,) = exchange(
+    grad_att, qkv_s2 = join(grad_att, qkv_s2)
+    qkv_s2 = scatter_first(qkv_s2)
+    (grad_out,), sums1 = exchange(
         "back_to_heads_1", 8,
-        [Swap([grad_att], True),
-         Scatter(gate_up_g1, ColumnBlocks(count, ff, 0)),
-         Scatter(gate_up_g1, ColumnBlocks(count, ff, 1), 1),
-         Scatter(qkv_g2, own(qkv_g2), 2)],
-        44,
-    )
+        [Swap([grad_att], True), feed_sums(out_g1, gate_up_g1, down_g1)],
+        48,
+    )
+    grad_out, (sums2, qkv_s2) = join(grad_out, (sums2, qkv_s2))
+    qkv_s2 = scatter_z(qkv_s2)
+    sums1 = scatter_second(sums1)
     q, k, v, out, stat = kept1[3:8]
     grads = attend_back(q, k, v, None, bounds, ranges, out, stat, grad_out)
-    (grad_qkv,), (down_s1,), (out_s1,) = exchange(
-        "back_to_rows_1", 9,
-        [Swap(list(grads), False), Scatter(down_g1, pairs), Scatter(out_g1, own(out_g1), 1)],
-        40,
-    )
+    ((grad_qkv,),) = exchange("back_to_rows_1", 9, [Swap(list(grads), False)])
+    grad_qkv, (sums1, qkv_s2) = join(grad_qkv, (sums1, qkv_s2))
+    sums1 = scatter_first(sums1)
     grad_rows, gain_a1, qkv_g1 = projections_back(grad_mixed, grad_qkv, weights1, kept1)
     gain_grads = gain_columns((gain_a1, gain_b1, gain_a2, gain_b2)).astype(BF)
+    grad_rows, sums1 = join(grad_rows, sums1)
+    sums1 = scatter_z(sums1)
     (grad_tokens,), (q_s1,), (k_s1,), (v_s1,), (gain_s,) = exchange(
         "back_to_owners", 10,
         [Chunks(grad_rows.astype(BF))]
@@ -1345,11 +1673,16 @@
         + [Scatter(gain_grads, own(gain_grads), 2)],
         40,
     )
+    gate_up_s2, out_s2, down_s2 = unpack(scatter_end(sums2), shapes)
+    gate_up_s1, out_s1, down_s1 = unpack(scatter_end(sums1), shapes)
+    (qkv_s2,) = unpack(scatter_end(qkv_s2), ((count, 3 * width),))
     q_s2, k_s2, v_s2 = columns(qkv_s2, (width,) * 3)
+    gate_s1, up_s1 = columns(gate_up_s1, (ff, ff))
+    gate_s2, up_s2 = columns(gate_up_s2, (ff, ff))
     return (
         output, grad_tokens.astype(F32),
-        gain_s[:, 0], q_s1, k_s1, v_s1, out_s1, gain_s[:, 1], gate_s1, up_s1, down_s1,
-        gain_s[:, 2], q_s2, k_s2, v_s2, out_s2, gain_s[:, 3], gate_s2, up_s2, down_s2,
+        gain_s[:, 0], q_s1, k_s1, v_s1, out_s1, gain_s[:, 1], gate_s1, up_s1, pair_sum(down_s1),
+        gain_s[:, 2], q_s2, k_s2, v_s2, out_s2, gain_s[:, 3], gate_s2, up_s2, pair_sum(down_s2),
     )
 
 
@@ -1403,5 +1736,5 @@
         P(("grp", "key"), None),
         P(("grp", "key"), None),
     )
-    body = head_local if mesh.shape["key"] == HEADS else gathered_local
+    body = head_local if dict(mesh.shape) == {"grp": 4, "key": HEADS} else gathered_local
     return jax.shard_map(body, mesh=mesh, in_specs=in_specs, out_specs=out_specs, check_vma=False)

time: 1190 us -> 916 us (0.77)
  Pallas kernels: 945 us -> 574 us
  starting transfers between devices: 0 us -> 44.7 us
  local copies, waits for them, and re-layouts: 36.5 us -> 57.4 us
  waiting for transfers between devices: 0 us -> 19.9 us
  other arithmetic: 33.2 us -> 47.9 us
    pallas_call x10 -> x11, Pallas kernels: 779 us -> 479 us  [exchange(): pl.pallas_call(kernel, name=name, out_shape=[o for p in parts for o in p....]
    ppermute x0 -> x33, starting transfers between devices: none -> 44.7 us  [the longest x29 36.8 us: hop(): return lax.ppermute(values, ('grp', 'key'), pairs)]
    pallas_call x2, Pallas kernels: 80.6 us -> 36 us  [attend(): pl.pallas_call(functools.partial(attend_kernel, memory is not None), name...]
    pallas_call x2, Pallas kernels: 85.5 us -> 58.1 us  [attend_back(): pl.pallas_call(functools.partial(attend_back_kernel, memory is not None),...]
    ppermute x0 -> x33, waiting for transfers between devices: none -> 19.9 us  [the longest x29 19.9 us: hop(): return lax.ppermute(values, ('grp', 'key'), pairs)]
    another operation x0 -> x7, other arithmetic: none -> 12.7 us
    unnamed x158 -> x211, local copies, waits for them, and re-layouts: 29.4 us -> 31.9 us
  transfers between devices with their start and end apart: 0 -> 33, of which waited for: 0 -> 4; matrix products, arithmetic and copies ran while one was open for 0% -> 17% of each run, Pallas kernels for 0% -> 39%
where the time goes in v2:
time: 916 us; the launch traced here: 908 us
  Pallas kernels  574 us (63%)
  matrix products  161 us (18%)
  local copies, waits for them, and re-layouts  57.4 us (6%)
  other arithmetic  47.9 us (5%)
  starting transfers between devices  44.7 us (5%)
  waiting for transfers between devices  19.9 us (2%)
    pallas_call x11, Pallas kernels, exchange(): pl.pallas_call(kernel, name=name, out_shape=[o for p in parts for o in p....  479 us
    dot_general x8, matrix products, dot_nt(): lax.dot_general(a, b, (((1,), (1,)), ((), ())), preferred_element_type=F32)  64.4 us
    pallas_call x2, Pallas kernels, attend_back(): pl.pallas_call(functools.partial(attend_back_kernel, memory is not None),...  58.1 us
    dot_general x8, matrix products, dot_tn(): lax.dot_general(a, b, (((0,), (0,)), ((), ())), preferred_element_type=F32)  46.4 us
    ppermute x29, starting transfers between devices, hop(): return lax.ppermute(values, ('grp', 'key'), pairs)  36.8 us
    pallas_call x2, Pallas kernels, attend(): pl.pallas_call(functools.partial(attend_kernel, memory is not None), name...  36 us
    unnamed x211, local copies, waits for them, and re-layouts  31.9 us
    ppermute x29, waiting for transfers between devices, hop(): return lax.ppermute(values, ('grp', 'key'), pairs)  19.9 us
  transfers between devices with their start and end apart: 33, of which 4 were waited for; matrix products, arithmetic and copies ran while one was open for 17% of the time, Pallas kernels for 39%

profile of v2, /device:TPU:1, one launch (start us, length us, event | category | flops | bytes accessed | tf_op | source)
XLA Modules:
  0.0 907.7 jit_solution(15370195446574453673)
XLA Ops:
  5.4 39.7 %bring_tokens.1 = (bf16[512,1024]{1,0:T(8,128)(2,1)S(1)}, s32[4,2048]{1,0:T(4,128)S(1)}, bf16[176,1024]{1,0:T(8,128)(2,1)S(1)}, bf16[1024,3072]{1,0:T(8,128)(2,1)S(1)}, bf16[1024,128]{1,0:T(8,128)(2,1)S(1)}) custom-call(bf16[2,256,1024]{2,1,0:T(8,128)(2,1)S(1)} %copy-done.16, s32[4,256]{1,0:T(4,128)S(1)} %pad_add_fusion.refs_1_, ...), custom_call_target="tpu_custom_call" | custom-call | tf_op jit(solution)/shard_map/bring_tokens/pallas_call | solution.py:1050
  50.1 7.0 convolution_convert_fusion.7.refs_0_
  58.0 131.1 %to_heads_1.1 = (bf16[2048,256]{1,0:T(8,128)(2,1)S(1)}, bf16[2048,256]{1,0:T(8,128)(2,1)S(1)}, bf16[2048,256]{1,0:T(8,128)(2,1)S(1)}, bf16[2048,256]{1,0:T(8,128...) custom-call(bf16[512,3072]{1,0:T(8,128)(2,1)S(1)} %convolution_conve, ...), custom_call_target="tpu_custom_call" | custom-call | tf_op jit(solution)/shard_map/to_heads_1/pallas_call | solution.py:1050
  214.8 12.6 %attend.2 = (bf16[2048,256]{1,0:T(8,128)(2,1)S(1)}, f32[8,2048]{1,0:T(8,128)S(1)}) custom-call(s32[4,8]{1,0:T(4,128)S(1)} %stack.132.ranges, bf16[2048,256]{1,0:T(8,128)(2,1)S(1)} %get-tuple-element.135.refs_0_, bf16[2048,256]{1,0:T(8,128)(2,1)S(1)} %get-tuple-element.136.refs_1_.refs_5_, bf16[2048,256]{1,0:T(8,128)(2,1)S(1)} %get-tuple-element.137.refs_2_.refs_6_, ...), custom_call_target="tpu_custom_call" | custom-call | tf_op jit(solution)/shard_map/attend/pallas_call | solution.py:1264
  228.0 18.5 %to_rows_1.1 = bf16[512,1024]{1,0:T(8,128)(2,1)S(1)} custom-call(bf16[2048,256]{1,0:T(8,128)(2,1)S(1)} %get-tuple-element.138.refs_0_.refs_2_), custom_call_target="tpu_custom_call" | custom-call | tf_op jit(solution)/shard_map/to_rows_1/pallas_call | solution.py:1050
  248.5 9.5 %fusion.58 = f32[512,5632]{1,0:T(8,128)S(1)} fusion(bf16[1024,5632]{1,0:T(8,128)(2,1)} %copy-done.26, f32[512,1024]{1,0:T(8,128)S(1)} %get-tuple-element.321, f32[1024]{0:T(1024)S(1)} %get-tuple-element.244, f32[512]{0:T(512)S(1)} %get-tuple-element.315), kind=kOutput, calls=%fused_computation.239 | convolution fusion | flops 5907152896 | bytes 25171968 | tf_op jit(solution)/shard_map/dot_general | solution.py:1474
  272.1 5.3 collective-permute-done.2
  286.9 44.4 %to_heads_2.1 = (bf16[2048,256]{1,0:T(8,128)(2,1)S(1)}, bf16[2048,256]{1,0:T(8,128)(2,1)S(1)}, bf16[2048,256]{1,0:T(8,128)(2,1)S(1)}) custom-call(bf16[512,3072]{1,0:T(8,128)(2,1)S(1)} %convolution_convert_fusion.6.refs_0_), custom_call_target="tpu_custom_call" | custom-call | tf_op jit(solution)/shard_map/to_heads_2/pallas_call | solution.py:1050
  340.3 5.6 fusion.7.refs_5_.refs_8_
  345.9 23.5 %attend.3 = (bf16[2048,256]{1,0:T(8,128)(2,1)S(1)}, f32[8,2048]{1,0:T(8,128)S(1)}) custom-call(s32[4,8]{1,0:T(4,128)S(1)} %stack.132.ranges, bf16[2048,256]{1,0:T(8,128)(2,1)S(1)} %get-tuple-element.151.refs_0_, bf16[2048,256]{1,0:T(8,128)(2,1)S(1)} %copy-done.6, bf16[2048,256]{1,0:T(8,128)(2,1)S(1)} %copy-done.8, s32[8,2048]{1,0:T(8,128)S(1)} %stack.144.refs_3_.refs_4_, ...), custom_call_target="tpu_custom_call" | custom-call | tf_op jit(solution)/shard_map/attend/pallas_call | solution.py:1264
  370.0 19.3 %to_rows_2.1 = (bf16[512,1024]{1,0:T(8,128)(2,1)S(1)}, bf16[1024,5632]{1,0:T(8,128)(2,1)S(1)}, bf16[1024,1024]{1,0:T(8,128)(2,1)S(1)}, bf16[2816,1024]{1,0:T(8,128)(2,1)S(1)}) custom-call(bf16[2048,256]{1,0:T(8,128)(2,1)S(1)} %get-tuple-element.159.refs_0_.refs_2_, bf16[4,32,6656]{2,1,0:T(8,128)(2,1)S(1)} %pad_maximum_fusion.6.refs_1_, ...), custom_call_target="tpu_custom_call" | custom-call | tf_op jit(solution)/shard_map/to_rows_2/pallas_call | solution.py:1050
  395.3 9.0 fusion.59
  404.5 11.0 %multiply_convert_fusion.4 = (bf16[512,2816]{1,0:T(8,128)(2,1)}, bf16[512,2816]{1,0:T(8,128)(2,1)}, bf16[512,2816]{1,0:T(8,128)(2,1)}) fusion(f32[512,5632]{1,0:T(8,128)} %fusion.59, bf16[2816,1024]{1,0:T(8,128)(2,1)S(1)} %get-tuple-element.172, bf16[256,1024]{1,0:T(8,128)(2,1)S(1)} %get-tuple-element.291, bf16[256,1024]{1,0:T(8,128)(2,1)S(1)} %get-tuple-element.290), kind=kOutput, calls=%fused_computation.13 | convolution fusion | flops 2977955840 | bytes 27000832 | tf_op jit(solution)/shard_map/dot_general | solution.py:1146
  415.4 12.7 %multiply_reduce_fusion = (bf16[1024]{0:T(1024)(128)(2,1)S(1)}, f32[512]{0:T(512)S(1)}, f32[512,1024]{1,0:T(8,128)}) fusion(f32[512,1024]{1,0:T(8,128)S(1)} %get-tuple-element.323, f32[512]{0:T(512)S(1)} %get-tuple-element.319, f32[1024]{0:T(1024)S(1)} %get-tuple-element.242, bf16[1024,5632]{1,0:T(8,128)(2,1)} %copy-done.27, ...), kind=kOutput, calls=%fused_computation.46 | convolution fusion | flops 5920258560 | bytes 21506048 | tf_op jit(solution)/shard_map/dot_general | solution.py:1146
  428.2 12.1 %convolution_convert_fusion.1.refs_1_ = bf16[1024,5632]{1,0:T(8,128)(2,1)} fusion(bf16[512,2816]{1,0:T(8,128)(2,1)} %get-tuple-element.278, bf16[512,2816]{1,0:T(8,128)(2,1)} %get-tuple-element.277, f32[512,1024]{1,0:T(8,128)S(1)} %get-tuple-element.323, f32[1024]{0:T(1024)S(1)} %get-tuple-element.242, f32[512]{0:T(512)S(1)} %get-tuple-element.319), kind=kOutput, calls=%fused_computation.4 | convolution fusion | flops 5924454400 | bytes 19404800 | tf_op jit(solution)/shard_map/dot_general | solution.py:1449
  445.9 5.1 convolution_convert_fusion.5.refs_3_
  450.9 29.7 %back_to_heads_2.1 = (bf16[2048,256]{1,0:T(8,128)(2,1)S(1)}, bf16[4,16,18944]{2,1,0:T(8,128)(2,1)}, bf16[4,16,18944]{2,1,0:T(8,128)(2,1)}, bf16[8,16,18944]{2,1,0:T(8,128)(2,1)}) custom-call(bf16[512,1024]{1,0:T(8,128)(2,1)S(1)} %convolution_convert_fusion.11.refs_0_, bf16[1024,5632]{1,0:T(8,128)(2,1)} %convolution_convert_fusion.1.refs_1_, ...), custom_call_target="tpu_custom_call" | custom-call | tf_op jit(solution)/shard_map/back_to_heads_2/pallas_call | solution.py:1050
  490.4 34.6 %attend_back.2 = (bf16[2048,256]{1,0:T(8,128)(2,1)S(1)}, bf16[2048,256]{1,0:T(8,128)(2,1)S(1)}, bf16[2048,256]{1,0:T(8,128)(2,1)S(1)}) custom-call(s32[4,8]{1,0:T(4,128)S(1)} %stack.132.ranges, bf16[2048,256]{1,0:T(8,128)(2,1)S(1)} %get-tuple-element.151.refs_0_, bf16[2048,256]{1,0:T(8,128)(2,1)S(1)} %get-tuple-element.174.refs_1_, ...), custom_call_target="tpu_custom_call" | custom-call | tf_op jit(solution)/shard_map/attend_back/pallas_call | solution.py:1354
  525.0 36.9 %back_to_rows_2.1 = bf16[512,3072]{1,0:T(8,128)(2,1)S(1)} custom-call(bf16[2048,256]{1,0:T(8,128)(2,1)S(1)} %get-tuple-element.176.refs_0_, bf16[2048,256]{1,0:T(8,128)(2,1)S(1)} %get-tuple-element.177.refs_1_, bf16[2048,256]{1,0:T(8,128)(2,1)S(1)} %get-tuple-element.178.refs_2_), custom_call_target="tpu_custom_call" | custom-call | tf_op jit(solution)/shard_map/back_to_rows_2/pallas_call | solution.py:1050
  568.7 5.7 convolution_convert_fusion.4.refs_0_
  574.5 10.7 %projection_sums_2.1 = (bf16[4,16,6144]{2,1,0:T(8,128)(2,1)S(1)}, bf16[4,16,6144]{2,1,0:T(8,128)(2,1)S(1)}, bf16[8,16,6144]{2,1,0:T(8,128)(2,1)}) custom-call(bf16[1024,3072]{1,0:T(8,128)(2,1)S(1)} %convolution_convert_fusion.4.refs_0_), custom_call_target="tpu_custom_call" | custom-call | tf_op jit(solution)/shard_map/projection_sums_2/pallas_call | solution.py:1050
  586.1 6.1 multiply_reduce_fusion.1
  596.6 9.6 %multiply_convert_fusion.1 = (bf16[512,2816]{1,0:T(8,128)(2,1)}, bf16[512,2816]{1,0:T(8,128)(2,1)}) fusion(f32[512,5632]{1,0:T(8,128)} %copy-done.42, bf16[2816,1024]{1,0:T(8,128)(2,1)S(1)} %bitcast.134, f32[512,1024]{1,0:T(8,128)S(1)} %subtract_add_fusion.1), kind=kOutput, calls=%fused_computation.10 | convolution fusion | flops 2972057600 | bytes 25165824 | tf_op jit(solution)/shard_map/dot_general | solution.py:1146
  616.3 13.0 %multiply_reduce_fusion.2 = (bf16[1024]{0:T(1024)(128)(2,1)S(1)}, f32[512]{0:T(512)S(1)}, f32[512,1024]{1,0:T(8,128)}) fusion(f32[512,1024]{1,0:T(8,128)S(1)} %copy-done.61, f32[512]{0:T(512)S(1)} %copy-done.89, f32[1024]{0:T(1024)S(1)} %copy-done.78, bf16[1024,5632]{1,0:T(8,128)(2,1)} %copy-done.26, bf16[512,2816]{1,0:T(8,128)(2,1)} %get-tuple-element.276, ...), kind=kOutput, calls=%fused_computation.48 | convolution fusion | flops 5920258560 | bytes 21506048 | tf_op jit(solution)/shard_map/dot_general | solution.py:1146
  637.3 11.9 %convolution_convert_fusion.refs_1_ = bf16[1024,5632]{1,0:T(8,128)(2,1)} fusion(bf16[512,2816]{1,0:T(8,128)(2,1)} %get-tuple-element.276, bf16[512,2816]{1,0:T(8,128)(2,1)} %get-tuple-element.275, f32[512,1024]{1,0:T(8,128)S(1)} %copy-done.62, f32[1024]{0:T(1024)S(1)} %copy-done.78, f32[512]{0:T(512)S(1)} %copy-done.89), kind=kOutput, calls=%fused_computation.3 | convolution fusion | flops 5924454400 | bytes 19404800 | tf_op jit(solution)/shard_map/dot_general | solution.py:1449
  649.8 5.1 convolution_convert_fusion.3.refs_3_
  654.8 22.3 %back_to_heads_1.1 = (bf16[2048,256]{1,0:T(8,128)(2,1)S(1)}, bf16[4,16,18944]{2,1,0:T(8,128)(2,1)}, bf16[4,16,18944]{2,1,0:T(8,128)(2,1)}, bf16[8,16,18944]{2,1,0:T(8,128)(2,1)}) custom-call(bf16[512,1024]{1,0:T(8,128)(2,1)S(1)} %convolution_convert_fusion.10.refs_0_, bf16[1024,5632]{1,0:T(8,128)(2,1)} %convolution_convert_fusion.refs_1_, ...), custom_call_target="tpu_custom_call" | custom-call | tf_op jit(solution)/shard_map/back_to_heads_1/pallas_call | solution.py:1050
  697.5 23.6 %attend_back.3 = (bf16[2048,256]{1,0:T(8,128)(2,1)S(1)}, bf16[2048,256]{1,0:T(8,128)(2,1)S(1)}, bf16[2048,256]{1,0:T(8,128)(2,1)S(1)}) custom-call(s32[4,8]{1,0:T(4,128)S(1)} %stack.132.ranges, bf16[2048,256]{1,0:T(8,128)(2,1)S(1)} %copy-done.2, bf16[2048,256]{1,0:T(8,128)(2,1)S(1)} %get-tuple-element.202.refs_1_, bf16[2048,256]{1,0:T(8,128)(2,1)} %copy-done, ...), custom_call_target="tpu_custom_call" | custom-call | tf_op jit(solution)/shard_map/attend_back/pallas_call | solution.py:1354
  721.1 37.4 %back_to_rows_1.1 = bf16[512,3072]{1,0:T(8,128)(2,1)S(1)} custom-call(bf16[2048,256]{1,0:T(8,128)(2,1)S(1)} %get-tuple-element.204.refs_0_, bf16[2048,256]{1,0:T(8,128)(2,1)S(1)} %get-tuple-element.205.refs_1_, bf16[2048,256]{1,0:T(8,128)(2,1)S(1)} %get-tuple-element.206.refs_2_), custom_call_target="tpu_custom_call" | custom-call | tf_op jit(solution)/shard_map/back_to_rows_1/pallas_call | solution.py:1050
  769.0 9.5 %fusion.16 = (bf16[1024]{0:T(1024)(128)(2,1)S(1)}, f32[512]{0:T(512)}, f32[512,1024]{1,0:T(8,128)}) fusion(bf16[512,1024]{1,0:T(8,128)(2,1)S(1)} %copy-done.12, f32[512]{0:T(512)S(1)} %copy-done.85, f32[1024]{0:T(1024)S(1)} %copy-done.82, bf16[512,3072]{1,0:T(8,128)(2,1)} %copy-done.14, bf16[1024,3072]{1,0:T(8,128)(2,1)} %copy-done.28), kind=kOutput, calls=%fused_computation.45 | convolution fusion | flops 3224893952 | bytes 12593152 | tf_op jit(solution)/shard_map/dot_general | solution.py:1146
  784.2 10.7 %collective-permute-done.27 = bf16[4,16,18944]{2,1,0:T(8,128)(2,1)} collective-permute-done((bf16[4,16,18944]{2,1,0:T(8,128)(2,1)}, bf16[4,16,18944]{2,1,0:T(8,128)(2,1)}, u32[]{:S(2)}, u32[]{:S(2)}) %collective-permute-start.27) | collective-permute-done | bytes 2424864 | tf_op jit(solution)/shard_map/ppermute | solution.py:1080
  806.0 89.4 %back_to_owners.1 = (bf16[2,256,1024]{2,1,0:T(8,128)(2,1)S(1)}, f32[32,1024]{1,0:T(8,128)S(1)}, f32[32,1024]{1,0:T(8,128)S(1)}, f32[32,1024]{1,0:T(8,128)S(1)}, f32[32,128]{1,0:T(8,128)S(1)}) custom-call(bf16[512,1024]{1,0:T(8,128)(2,1)S(1)} %fusion.13.refs_0_, bf16[1024,3072]{1,0:T(8,128)(2,1)S(1)} %convolution_convert_fusion.2.refs_1_.refs_2_.refs_3_, ...), custom_call_target="tpu_custom_call" | custom-call | tf_op jit(solution)/shard_map/back_to_owners/pallas_call | solution.py:1050
  (418 shorter events, 182.3 us)
Async XLA Ops:
  201.8 61.6 %collective-permute-start.3 = (bf16[176,512]{1,0:T(8,128)(2,1)S(1)}, bf16[176,512]{1,0:T(8,128)(2,1)}, u32[]{:S(2)}, u32[]{:S(2)}) collective-permute-start(bf16[176,512]{1,0:T(8,128)(2,1)S(1)} %constant_dynamic-slice_fusion.2), channel_id=1, source_target_pairs={{0,2},{1,3},{2,0},{3,1},{4,6},{5,7},{6,4},{7,5},{8,10},{9,11},{10,... | collective-permute-start | bytes 540680 | tf_op jit(solution)/shard_map/ppermute | solution.py:1080
  201.8 68.4 %collective-permute-start.4 = (bf16[176,512]{1,0:T(8,128)(2,1)S(1)}, bf16[176,512]{1,0:T(8,128)(2,1)}, u32[]{:S(2)}, u32[]{:S(2)}) collective-permute-start(bf16[176,512]{1,0:T(8,128)(2,1)S(1)} %constant_dynamic-slice_fusion.2), channel_id=1, source_target_pairs={{0,4},{1,5},{2,6},{3,7},{4,0},{5,1},{6,2},{7,3},{8,12},{9,13},{10,... | collective-permute-start | bytes 540680 | tf_op jit(solution)/shard_map/ppermute | solution.py:1080
  206.5 63.8 %collective-permute-start.5 = (bf16[176,512]{1,0:T(8,128)(2,1)S(1)}, bf16[176,512]{1,0:T(8,128)(2,1)}, u32[]{:S(2)}, u32[]{:S(2)}) collective-permute-start(bf16[176,512]{1,0:T(8,128)(2,1)S(1)} %constant_dynamic-slice_fusion.2), channel_id=1, source_target_pairs={{0,6},{1,7},{2,4},{3,5},{4,2},{5,3},{6,0},{7,1},{8,14},{9,15},{10,... | collective-permute-start | bytes 540680 | tf_op jit(solution)/shard_map/ppermute | solution.py:1080
  206.5 65.6 %collective-permute-start = (bf16[32,6656]{1,0:T(8,128)(2,1)}, bf16[32,6656]{1,0:T(8,128)(2,1)}, u32[]{:S(2)}, u32[]{:S(2)}) collective-permute-start(bf16[32,6656]{1,0:T(8,128)(2,1)} %pad_maximum_fusion.10), channel_id=1, source_target_pairs={{0,2},{1,3},{2,0},{3,1},{4,6},{5,7},{6,4},{7,5},{8,10},{9,11},{10,... | collective-permute-start | bytes 1277960 | tf_op jit(solution)/shard_map/ppermute | solution.py:1080
  206.7 65.3 %collective-permute-start.1 = (bf16[32,6656]{1,0:T(8,128)(2,1)}, bf16[32,6656]{1,0:T(8,128)(2,1)}, u32[]{:S(2)}, u32[]{:S(2)}) collective-permute-start(bf16[32,6656]{1,0:T(8,128)(2,1)} %pad_maximum_fusion.10), channel_id=1, source_target_pairs={{0,4},{1,5},{2,6},{3,7},{4,0},{5,1},{6,2},{7,3},{8,12},{9,13},{10,... | collective-permute-start | bytes 1277960 | tf_op jit(solution)/shard_map/ppermute | solution.py:1080
  263.3 14.0 %collective-permute-start.2 = (bf16[32,6656]{1,0:T(8,128)(2,1)}, bf16[32,6656]{1,0:T(8,128)(2,1)S(1)}, u32[]{:S(2)}, u32[]{:S(2)}) collective-permute-start(bf16[32,6656]{1,0:T(8,128)(2,1)} %pad_maximum_fusion.10), channel_id=1, source_target_pairs={{0,6},{1,7},{2,4},{3,5},{4,2},{5,3},{6,0},{7,1},{8,14},{9,15},{10,... | collective-permute-start | bytes 1277960 | tf_op jit(solution)/shard_map/ppermute | solution.py:1080
  278.8 54.4 %collective-permute-start.6 = (bf16[4,32,6656]{2,1,0:T(8,128)(2,1)S(1)}, bf16[4,32,6656]{2,1,0:T(8,128)(2,1)}, u32[]{:S(2)}, u32[]{:S(2)}) collective-permute-start(bf16[4,32,6656]{2,1,0:T(8,128)(2,1)S(1)} %pad_maximum_fusion.6.refs_1_), channel_id=1, source_target_pairs={{0,8},{1,17},{2,10},{3,19},{4,12},{5,21},{6,14},{7,23},{8,0},{9,25... | collective-permute-start | bytes 5111816 | tf_op jit(solution)/shard_map/ppermute | solution.py:1080
  279.4 90.0 %collective-permute-start.8 = (bf16[4,32,6656]{2,1,0:T(8,128)(2,1)S(1)}, bf16[4,32,6656]{2,1,0:T(8,128)(2,1)}, u32[]{:S(2)}, u32[]{:S(2)}) collective-permute-start(bf16[4,32,6656]{2,1,0:T(8,128)(2,1)S(1)} %pad_maximum_fusion.6.refs_1_), channel_id=1, source_target_pairs={{0,16},{1,9},{2,18},{3,11},{4,20},{5,13},{6,22},{7,15},{8,24},{9,1... | collective-permute-start | bytes 5111816 | tf_op jit(solution)/shard_map/ppermute | solution.py:1080
  280.7 52.6 %collective-permute-start.7 = (bf16[4,176,512]{2,1,0:T(8,128)(2,1)S(1)}, bf16[4,176,512]{2,1,0:T(8,128)(2,1)}, u32[]{:S(2)}, u32[]{:S(2)}) collective-permute-start(bf16[4,176,512]{2,1,0:T(8,128)(2,1)S(1)} %pad_maximum_fusion.9.refs_5_), channel_id=1, source_target_pairs={{0,8},{1,17},{2,10},{3,19},{4,12},{5,21},{6,14},{7,23},{8,0},{9,25... | collective-permute-start | bytes 2162696 | tf_op jit(solution)/shard_map/ppermute | solution.py:1080
  333.3 36.7 %collective-permute-start.9 = (bf16[4,32,6656]{2,1,0:T(8,128)(2,1)}, bf16[4,32,6656]{2,1,0:T(8,128)(2,1)}, u32[]{:S(2)}, u32[]{:S(2)}) collective-permute-start(bf16[4,32,6656]{2,1,0:T(8,128)(2,1)} %collective-permute-done.6.refs_2_), channel_id=1, source_target_pairs={{0,16},{1,9},{2,18},{3,11},{4,20},{5,13},{6,22},{7,15},{8,24},{9,1... | collective-permute-start | bytes 5111816 | tf_op jit(solution)/shard_map/ppermute | solution.py:1080
  334.6 34.7 %collective-permute-start.10 = (bf16[4,176,512]{2,1,0:T(8,128)(2,1)S(1)}, bf16[4,176,512]{2,1,0:T(8,128)(2,1)}, u32[]{:S(2)}, u32[]{:S(2)}) collective-permute-start(bf16[4,176,512]{2,1,0:T(8,128)(2,1)S(1)} %pad_maximum_fusion.9.refs_5_), channel_id=1, source_target_pairs={{0,16},{1,9},{2,18},{3,11},{4,20},{5,13},{6,22},{7,15},{8,24},{9,1... | collective-permute-start | bytes 2162696 | tf_op jit(solution)/shard_map/ppermute | solution.py:1080
  334.7 35.3 %collective-permute-start.11 = (bf16[4,176,512]{2,1,0:T(8,128)(2,1)}, bf16[4,176,512]{2,1,0:T(8,128)(2,1)}, u32[]{:S(2)}, u32[]{:S(2)}) collective-permute-start(bf16[4,176,512]{2,1,0:T(8,128)(2,1)} %collective-permute-done.7.refs_6_), channel_id=1, source_target_pairs={{0,16},{1,9},{2,18},{3,11},{4,20},{5,13},{6,22},{7,15},{8,24},{9,1... | collective-permute-start | bytes 2162696 | tf_op jit(solution)/shard_map/ppermute | solution.py:1080
  389.5 14.9 %collective-permute-start.12 = (bf16[256,1024]{1,0:T(8,128)(2,1)S(1)}, bf16[256,1024]{1,0:T(8,128)(2,1)S(1)}, u32[]{:S(2)}, u32[]{:S(2)}) collective-permute-start(bf16[256,1024]{1,0:T(8,128)(2,1)S(1)} %get-tuple-element.292), channel_id=1, source_target_pairs={{0,4},{1,0},{2,5},{3,1},{4,6},{5,2},{6,7},{7,3},{8,12},{9,8},{10,1... | collective-permute-start | bytes 1572872 | tf_op jit(solution)/shard_map/ppermute | solution.py:1086
  389.7 14.7 %collective-permute-start.13 = (bf16[256,1024]{1,0:T(8,128)(2,1)S(1)}, bf16[256,1024]{1,0:T(8,128)(2,1)S(1)}, u32[]{:S(2)}, u32[]{:S(2)}) collective-permute-start(bf16[256,1024]{1,0:T(8,128)(2,1)S(1)} %get-tuple-element.293), channel_id=1, source_target_pairs={{0,0},{1,4},{2,1},{3,5},{4,2},{5,6},{6,3},{7,7},{8,8},{9,12},{10,9... | collective-permute-start | bytes 1572872 | tf_op jit(solution)/shard_map/ppermute | solution.py:1086
  480.7 82.4 %collective-permute-start.14 = (bf16[8,16,18944]{2,1,0:T(8,128)(2,1)}, bf16[8,16,18944]{2,1,0:T(8,128)(2,1)}, u32[]{:S(2)}, u32[]{:S(2)}) collective-permute-start(bf16[8,16,18944]{2,1,0:T(8,128)(2,1)} %get-tuple-element.181), channel_id=1, source_target_pairs={{0,16},{1,9},{2,18},{3,11},{4,20},{5,13},{6,22},{7,15},{8,24},{9,1... | collective-permute-start | bytes 14549000 | tf_op jit(solution)/shard_map/ppermute | solution.py:1080
  486.9 74.9 %collective-permute-start.15 = (bf16[256,1024]{1,0:T(8,128)(2,1)S(1)}, bf16[256,1024]{1,0:T(8,128)(2,1)S(1)}, u32[]{:S(2)}, u32[]{:S(2)}) collective-permute-start(bf16[256,1024]{1,0:T(8,128)(2,1)S(1)} %get-tuple-element.288), channel_id=1, source_target_pairs={{4,0},{0,1},{5,2},{1,3},{6,4},{2,5},{7,6},{3,7},{12,8},{8,9},{13,1... | collective-permute-start | bytes 1572872 | tf_op jit(solution)/shard_map/ppermute | solution.py:1086
  487.3 74.6 %collective-permute-start.16 = (bf16[256,1024]{1,0:T(8,128)(2,1)S(1)}, bf16[256,1024]{1,0:T(8,128)(2,1)S(1)}, u32[]{:S(2)}, u32[]{:S(2)}) collective-permute-start(bf16[256,1024]{1,0:T(8,128)(2,1)S(1)} %get-tuple-element.289), channel_id=1, source_target_pairs={{0,0},{4,1},{1,2},{5,3},{2,4},{6,5},{3,6},{7,7},{8,8},{12,9},{9,10... | collective-permute-start | bytes 1572872 | tf_op jit(solution)/shard_map/ppermute | solution.py:1086
  567.6 29.0 %collective-permute-start.17 = (bf16[4,16,18944]{2,1,0:T(8,128)(2,1)}, bf16[4,16,18944]{2,1,0:T(8,128)(2,1)}, u32[]{:S(2)}, u32[]{:S(2)}) collective-permute-start(bf16[4,16,18944]{2,1,0:T(8,128)(2,1)} %add_convert_fusion.1), channel_id=1, source_target_pairs={{0,8},{1,17},{2,10},{3,19},{4,12},{5,21},{6,14},{7,23},{8,0},{9,25... | collective-permute-start | bytes 7274504 | tf_op jit(solution)/shard_map/ppermute | solution.py:1080
  606.2 29.0 %collective-permute-start.18 = (bf16[8,16,6144]{2,1,0:T(8,128)(2,1)}, bf16[8,16,6144]{2,1,0:T(8,128)(2,1)}, u32[]{:S(2)}, u32[]{:S(2)}) collective-permute-start(bf16[8,16,6144]{2,1,0:T(8,128)(2,1)} %get-tuple-element.193), channel_id=1, source_target_pairs={{0,16},{1,9},{2,18},{3,11},{4,20},{5,13},{6,22},{7,15},{8,24},{9,1... | collective-permute-start | bytes 4718600 | tf_op jit(solution)/shard_map/ppermute | solution.py:1080
  611.7 65.6 %collective-permute-start.19 = (bf16[16,18944]{1,0:T(8,128)(2,1)}, bf16[16,18944]{1,0:T(8,128)(2,1)}, u32[]{:S(2)}, u32[]{:S(2)}) collective-permute-start(bf16[16,18944]{1,0:T(8,128)(2,1)} %get-tuple-element.285), channel_id=1, source_target_pairs={{0,2},{1,3},{2,0},{3,1},{4,6},{5,7},{6,4},{7,5},{8,10},{9,11},{10,... | collective-permute-start | bytes 1818632 | tf_op jit(solution)/shard_map/ppermute | solution.py:1080
  612.2 65.1 %collective-permute-start.20 = (bf16[16,18944]{1,0:T(8,128)(2,1)S(1)}, bf16[16,18944]{1,0:T(8,128)(2,1)}, u32[]{:S(2)}, u32[]{:S(2)}) collective-permute-start(bf16[16,18944]{1,0:T(8,128)(2,1)S(1)} %get-tuple-element.284), channel_id=1, source_target_pairs={{0,4},{1,5},{2,6},{3,7},{4,0},{5,1},{6,2},{7,3},{8,12},{9,13},{10,... | collective-permute-start | bytes 1818632 | tf_op jit(solution)/shard_map/ppermute | solution.py:1080
  613.3 63.9 %collective-permute-start.21 = (bf16[16,18944]{1,0:T(8,128)(2,1)S(1)}, bf16[16,18944]{1,0:T(8,128)(2,1)}, u32[]{:S(2)}, u32[]{:S(2)}) collective-permute-start(bf16[16,18944]{1,0:T(8,128)(2,1)S(1)} %get-tuple-element.283), channel_id=1, source_target_pairs={{0,6},{1,7},{2,4},{3,5},{4,2},{5,3},{6,0},{7,1},{8,14},{9,15},{10,... | collective-permute-start | bytes 1818632 | tf_op jit(solution)/shard_map/ppermute | solution.py:1080
  636.6 40.7 %collective-permute-start.22 = (bf16[4,16,6144]{2,1,0:T(8,128)(2,1)S(1)}, bf16[4,16,6144]{2,1,0:T(8,128)(2,1)S(1)}, u32[]{:S(2)}, u32[]{:S(2)}) collective-permute-start(bf16[4,16,6144]{2,1,0:T(8,128)(2,1)S(1)} %add_convert_fusion.3), channel_id=1, source_target_pairs={{0,8},{1,17},{2,10},{3,19},{4,12},{5,21},{6,14},{7,23},{8,0},{9,25... | collective-permute-start | bytes 2359304 | tf_op jit(solution)/shard_map/ppermute | solution.py:1080
  677.1 84.9 %collective-permute-start.23 = (bf16[8,16,18944]{2,1,0:T(8,128)(2,1)}, bf16[8,16,18944]{2,1,0:T(8,128)(2,1)}, u32[]{:S(2)}, u32[]{:S(2)}) collective-permute-start(bf16[8,16,18944]{2,1,0:T(8,128)(2,1)} %get-tuple-element.209), channel_id=1, source_target_pairs={{0,16},{1,9},{2,18},{3,11},{4,20},{5,13},{6,22},{7,15},{8,24},{9,1... | collective-permute-start | bytes 14549000 | tf_op jit(solution)/shard_map/ppermute | solution.py:1080
  683.2 77.0 %collective-permute-start.32 = (f32[88,512]{1,0:T(8,128)}, f32[88,512]{1,0:T(8,128)}, u32[]{:S(2)}, u32[]{:S(2)}) collective-permute-start(f32[88,512]{1,0:T(8,128)} %get-tuple-element.305), channel_id=1, source_target_pairs={{0,1},{1,0},{2,3},{3,2},{4,5},{5,4},{6,7},{7,6},{8,9},{9,8},{10,11... | collective-permute-start | bytes 540680 | tf_op jit(solution)/shard_map/ppermute | solution.py:1080
  689.9 72.1 %collective-permute-start.24 = (bf16[16,6144]{1,0:T(8,128)(2,1)}, bf16[16,6144]{1,0:T(8,128)(2,1)}, u32[]{:S(2)}, u32[]{:S(2)}) collective-permute-start(bf16[16,6144]{1,0:T(8,128)(2,1)} %get-tuple-element.296), channel_id=1, source_target_pairs={{0,2},{1,3},{2,0},{3,1},{4,6},{5,7},{6,4},{7,5},{8,10},{9,11},{10,... | collective-permute-start | bytes 589832 | tf_op jit(solution)/shard_map/ppermute | solution.py:1080
  690.2 71.9 %collective-permute-start.25 = (bf16[16,6144]{1,0:T(8,128)(2,1)}, bf16[16,6144]{1,0:T(8,128)(2,1)}, u32[]{:S(2)}, u32[]{:S(2)}) collective-permute-start(bf16[16,6144]{1,0:T(8,128)(2,1)} %get-tuple-element.295), channel_id=1, source_target_pairs={{0,4},{1,5},{2,6},{3,7},{4,0},{5,1},{6,2},{7,3},{8,12},{9,13},{10,... | collective-permute-start | bytes 589832 | tf_op jit(solution)/shard_map/ppermute | solution.py:1080
  691.7 70.3 %collective-permute-start.26 = (bf16[16,6144]{1,0:T(8,128)(2,1)}, bf16[16,6144]{1,0:T(8,128)(2,1)}, u32[]{:S(2)}, u32[]{:S(2)}) collective-permute-start(bf16[16,6144]{1,0:T(8,128)(2,1)} %get-tuple-element.294), channel_id=1, source_target_pairs={{0,6},{1,7},{2,4},{3,5},{4,2},{5,3},{6,0},{7,1},{8,14},{9,15},{10,... | collective-permute-start | bytes 589832 | tf_op jit(solution)/shard_map/ppermute | solution.py:1080
  765.9 29.0 %collective-permute-start.27 = (bf16[4,16,18944]{2,1,0:T(8,128)(2,1)}, bf16[4,16,18944]{2,1,0:T(8,128)(2,1)}, u32[]{:S(2)}, u32[]{:S(2)}) collective-permute-start(bf16[4,16,18944]{2,1,0:T(8,128)(2,1)} %add_convert_fusion), channel_id=1, source_target_pairs={{0,8},{1,17},{2,10},{3,19},{4,12},{5,21},{6,14},{7,23},{8,0},{9,25... | collective-permute-start | bytes 7274504 | tf_op jit(solution)/shard_map/ppermute | solution.py:1080
  798.4 99.4 %collective-permute-start.28 = (bf16[16,18944]{1,0:T(8,128)(2,1)S(1)}, bf16[16,18944]{1,0:T(8,128)(2,1)S(1)}, u32[]{:S(2)}, u32[]{:S(2)}) collective-permute-start(bf16[16,18944]{1,0:T(8,128)(2,1)S(1)} %get-tuple-element.280), channel_id=1, source_target_pairs={{0,2},{1,3},{2,0},{3,1},{4,6},{5,7},{6,4},{7,5},{8,10},{9,11},{10,... | collective-permute-start | bytes 1818632 | tf_op jit(solution)/shard_map/ppermute | solution.py:1080
  799.2 98.5 %collective-permute-start.29 = (bf16[16,18944]{1,0:T(8,128)(2,1)S(1)}, bf16[16,18944]{1,0:T(8,128)(2,1)S(1)}, u32[]{:S(2)}, u32[]{:S(2)}) collective-permute-start(bf16[16,18944]{1,0:T(8,128)(2,1)S(1)} %get-tuple-element.282), channel_id=1, source_target_pairs={{0,4},{1,5},{2,6},{3,7},{4,0},{5,1},{6,2},{7,3},{8,12},{9,13},{10,... | collective-permute-start | bytes 1818632 | tf_op jit(solution)/shard_map/ppermute | solution.py:1080
  800.8 96.9 %collective-permute-start.30 = (bf16[16,18944]{1,0:T(8,128)(2,1)S(1)}, bf16[16,18944]{1,0:T(8,128)(2,1)S(1)}, u32[]{:S(2)}, u32[]{:S(2)}) collective-permute-start(bf16[16,18944]{1,0:T(8,128)(2,1)S(1)} %get-tuple-element.281), channel_id=1, source_target_pairs={{0,6},{1,7},{2,4},{3,5},{4,2},{5,3},{6,0},{7,1},{8,14},{9,15},{10,... | collective-permute-start | bytes 1818632 | tf_op jit(solution)/shard_map/ppermute | solution.py:1080
  (105 other events, 1494.2 us)

commit v3 on v2

--- a/solution.py
+++ b/solution.py
@@ -377,6 +377,7 @@
 LOG2E = 1.4426950408889634
 BLOCK = 512
 QUERIES = 512
+ROOM = 60 * 2**20
 LOCAL = 4
 HEAD = 128
 PAIR = 2 * HEAD
@@ -717,7 +718,7 @@
             first(dz).start()
             second(0, dz).start()
             across((0, 0, dz)).start()
-        yield
+            yield
         for dz in (0,) + turns:
             arrived((1, 0, dz), 8 + dz)
             second(1, dz).start()
@@ -744,16 +745,104 @@
         mine.wait()
 
 
-def add_into(dst, parts, tile):
+def tile_of(rows, width):
+    sizes = [width // n for n in range(1, width // HEAD + 1) if width % (n * HEAD) == 0]
+    return next((size for size in sizes if rows * size <= 32768), HEAD)
+
+
+def add_into(dst, parts):
     rows, width = dst.shape
-
-    @pl.loop(0, width // tile)
-    def _(t):
-        cut = pl.ds(pl.multiple_of(t * tile, tile), tile)
+    tile = tile_of(rows, width)
+
+    def one(cut):
         total = parts[0][:, cut].astype(F32)
         for part in parts[1:]:
             total += part[:, cut].astype(F32)
         dst[:, cut] = total.astype(dst.dtype)
+
+    if tile == width:
+        one(pl.ds(0, width))
+    else:
+
+        @pl.loop(0, width // tile)
+        def _(t):
+            one(pl.ds(pl.multiple_of(t * tile, tile), tile))
+
+
+class Front:
+    def __init__(self, tokens, shard, blocks, gains, gain_blocks, rest):
+        self.rest = rest
+        self.parts = [Gather(shard, blocks), Gather(gains, gain_blocks), Rows(tokens)]
+        (rows,) = self.parts[2].outs
+        rows, width = rows.shape
+        columns = blocks.shape[1]
+        qkv = jax.ShapeDtypeStruct((rows, columns), BF)
+        self.swap = Swap([qkv], True)
+        self.arrays = [part.arrays[0] for part in self.parts]
+        self.outs = [part.outs[0] for part in self.parts]
+        self.outs += [jax.ShapeDtypeStruct((rows, width), BF)] + self.swap.outs
+        self.out_specs = [ANY] * 3 + [VMEM] + self.swap.out_specs
+        self.scratch = [s for part in self.parts for s in part.scratch] + self.swap.scratch
+        self.scratch += [
+            pltpu.VMEM((width, columns), BF),
+            pltpu.VMEM((rows, width), BF),
+            pltpu.VMEM(self.parts[1].outs[0].shape, BF),
+            pltpu.VMEM((rows, columns), BF),
+            SEND((3,)),
+        ]
+
+    def run(self, at, ins, outs, scratch):
+        stages, rest = [], list(scratch)
+        for index, part in enumerate(self.parts):
+            held = [rest.pop(0) for _ in part.scratch]
+            stages.append(part.run(at, [ins[index]], [outs[index]], held))
+        swap_scratch = [rest.pop(0) for _ in self.swap.scratch]
+        weights, tokens, gains, qkv, load = rest
+        normed, swapped = outs[3], outs[4:]
+        gathers, rows = stages[:2], stages[2]
+
+        def step():
+            for stage in gathers:
+                next(stage)
+
+        step()
+        yield
+        for _ in range(3):
+            step()
+        next(rows)
+        yield
+        step()
+        step()
+        for stage in stages:
+            for _ in stage:
+                pass
+        copies = [
+            local(src, dst, load.at[i])
+            for i, (src, dst) in enumerate(zip((outs[2], outs[1], outs[0]), (tokens, gains, weights)))
+        ]
+        for copy in copies:
+            copy.start()
+        yield
+        for copy in copies:
+            copy.wait()
+        values = tokens[...].astype(F32)
+        gain = gains[...].astype(F32).T[0:1, :]
+        normed[...] = (values * inverse_rms(values) * gain).astype(BF)
+        tile = 512
+
+        @pl.loop(0, qkv.shape[1] // tile)
+        def _(t):
+            cut = pl.ds(pl.multiple_of(t * tile, tile), tile)
+            qkv[:, cut] = dot_nn(normed[...], weights[:, cut]).astype(BF)
+
+        for _ in range(self.rest):
+            yield
+        swap = self.swap.run(at, [qkv], swapped, swap_scratch)
+        next(swap)
+        yield
+        yield "last"
+        for _ in swap:
+            pass
 
 
 class Assemble:
@@ -763,32 +852,40 @@
         self.outs = [jax.ShapeDtypeStruct(b.whole(4 * LOCAL), groups[0].dtype) for b in blocks]
         self.out_specs = [ANY] * len(blocks)
         n = len(blocks)
-        self.scratch = [SEND((n, 16)), SEND((n, 16)), SEND((n, 16))]
+        self.scratch = [SEND((n, 16)), SEND((n, 16)), SEND((n, 16)), SEND((16,))]
+        self.scratch += [pltpu.VMEM((16,) + groups[0].shape[1:], groups[0].dtype)]
 
     def run(self, at, ins, outs, scratch):
-        send, recv, here = scratch
+        send, recv, here, load, held = scratch
+
+        def fetch(slot):
+            return local(ins[slot // 4].at[slot % 4], held.at[slot], load.at[slot])
 
         def each():
-            begin = 0
-            for index, blocks in enumerate(self.blocks):
-                for slot in range(16):
+            for slot in range(16):
+                begin = 0
+                for index, blocks in enumerate(self.blocks):
                     yield index, slot, pl.ds(begin, blocks.shape[1])
-                begin += blocks.shape[1]
+                    begin += blocks.shape[1]
 
         def spot(index, slot, core):
             return self.blocks[index].at(outs[index], at.chip(*STEPS[slot], core), core)
 
         def copies(index, slot, cut):
-            src = ins[slot // 4].at[slot % 4, :, cut]
+            src = held.at[slot, :, cut]
             dst = spot(index, slot, at.core)
             return remote(
                 src, dst, send.at[index, slot], recv.at[index, slot], at.sibling()
             ), local(src, dst, here.at[index, slot])
 
-        for spec in each():
-            for copy in copies(*spec):
+        for slot in range(16):
+            fetch(slot).start()
+        yield
+        for index, slot, cut in each():
+            if index == 0:
+                fetch(slot).wait()
+            for copy in copies(index, slot, cut):
                 copy.start()
-        yield
         yield "last"
         for index, slot, cut in each():
             across, own = copies(index, slot, cut)
@@ -859,7 +956,6 @@
                         add_into(
                             packed.at[slot, :, pl.ds(begin, width)],
                             [own[index].at[slot, cut, :], near[index].at[slot, cut, :]],
-                            512,
                         )
                         begin += width
                 keep(slot, group, first).start()
@@ -879,11 +975,139 @@
 def unpack(total, shapes):
     blocks, begin = [], 0
     for rows, width in shapes:
-        parts = rows // PACK
-        cut = total[:, begin : begin + parts * width].reshape(PACK, parts, width)
-        blocks.append(cut.transpose(1, 0, 2).reshape(rows, width))
-        begin += parts * width
+        parts = []
+        for _ in range(rows // PACK):
+            parts.append(total[:, begin : begin + width])
+            begin += width
+        blocks.append(jnp.concatenate(parts, axis=0))
     return blocks
+
+
+class LineSums:
+    def __init__(self, terms, shapes, cuts, rest=0):
+        self.arrays = list(terms)
+        self.rest = rest
+        self.shapes = shapes
+        self.outs = [jax.ShapeDtypeStruct(shape, F32) for shape in shapes]
+        self.out_specs = [VMEM] * len(shapes)
+        self.segments, begin = [], 0
+        for index, (rows, width) in enumerate(shapes):
+            for part in range(rows // PACK):
+                self.segments.append((index, part, begin, width))
+                begin += width
+        self.pieces = []
+        for group in cuts:
+            held = [s for s in self.segments if s[0] in group]
+            first = held[0][2]
+            self.pieces.append((first, held[-1][2] + held[-1][3] - first, held))
+        n = len(self.pieces)
+        box = (PACK, begin)
+        self.scratch = [pltpu.VMEM((4,) + box, BF) for _ in terms]
+        self.scratch += [pltpu.VMEM((4,) + box, BF), pltpu.VMEM((4,) + box, BF)]
+        self.scratch += [pltpu.VMEM((2,) + box, BF), pltpu.VMEM(box, BF)]
+        self.scratch += [SEND((len(terms), 4)), SEND((6, n)), SEND((6, n))]
+
+    def run(self, at, ins, outs, scratch):
+        n = len(ins)
+        terms = scratch[:n]
+        low, outer_box, far_box, inner_box, load, send, recv = scratch[n:]
+        inner = flip(at.z // 2, lax.rem(at.z, 2))
+        inside, outside = pl.when(inner == 1), pl.when(inner == 0)
+        near, far = at.device(0, 0, 1), at.device(0, 0, 3)
+        pieces = range(len(self.pieces))
+
+        def fetch(index, dz):
+            return local(ins[index].at[dz], terms[index].at[dz], load.at[index, dz])
+
+        def columns_of(c):
+            first, width, _ = self.pieces[c]
+            return pl.ds(first, width)
+
+        def hand(kind, c):
+            cut = columns_of(c)
+            src, dst, target = {
+                1: (low.at[1, :, cut], outer_box.at[1, :, cut], near),
+                2: (low.at[2, :, cut], outer_box.at[2, :, cut], near),
+                3: (low.at[3, :, cut], outer_box.at[3, :, cut], near),
+                0: (low.at[3, :, cut], far_box.at[0, :, cut], far),
+                4: (low.at[2, :, cut], far_box.at[1, :, cut], far),
+                5: (low.at[1, :, cut], inner_box.at[:, cut], near),
+            }[kind]
+            return remote(src, dst, send.at[kind, c], recv.at[kind, c], target)
+
+        def settle(c, dz, more):
+            for _, _, begin, width in self.pieces[c][2]:
+                cut = pl.ds(begin, width)
+                parts = [term.at[dz, :, cut] for term in terms] + [m.at[:, cut] for m in more]
+                add_into(low.at[dz, :, cut], parts)
+
+        def finish(c, more):
+            for index, part, begin, width in self.pieces[c][2]:
+                cut = pl.ds(begin, width)
+                parts = [term.at[0, :, cut] for term in terms] + [m.at[:, cut] for m in more]
+                add_into(outs[index].at[pl.ds(part * PACK, PACK), :], parts)
+
+        for dz in (2, 3, 1, 0):
+            for index in range(n):
+                fetch(index, dz).start()
+        yield
+        for dz in (2, 3, 1, 0):
+            for index in range(n):
+                fetch(index, dz).wait()
+
+        @outside
+        def _():
+            for c in pieces:
+                for dz in (2, 3, 1):
+                    settle(c, dz, [])
+                    hand(dz, c).start()
+
+        def inwards(c):
+            @inside
+            def _():
+                hand(2, c).wait_recv()
+                settle(c, 3, [outer_box.at[2]])
+                hand(0, c).start()
+                hand(3, c).wait_recv()
+                settle(c, 2, [outer_box.at[3]])
+                hand(4, c).start()
+
+        def outwards(c):
+            @inside
+            def _():
+                hand(4, c).wait_recv()
+                settle(c, 1, [far_box.at[1]])
+                hand(5, c).start()
+                hand(0, c).wait_recv()
+                hand(1, c).wait_recv()
+                finish(c, [outer_box.at[1], far_box.at[0]])
+
+            @outside
+            def _():
+                hand(5, c).wait_recv()
+                finish(c, [inner_box])
+
+        for _ in range(1 + self.rest):
+            yield
+        for c in pieces:
+            inwards(c)
+            yield
+            if c:
+                outwards(c - 1)
+                yield
+        yield "last"
+        outwards(len(self.pieces) - 1)
+        for c in pieces:
+
+            @outside
+            def _():
+                for kind in (1, 2, 3):
+                    hand(kind, c).wait_send()
+
+            @inside
+            def _():
+                for kind in (0, 4, 5):
+                    hand(kind, c).wait_send()
 
 
 class Scatter:
@@ -893,7 +1117,6 @@
         self.turn = turn
         shape = blocks.shape
         self.pair = isinstance(blocks, PairBlocks)
-        self.tile = 256 if shape[1] % 256 == 0 else 128
         out = (shape[0] // 2, 2 * shape[1]) if self.pair else shape
         self.outs = [jax.ShapeDtypeStruct(out, F32)]
         self.out_specs = [VMEM]
@@ -957,7 +1180,7 @@
             fetch(slot).wait()
             across(slot).wait_recv()
             parts = [own.at[slot], near.at[slot]] + more
-            add_into(own.at[slot] if dst is None else dst, parts, self.tile)
+            add_into(own.at[slot] if dst is None else dst, parts)
 
         for da in (1, 0):
             for dz in (3, 2, 1, 0):
@@ -974,7 +1197,7 @@
             first(dz).wait_recv()
             settle((0, 0, dz), [from_b.at[dz], from_a.at[dz]])
             along_z(dz).start()
-        yield
+        yield "last"
         second(0, 0).wait_recv()
         first(0).wait_recv()
         for dz in (1, 2, 3):
@@ -992,7 +1215,6 @@
             )
             swap.start()
             out[:, columns] = total[span(core, half), :]
-        yield "last"
         if self.pair:
             swap.wait()
         for slot in range(16):
@@ -1016,7 +1238,7 @@
     yield from part.run(*refs)
 
 
-def exchange(name, collective, parts, vmem=4):
+def exchange(name, collective, parts):
     sizes = [(len(p.arrays), len(p.outs), len(p.scratch)) for p in parts]
     n_in = sum(size[0] for size in sizes)
     n_out = sum(size[1] for size in sizes)
@@ -1055,7 +1277,7 @@
         out_specs=[o for p in parts for o in p.out_specs],
         scratch_shapes=[s for p in parts for s in p.scratch],
         compiler_params=pltpu.CompilerParams(
-            collective_id=collective, has_side_effects=True, vmem_limit_bytes=vmem * 2**20
+            collective_id=collective, has_side_effects=True, vmem_limit_bytes=ROOM
         ),
     )(*[a for p in parts for a in p.arrays])
     outs = list(outs)
@@ -1158,10 +1380,14 @@
     return pl.ds(pl.multiple_of(j * BLOCK, BLOCK), BLOCK)
 
 
+def turned(values):
+    return values.astype(F32).T.astype(BF)
+
+
 def transpose_blocks(src, dst):
     @pl.loop(0, src.shape[0] // BLOCK)
     def _(j):
-        dst[j] = src[block_rows(j), :].astype(F32).T.astype(BF)
+        dst[j] = turned(src[block_rows(j), :])
 
 
 def visible(bounds, low, high, j):
@@ -1281,7 +1507,7 @@
             jax.ShapeDtypeStruct((rows, PAIR), BF),
             jax.ShapeDtypeStruct((8, rows), F32),
         ),
-        compiler_params=pltpu.CompilerParams(vmem_limit_bytes=48 * 2**20),
+        compiler_params=pltpu.CompilerParams(vmem_limit_bytes=ROOM),
     )(ranges, *operands)
 
 
@@ -1368,7 +1594,7 @@
             ],
         ),
         out_shape=(whole, whole, whole),
-        compiler_params=pltpu.CompilerParams(vmem_limit_bytes=48 * 2**20),
+        compiler_params=pltpu.CompilerParams(vmem_limit_bytes=ROOM),
     )(ranges, *operands)
 
 
@@ -1449,64 +1675,179 @@
     return lax.dot_general(a, b, (((0,), (0,)), ((), ())), preferred_element_type=F32)
 
 
-def norm_rows(values, gain):
-    inverse = lax.rsqrt(jnp.mean(values * values, axis=-1, keepdims=True) + EPS)
-    return (values * inverse * gain).astype(BF), inverse
-
-
-def norm_rows_back(values, gain, inverse, grad):
-    grad_gain = jnp.sum(grad * values * inverse, axis=0)
+FEED = 256
+
+
+def inverse_rms(values):
+    return lax.rsqrt(jnp.mean(values * values, axis=-1, keepdims=True) + EPS)
+
+
+def norm_back(values, gain, grad):
+    inverse = inverse_rms(values)
     scaled = grad * gain
     mean = jnp.mean(scaled * values, axis=-1, keepdims=True)
-    return inverse * scaled - values * inverse**3 * mean, grad_gain
-
-
-def layer(stream, qkv_w, gains, steps, memory, bounds, ranges):
+    grad_gain = jnp.sum(grad * values * inverse, axis=0, keepdims=True)
+    return inverse * scaled - values * (inverse * inverse * inverse) * mean, grad_gain
+
+
+def feed_kernel(att, stream, out_w, gain, gate_w, up_w, down_w, result, mixed, normed, gate, up):
+    step = pl.program_id(0)
+
+    @pl.when(step == 0)
+    def _():
+        both = stream[...] + dot_nn(att[...], out_w[...])
+        mixed[...] = both
+        normed[...] = (both * inverse_rms(both) * gain[...]).astype(BF)
+        result[...] = both
+
+    gated = dot_nn(normed[...], gate_w[...])
+    raised = dot_nn(normed[...], up_w[...])
+    gate[...] = gated
+    up[...] = raised
+    activated = (gated * jax.nn.sigmoid(gated) * raised).astype(BF)
+    result[...] += dot_nn(activated, down_w[...])
+
+
+def feed(attended, stream, out_w, gain, gate_up_w, down_w):
+    rows, width = stream.shape
+    ff = down_w.shape[0]
+    steps = ff // FEED
+    part = pl.BlockSpec((rows, FEED), lambda f: (0, f))
+    whole = jax.ShapeDtypeStruct((rows, width), F32)
+    wide = jax.ShapeDtypeStruct((rows, ff), F32)
+    return pl.pallas_call(
+        feed_kernel,
+        name="feed",
+        grid=(steps,),
+        in_specs=[
+            VMEM, VMEM, VMEM, VMEM,
+            pl.BlockSpec((width, FEED), lambda f: (0, f)),
+            pl.BlockSpec((width, FEED), lambda f: (0, steps + f)),
+            pl.BlockSpec((FEED, width), lambda f: (f, 0)),
+        ],
+        out_specs=(VMEM, VMEM, VMEM, part, part),
+        out_shape=(whole, whole, jax.ShapeDtypeStruct((rows, width), BF), wide, wide),
+        compiler_params=pltpu.CompilerParams(vmem_limit_bytes=ROOM),
+    )(attended, stream, out_w, gain, gate_up_w, gate_up_w, down_w)
+
+
+def feed_back_kernel(
+    grad_new, gate, up, normed, mixed, gain, att, out_w, gate_w, up_w, down_w,
+    gate_g, up_g, down_g, grad_mixed, grad_att, out_g, gain_g, branch, normed_t, total,
+):
+    step = pl.program_id(0)
+
+    @pl.when(step == 0)
+    def _():
+        branch[...] = grad_new[...].astype(BF)
+        normed_t[...] = turned(normed[...])
+        total[...] = jnp.zeros_like(total)
+
+    gated, raised = gate[...], up[...]
+    sig = jax.nn.sigmoid(gated)
+    swish = gated * sig
+    grad_act = dot_nt(branch[...], down_w[...])
+    down_g[...] = dot_tn((swish * raised).astype(BF), branch[...]).astype(BF)
+    grad_gate = (grad_act * raised * sig * (1.0 + gated * (1.0 - sig))).astype(BF)
+    grad_up = (grad_act * swish).astype(BF)
+    gate_g[...] = dot_nn(normed_t[...], grad_gate).astype(BF)
+    up_g[...] = dot_nn(normed_t[...], grad_up).astype(BF)
+    total[...] += dot_nt(grad_gate, gate_w[...]) + dot_nt(grad_up, up_w[...])
+
+    @pl.when(step == pl.num_programs(0) - 1)
+    def _():
+        back, grad_gain = norm_back(mixed[...], gain[...], total[...])
+        both = grad_new[...] + back
+        grad_mixed[...] = both
+        gain_g[...] = grad_gain
+        low = both.astype(BF)
+        grad_att[...] = dot_nt(low, out_w[...]).astype(BF)
+        out_g[...] = dot_tn(att[...], low).astype(BF)
+
+
+def feed_back(grad_new, weights, kept):
+    gain_a, qkv_w, out_w, gain, gate_up_w, down_w = weights
+    attended, mixed, normed, gate, up = kept[7:]
+    rows, width = grad_new.shape
+    ff = down_w.shape[0]
+    steps = ff // FEED
+    part = pl.BlockSpec((rows, FEED), lambda f: (0, f))
+    columns_of = pl.BlockSpec((width, FEED), lambda f: (0, f))
+    rows_of = pl.BlockSpec((FEED, width), lambda f: (f, 0))
+
+    def shape(a, b, kind=BF):
+        return jax.ShapeDtypeStruct((a, b), kind)
+
+    return pl.pallas_call(
+        feed_back_kernel,
+        name="feed_back",
+        grid=(steps,),
+        in_specs=[
+            VMEM, part, part, VMEM, VMEM, VMEM, VMEM, VMEM,
+            columns_of, pl.BlockSpec((width, FEED), lambda f: (0, steps + f)), rows_of,
+        ],
+        out_specs=(columns_of, columns_of, rows_of, VMEM, VMEM, VMEM, VMEM),
+        out_shape=(
+            shape(width, ff), shape(width, ff), shape(ff, width),
+            shape(rows, width, F32), shape(rows, width), shape(width, width), shape(1, width, F32),
+        ),
+        scratch_shapes=[
+            pltpu.VMEM((rows, width), BF), pltpu.VMEM((width, rows), BF), pltpu.VMEM((rows, width), F32),
+        ],
+        compiler_params=pltpu.CompilerParams(vmem_limit_bytes=ROOM),
+    )(grad_new, gate, up, normed, mixed, gain, attended, out_w, gate_up_w, gate_up_w, down_w)
+
+
+def project_kernel(grad_mixed, stream, gain, normed, grad_qkv, qkv_w, qkv_g, grad_stream, gain_g, normed_t, total):
+    step = pl.program_id(0)
+
+    @pl.when(step == 0)
+    def _():
+        normed_t[...] = turned(normed[...])
+        total[...] = jnp.zeros_like(total)
+
+    qkv_g[...] = dot_nn(normed_t[...], grad_qkv[...]).astype(BF)
+    total[...] += dot_nt(grad_qkv[...], qkv_w[...])
+
+    @pl.when(step == pl.num_programs(0) - 1)
+    def _():
+        back, grad_gain = norm_back(stream[...], gain[...], total[...])
+        grad_stream[...] = grad_mixed[...] + back
+        gain_g[...] = grad_gain
+
+
+def projections_back(grad_mixed, grad_qkv, weights, kept):
+    gain, qkv_w = weights[:2]
+    stream, normed = kept[:2]
+    rows, width = stream.shape
+    size = 512
+    part = pl.BlockSpec((width, size), lambda f: (0, f))
+    grad_qkv_w, grad_stream, grad_gain = pl.pallas_call(
+        project_kernel,
+        name="projections_back",
+        grid=(grad_qkv.shape[1] // size,),
+        in_specs=[VMEM, VMEM, VMEM, VMEM, pl.BlockSpec((rows, size), lambda f: (0, f)), part],
+        out_specs=(part, VMEM, VMEM),
+        out_shape=(
+            jax.ShapeDtypeStruct(qkv_w.shape, BF),
+            jax.ShapeDtypeStruct((rows, width), F32),
+            jax.ShapeDtypeStruct((1, width), F32),
+        ),
+        scratch_shapes=[pltpu.VMEM((width, rows), BF), pltpu.VMEM((rows, width), F32)],
+        compiler_params=pltpu.CompilerParams(vmem_limit_bytes=ROOM),
+    )(grad_mixed, stream, gain, normed, grad_qkv, qkv_w)
+    return grad_stream, grad_gain, grad_qkv_w
+
+
+def layer(stream, normed, heads, qkv_w, gains, to_rows, memory, bounds, ranges):
     gain_a, gain_b = gains
-    normed, inverse_a = norm_rows(stream, gain_a)
-    qkv = jnp.dot(normed, qkv_w, preferred_element_type=F32).astype(BF)
-    q, k, v = steps[0](qkv)
-    out, stat = attend(q, k, v, memory() if memory else None, bounds, ranges)
-    attended, out_w, gate_up_w, down_w = steps[1](out)
-    ff = down_w.shape[0]
-    mixed = stream + jnp.dot(attended, out_w, preferred_element_type=F32)
-    normed_ff, inverse_b = norm_rows(mixed, gain_b)
-    gate_up = jnp.dot(normed_ff, gate_up_w, preferred_element_type=F32)
-    gate, up = gate_up[:, :ff], gate_up[:, ff:]
-    activated = (gate * jax.nn.sigmoid(gate) * up).astype(BF)
-    result = mixed + jnp.dot(activated, down_w, preferred_element_type=F32)
+    q, k, v = heads
+    out, stat = attend(q, k, v, memory, bounds, ranges)
+    attended, out_w, gate_up_w, down_w = to_rows(out)
+    result, mixed, normed_ff, gate, up = feed(attended, stream, out_w, gain_b, gate_up_w, down_w)
     weights = (gain_a, qkv_w, out_w, gain_b, gate_up_w, down_w)
-    kept = (stream, inverse_a, normed, q, k, v, out, stat, attended, mixed, inverse_b, normed_ff, gate, up, activated)
+    kept = (stream, normed, q, k, v, out, stat, attended, mixed, normed_ff, gate, up)
     return result, weights, kept
-
-
-def ffn_back(grad_new, weights, kept):
-    gain_a, qkv_w, out_w, gain_b, gate_up_w, down_w = weights
-    attended, mixed, inverse_b, normed_ff, gate, up, activated = kept[8:]
-    branch = grad_new.astype(BF)
-    grad_down = dot_tn(activated, branch).astype(BF)
-    grad_act = dot_nt(branch, down_w)
-    sig = jax.nn.sigmoid(gate)
-    grad_gate = (grad_act * up * sig * (1.0 + gate * (1.0 - sig))).astype(BF)
-    grad_up = (grad_act * gate * sig).astype(BF)
-    grad_gate_up = jnp.concatenate((grad_gate, grad_up), axis=1)
-    grad_gate_up_w = dot_tn(normed_ff, grad_gate_up).astype(BF)
-    grad_normed_ff = dot_nt(grad_gate_up, gate_up_w)
-    back, grad_gain_b = norm_rows_back(mixed, gain_b, inverse_b, grad_normed_ff)
-    grad_mixed = grad_new + back
-    attn = grad_mixed.astype(BF)
-    grad_out_w = dot_tn(attended, attn).astype(BF)
-    grad_attended = dot_nt(attn, out_w).astype(BF)
-    return grad_mixed, grad_attended, grad_out_w, grad_gain_b, grad_gate_up_w, grad_down
-
-
-def projections_back(grad_mixed, grad_qkv, weights, kept):
-    gain_a, qkv_w = weights[:2]
-    stream, inverse_a, normed = kept[:3]
-    grad_qkv_w = dot_tn(normed, grad_qkv).astype(BF)
-    grad_normed = dot_nt(grad_qkv, qkv_w)
-    back, grad_gain_a = norm_rows_back(stream, gain_a, inverse_a, grad_normed)
-    return grad_mixed + back, grad_gain_a, grad_qkv_w
 
 
 def gain_columns(gains):
@@ -1547,46 +1888,30 @@
     def gather(matrix):
         return Gather(matrix, own(matrix))
 
-    (rows,), (docs,), (other,), (qkv1_w,), (gains,) = exchange(
-        "bring_tokens", 1,
-        [later(Rows(tokens)), Docs(docs), Sibling(downs), gather(qkv1), gather(gains)],
-    )
+    other = hop(downs, "core")
     down1 = pair_rows(down_weight1, other[:each], core)
     down2 = pair_rows(down_weight2, other[each:], core)
+    rest2 = jnp.concatenate((gate_up2, out_weight2), axis=1)
+    front, (docs,), (mk,), (mv,), (gu1_w,), (down1_w,), (out1_w,), (qkv2_w,) = exchange(
+        "front", 1,
+        [Front(tokens, qkv1, own(qkv1), gains, own(gains), 3), Docs(docs),
+         later(Memory(memory_keys), 1), later(Memory(memory_values), 7),
+         later(gather(gate_up1), 2), later(Gather(down1, pairs), 2),
+         later(gather(out_weight1), 2), later(gather(qkv2), 2)],
+    )
+    qkv1_w, gains, rows, normed1, *heads1 = front
     own_docs = lax.dynamic_index_in_dim(docs, seg, 0, keepdims=False)
     own_mem_docs = lax.dynamic_index_in_dim(docs, seg + 2, 0, keepdims=False)
     reset = lax.dynamic_index_in_dim(memory_resets, seg, 0, keepdims=False)
     bounds, ranges = mask_ranges(own_docs, own_mem_docs, reset)
-    gains = gains[:, :4].astype(F32)
-    held = {}
-
+    gains = [gains[:, i].astype(F32)[None] for i in range(4)]
     hops = {}
-    rest2 = jnp.concatenate((gate_up2, out_weight2), axis=1)
-
-    def heads1(qkv):
-        swapped, (mk,), (mv,), (held["gu1"],), (held["down1"],), (held["out1"],), (held["qkv2"],) = exchange(
-            "to_heads_1", 2,
-            [later(Swap([qkv], True)), later(Memory(memory_keys), 3), later(Memory(memory_values), 3),
-             gather(gate_up1), Gather(down1, pairs), gather(out_weight1), gather(qkv2)],
-        )
-        held["memory"] = mk, mv
-        swapped, shards = join(swapped, (rest2, down2))
-        hops["rest"] = [gather_column(shard) for shard in shards]
-        return swapped
+    heads1, shards = join(heads1, (rest2, down2))
+    hops["rest"] = [gather_column(shard) for shard in shards]
 
     def rows1(out):
         ((attended,),) = exchange("to_rows_1", 3, [Swap([out], False)])
-        return attended, held["out1"], held["gu1"], held["down1"]
-
-    def heads2(qkv):
-        held["memory"] = sort_memory(held["memory"], own_mem_docs)
-        (swapped,) = exchange("to_heads_2", 4, [Swap([qkv], True)])
-        swapped, firsts = join(swapped, [group[1] for group in hops["rest"]])
-        hops["rest"] = [
-            (group[0], first, group[2], hop(first, "b"))
-            for group, first in zip(hops["rest"], firsts)
-        ]
-        return swapped
+        return attended, out1_w, gu1_w, down1_w
 
     def rows2(out):
         out, (rest, down) = join(out, hops["rest"])
@@ -1600,14 +1925,20 @@
         return attended, out_w, gate_up_w, down_w
 
     middle, weights1, kept1 = layer(
-        rows.astype(F32), qkv1_w, (gains[:, 0], gains[:, 1]), (heads1, rows1), None, bounds, ranges
+        rows.astype(F32), normed1, heads1, qkv1_w, (gains[0], gains[1]), rows1, None, bounds, ranges
     )
     middle, rest = join(middle, hops["rest"])
     hops["rest"] = [(column, hop(column, "a"), hop(column, "b")) for column in rest]
-    qkv2_w = held["qkv2"]
+    normed2 = (middle * inverse_rms(middle) * gains[2]).astype(BF)
+    qkv = jnp.dot(normed2, qkv2_w, preferred_element_type=F32).astype(BF)
+    (heads2,) = exchange("to_heads_2", 4, [Swap([qkv], True)])
+    heads2, firsts = join(heads2, [group[1] for group in hops["rest"]])
+    hops["rest"] = [
+        (group[0], first, group[2], hop(first, "b")) for group, first in zip(hops["rest"], firsts)
+    ]
+    memory = sort_memory((mk, mv), own_mem_docs)
     result, weights2, kept2 = layer(
-        middle, qkv2_w, (gains[:, 2], gains[:, 3]), (heads2, rows2),
-        lambda: held["memory"], bounds, ranges,
+        middle, normed2, heads2, qkv2_w, (gains[2], gains[3]), rows2, memory, bounds, ranges
     )
     cot = hops["cot"]
     output = chunk_hops(result.astype(BF))
@@ -1619,66 +1950,59 @@
             core == 0, jnp.concatenate((half, other), 1), jnp.concatenate((other, half), 1)
         )
 
-    shapes = ((count, 2 * ff), (count, width), pairs.shape)
-
-    def feed_sums(out_g, gate_up_g, down_g):
-        return CoreSums((gate_up_g, own(gate_up_g)), (out_g, own(out_g)), (down_g, pairs))
-
-    grad_mixed, grad_att, out_g2, gain_b2, gate_up_g2, down_g2 = ffn_back(
+    shapes = ((count, ff), (count, ff), (count, width), pairs.shape)
+
+    def feed_sums(gate_g, up_g, down_g, out_g):
+        return CoreSums((gate_g, own(gate_g)), (up_g, own(up_g)), (out_g, own(out_g)), (down_g, pairs))
+
+    gate_g2, up_g2, down_g2, grad_mixed, grad_att, out_g2, gain_b2 = feed_back(
         cot.astype(F32), weights2, kept2
     )
     (grad_out,), sums2 = exchange(
         "back_to_heads_2", 6,
-        [Swap([grad_att], True), feed_sums(out_g2, gate_up_g2, down_g2)],
-        48,
+        [Swap([grad_att], True), feed_sums(gate_g2, up_g2, down_g2, out_g2)],
     )
     sums2 = scatter_second(sums2)
-    q, k, v, out, stat = kept2[3:8]
-    grads = attend_back(q, k, v, held["memory"], bounds, ranges, out, stat, grad_out)
+    q, k, v, out, stat = kept2[2:7]
+    grads = attend_back(q, k, v, memory, bounds, ranges, out, stat, grad_out)
     ((grad_qkv,),) = exchange("back_to_rows_2", 7, [Swap(list(grads), False)])
     grad_qkv, (sums2, output) = join(grad_qkv, (sums2, output))
     sums2 = scatter_first(sums2)
     grad_middle, gain_a2, qkv_g2 = projections_back(grad_mixed, grad_qkv, weights2, kept2)
-    (qkv_s2,) = exchange("projection_sums_2", 12, [CoreSums((qkv_g2, own(qkv_g2)))], 24)
+    (qkv_s2,) = exchange("projection_sums_2", 12, [CoreSums((qkv_g2, own(qkv_g2)))])
     grad_middle, (sums2, qkv_s2) = join(grad_middle, (sums2, qkv_s2))
     sums2 = scatter_z(sums2)
     qkv_s2 = scatter_second(qkv_s2)
 
-    grad_mixed, grad_att, out_g1, gain_b1, gate_up_g1, down_g1 = ffn_back(
+    gate_g1, up_g1, down_g1, grad_mixed, grad_att, out_g1, gain_b1 = feed_back(
         grad_middle, weights1, kept1
     )
     grad_att, qkv_s2 = join(grad_att, qkv_s2)
     qkv_s2 = scatter_first(qkv_s2)
     (grad_out,), sums1 = exchange(
         "back_to_heads_1", 8,
-        [Swap([grad_att], True), feed_sums(out_g1, gate_up_g1, down_g1)],
-        48,
+        [Swap([grad_att], True), feed_sums(gate_g1, up_g1, down_g1, out_g1)],
     )
     grad_out, (sums2, qkv_s2) = join(grad_out, (sums2, qkv_s2))
     qkv_s2 = scatter_z(qkv_s2)
     sums1 = scatter_second(sums1)
-    q, k, v, out, stat = kept1[3:8]
+    q, k, v, out, stat = kept1[2:7]
     grads = attend_back(q, k, v, None, bounds, ranges, out, stat, grad_out)
     ((grad_qkv,),) = exchange("back_to_rows_1", 9, [Swap(list(grads), False)])
     grad_qkv, (sums1, qkv_s2) = join(grad_qkv, (sums1, qkv_s2))
     sums1 = scatter_first(sums1)
     grad_rows, gain_a1, qkv_g1 = projections_back(grad_mixed, grad_qkv, weights1, kept1)
-    gain_grads = gain_columns((gain_a1, gain_b1, gain_a2, gain_b2)).astype(BF)
-    grad_rows, sums1 = join(grad_rows, sums1)
-    sums1 = scatter_z(sums1)
-    (grad_tokens,), (q_s1,), (k_s1,), (v_s1,), (gain_s,) = exchange(
+    gain_grads = gain_columns([g[0] for g in (gain_a1, gain_b1, gain_a2, gain_b2)]).astype(BF)
+    here, second, first = sums1
+    (grad_tokens,), (gate_s1, up_s1, out_s1, down_s1), (q_s1,), (k_s1,), (v_s1,), (gain_s,) = exchange(
         "back_to_owners", 10,
-        [Chunks(grad_rows.astype(BF))]
+        [Chunks(grad_rows.astype(BF)), LineSums((here, second, first), shapes, ((0,), (1,), (2, 3)))]
         + [Scatter(qkv_g1, ColumnBlocks(count, width, i), i) for i in range(3)]
-        + [Scatter(gain_grads, own(gain_grads), 2)],
-        40,
-    )
-    gate_up_s2, out_s2, down_s2 = unpack(scatter_end(sums2), shapes)
-    gate_up_s1, out_s1, down_s1 = unpack(scatter_end(sums1), shapes)
+        + [Scatter(gain_grads, own(gain_grads))],
+    )
+    gate_s2, up_s2, out_s2, down_s2 = unpack(scatter_end(sums2), shapes)
     (qkv_s2,) = unpack(scatter_end(qkv_s2), ((count, 3 * width),))
     q_s2, k_s2, v_s2 = columns(qkv_s2, (width,) * 3)
-    gate_s1, up_s1 = columns(gate_up_s1, (ff, ff))
-    gate_s2, up_s2 = columns(gate_up_s2, (ff, ff))
     return (
         output, grad_tokens.astype(F32),
         gain_s[:, 0], q_s1, k_s1, v_s1, out_s1, gain_s[:, 1], gate_s1, up_s1, pair_sum(down_s1),

time: 916 us -> 841 us (0.918)
  matrix products: 161 us -> 17.7 us
  Pallas kernels: 574 us -> 692 us
  local copies, waits for them, and re-layouts: 57.4 us -> 19.9 us
    dot_general x24 -> x1, matrix products: 151 us -> 7.91 us  [head_local(): qkv = jnp.dot(normed2, qkv2_w, preferred_element_type=F32).astype(BF)]
    pallas_call x0 -> x6, Pallas kernels: none -> 139 us  [the longest x2 68.5 us: feed_back(): pl.pallas_call(feed_back_kernel, name='feed_back', grid=(steps,), in_spec...]
    unnamed x211 -> x108, local copies, waits for them, and re-layouts: 31.9 us -> 8.51 us
    pallas_call x11 -> x10, Pallas kernels: 479 us -> 469 us  [exchange(): pl.pallas_call(kernel, name=name, out_shape=[o for p in parts for o in p....]
    ppermute x29 -> x27, waiting for transfers between devices: 19.9 us -> 14.2 us  [hop(): return lax.ppermute(values, ('grp', 'key'), pairs)]
    ppermute x29 -> x27, starting transfers between devices: 36.8 us -> 40.8 us  [hop(): return lax.ppermute(values, ('grp', 'key'), pairs)]
  transfers between devices with their start and end apart: 33 -> 31, of which waited for: 4 -> 3; matrix products, arithmetic and copies ran while one was open for 17% -> 7% of each run, Pallas kernels for 39% -> 45%
where the time goes in v3:
time: 841 us; the launch traced here: 839 us
  Pallas kernels  692 us (82%)
  starting transfers between devices  49.2 us (6%)
  other arithmetic  43.3 us (5%)
  local copies, waits for them, and re-layouts  19.9 us (2%)
  matrix products  17.7 us (2%)
  waiting for transfers between devices  14.2 us (2%)
    pallas_call x10, Pallas kernels, exchange(): pl.pallas_call(kernel, name=name, out_shape=[o for p in parts for o in p....  469 us
    pallas_call x2, Pallas kernels, feed_back(): pl.pallas_call(feed_back_kernel, name='feed_back', grid=(steps,), in_spec...  68.5 us
    pallas_call x2, Pallas kernels, attend_back(): pl.pallas_call(functools.partial(attend_back_kernel, memory is not None),...  51.7 us
    ppermute x27, starting transfers between devices, hop(): return lax.ppermute(values, ('grp', 'key'), pairs)  40.8 us
    pallas_call x2, Pallas kernels, feed(): pl.pallas_call(feed_kernel, name='feed', grid=(steps,), in_specs=[VMEM, V...  40.3 us
    pallas_call x2, Pallas kernels, attend(): pl.pallas_call(functools.partial(attend_kernel, memory is not None), name...  31.8 us
    pallas_call x2, Pallas kernels, projections_back(): pl.pallas_call(project_kernel, name='projections_back', grid=(grad_qkv.sh...  30.4 us
  transfers between devices with their start and end apart: 31, of which 3 were waited for; matrix products, arithmetic and copies ran while one was open for 7% of the time, Pallas kernels for 45%

profile of v3, /device:TPU:1, one launch (start us, length us, event | category | flops | bytes accessed | tf_op | source)
XLA Modules:
  0.0 838.9 jit_solution(10788731895658486591)
XLA Ops:
  10.2 164.4 %front.1 = (bf16[1024,3072]{1,0:T(8,128)(2,1)}, bf16[1024,128]{1,0:T(8,128)(2,1)}, bf16[512,1024]{1,0:T(8,128)(2,1)}, bf16[512,1024]{1,0:T(8,128)(2,1)}, bf16[20...) custom-call(bf16[32,3072]{1,0:T(8,128)(2,1)} %get-tuple-element.360., ...), custom_call_target="tpu_custom_call" | custom-call | tf_op jit(solution)/shard_map/front/pallas_call | solution.py:1272
  174.6 3.7 collective-permute-start.4
  190.7 15.2 %attend.2 = (bf16[2048,256]{1,0:T(8,128)(2,1)}, f32[8,2048]{1,0:T(8,128)}) custom-call(s32[4,8]{1,0:T(4,128)} %stack.120.ranges, bf16[2048,256]{1,0:T(8,128)(2,1)} %get-tuple-element.161.refs_0_, bf16[2048,256]{1,0:T(8,128)(2,1)} %get-tuple-element.162.refs_1_.refs_5_, bf16[2048,256]{1,0:T(8,128)(2,1)} %get-tuple-element.163.refs_2_.refs_6_, ...), custom_call_target="tpu_custom_call" | custom-call | tf_op jit(solution)/shard_map/attend/pallas_call | solution.py:1490
  206.0 27.4 %to_rows_1.1.att = bf16[512,1024]{1,0:T(8,128)(2,1)} custom-call(bf16[2048,256]{1,0:T(8,128)(2,1)} %get-tuple-element.164.refs_0_.refs_2_), custom_call_target="tpu_custom_call" | custom-call | tf_op jit(solution)/shard_map/to_rows_1/pallas_call | solution.py:1272
  236.2 19.9 %feed.2 = (f32[512,1024]{1,0:T(8,128)}, f32[512,1024]{1,0:T(8,128)}, bf16[512,1024]{1,0:T(8,128)(2,1)}, f32[512,2816]{1,0:T(8,128)}, f32[512,2816]{1,0:T(8,128)}) custom-call(bf16[512,1024]{1,0:T(8,128)(2,1)} %to_rows_1.1.att, f32[512,1024]{1,0:T(8,128)} %convert_element_type.178.stream, bf16[1024,1024]{1,0:T(8,128)(2,1)} %get-tuple-element.166.out_w, ...), custom_call_target="tpu_custom_call" | custom-call | tf_op jit(solution)/shard_map/feed/pallas_call | solution.py:1718
  258.7 5.2 collective-permute-start.7
  264.5 7.9 convolution_convert_fusion.refs_0_
  272.5 43.5 %to_heads_2.1 = (bf16[2048,256]{1,0:T(8,128)(2,1)}, bf16[2048,256]{1,0:T(8,128)(2,1)}, bf16[2048,256]{1,0:T(8,128)(2,1)}) custom-call(bf16[512,3072]{1,0:T(8,128)(2,1)} %convolution_convert_fusion.refs_0_), custom_call_target="tpu_custom_call" | custom-call | tf_op jit(solution)/shard_map/to_heads_2/pallas_call | solution.py:1272
  317.6 5.5 fusion.5.refs_5_.refs_8_
  323.0 4.2 fusion.4.refs_4_.refs_7_
  327.2 16.6 %attend.3 = (bf16[2048,256]{1,0:T(8,128)(2,1)}, f32[8,2048]{1,0:T(8,128)}) custom-call(s32[4,8]{1,0:T(4,128)} %stack.120.ranges, bf16[2048,256]{1,0:T(8,128)(2,1)} %get-tuple-element.180.refs_0_, bf16[2048,256]{1,0:T(8,128)(2,1)} %get-tuple-element.181.refs_1_.refs_5_, bf16[2048,256]{1,0:T(8,128)(2,1)} %get-tuple-element.182.refs_2_.refs_6_, ...), custom_call_target="tpu_custom_call" | custom-call | tf_op jit(solution)/shard_map/attend/pallas_call | solution.py:1490
  344.9 7.8 collective-permute-done.12.refs_8_
  352.8 20.0 %to_rows_2.1 = (bf16[512,1024]{1,0:T(8,128)(2,1)}, bf16[1024,5632]{1,0:T(8,128)(2,1)}, bf16[1024,1024]{1,0:T(8,128)(2,1)}, bf16[2816,1024]{1,0:T(8,128)(2,1)}) custom-call(bf16[2048,256]{1,0:T(8,128)(2,1)} %get-tuple-element.188.refs_0_.refs_2_, bf16[4,32,6656]{2,1,0:T(8,128)(2,1)} %copy-done.1, bf16[4,32,6656]{2,1,0:T(8,128)(2,1)} %collective-permute-done.7.refs_2_, ...), custom_call_target="tpu_custom_call" | custom-call | tf_op jit(solution)/shard_map/to_rows_2/pallas_call | solution.py:1272
  373.0 4.4 collective-permute-start.14
  377.5 20.4 %feed.3 = (f32[512,1024]{1,0:T(8,128)}, f32[512,1024]{1,0:T(8,128)}, bf16[512,1024]{1,0:T(8,128)(2,1)}, f32[512,2816]{1,0:T(8,128)}, f32[512,2816]{1,0:T(8,128)}) custom-call(bf16[512,1024]{1,0:T(8,128)(2,1)} %get-tuple-element.199.att, f32[512,1024]{1,0:T(8,128)} %get-tuple-element.173.stream, bf16[1024,1024]{1,0:T(8,128)(2,1)} %get-tuple-element.200.out_w, ...), custom_call_target="tpu_custom_call" | custom-call | tf_op jit(solution)/shard_map/feed/pallas_call | solution.py:1718
  399.5 34.2 %feed_back.2 = (bf16[1024,2816]{1,0:T(8,128)(2,1)}, bf16[1024,2816]{1,0:T(8,128)(2,1)}, bf16[2816,1024]{1,0:T(8,128)(2,1)}, f32[512,1024]{1,0:T(8,128)}, bf16[51...) custom-call(f32[512,1024]{1,0:T(8,128)} %maximum_convert_fusion.grad_new, ...), custom_call_target="tpu_custom_call" | custom-call | tf_op jit(solution)/shard_map/feed_back/pallas_call | solution.py:1781
  433.7 20.1 %back_to_heads_2.1 = (bf16[2048,256]{1,0:T(8,128)(2,1)}, bf16[4,16,18944]{2,1,0:T(8,128)(2,1)}, bf16[4,16,18944]{2,1,0:T(8,128)(2,1)}, bf16[8,16,18944]{2,1,0:T(8,128)(2,1)}) custom-call(bf16[512,1024]{1,0:T(8,128)(2,1)} %get-tuple-element.207.refs_0_, bf16[1024,2816]{1,0:T(8,128)(2,1)} %get-tuple-element.208.refs_1_, ...), custom_call_target="tpu_custom_call" | custom-call | tf_op jit(solution)/shard_map/back_to_heads_2/pallas_call | solution.py:1272
  459.4 26.3 %attend_back.2 = (bf16[2048,256]{1,0:T(8,128)(2,1)}, bf16[2048,256]{1,0:T(8,128)(2,1)}, bf16[2048,256]{1,0:T(8,128)(2,1)}) custom-call(s32[4,8]{1,0:T(4,128)} %stack.120.ranges, bf16[2048,256]{1,0:T(8,128)(2,1)} %get-tuple-element.180.refs_0_, bf16[2048,256]{1,0:T(8,128)(2,1)} %get-tuple-element.212.refs_1_, ...), custom_call_target="tpu_custom_call" | custom-call | tf_op jit(solution)/shard_map/attend_back/pallas_call | solution.py:1580
  485.7 41.7 %back_to_rows_2.1.grad_qkv = bf16[512,3072]{1,0:T(8,128)(2,1)} custom-call(bf16[2048,256]{1,0:T(8,128)(2,1)} %get-tuple-element.214.refs_0_, bf16[2048,256]{1,0:T(8,128)(2,1)} %get-tuple-element.215.refs_1_, bf16[2048,256]{1,0:T(8,128)(2,1)} %get-tuple-element.216.refs_2_), custom_call_target="tpu_custom_call" | custom-call | tf_op jit(solution)/shard_map/back_to_rows_2/pallas_call | solution.py:1272
  529.4 3.7 add_convert_fusion.1
  535.8 15.4 %projections_back.2 = (bf16[1024,3072]{1,0:T(8,128)(2,1)}, f32[512,1024]{1,0:T(8,128)}, f32[1,1024]{1,0:T(1,128)}) custom-call(f32[512,1024]{1,0:T(8,128)} %get-tuple-element.222.grad_mixed, f32[512,1024]{1,0:T(8,128)} %get-tuple-element.173.stream, f32[1,1024]{1,0:T(1,128)} %bitcast.112, bf16[512,1024]{1,0:T(8,128)(2,1)} %copy-done.3, ...), custom_call_target="tpu_custom_call" | custom-call | tf_op jit(solution)/shard_map/projections_back/pallas_call | solution.py:1825
  551.2 14.2 %projection_sums_2.1 = (bf16[4,16,6144]{2,1,0:T(8,128)(2,1)}, bf16[4,16,6144]{2,1,0:T(8,128)(2,1)}, bf16[8,16,6144]{2,1,0:T(8,128)(2,1)}) custom-call(bf16[1024,3072]{1,0:T(8,128)(2,1)} %get-tuple-element.228.refs_0_), custom_call_target="tpu_custom_call" | custom-call | tf_op jit(solution)/shard_map/projection_sums_2/pallas_call | solution.py:1272
  565.4 4.2 collective-permute-start.19
  569.6 5.4 fusion.32
  579.8 34.3 %feed_back.3 = (bf16[1024,2816]{1,0:T(8,128)(2,1)}, bf16[1024,2816]{1,0:T(8,128)(2,1)}, bf16[2816,1024]{1,0:T(8,128)(2,1)}, f32[512,1024]{1,0:T(8,128)}, bf16[51...) custom-call(f32[512,1024]{1,0:T(8,128)} %get-tuple-element.232.grad_new, ...), custom_call_target="tpu_custom_call" | custom-call | tf_op jit(solution)/shard_map/feed_back/pallas_call | solution.py:1781
  618.4 21.9 %back_to_heads_1.1 = (bf16[2048,256]{1,0:T(8,128)(2,1)}, bf16[4,16,18944]{2,1,0:T(8,128)(2,1)}, bf16[4,16,18944]{2,1,0:T(8,128)(2,1)}, bf16[8,16,18944]{2,1,0:T(8,128)(2,1)}) custom-call(bf16[512,1024]{1,0:T(8,128)(2,1)} %get-tuple-element.243.refs_0_, bf16[1024,2816]{1,0:T(8,128)(2,1)} %get-tuple-element.244.refs_1_, ...), custom_call_target="tpu_custom_call" | custom-call | tf_op jit(solution)/shard_map/back_to_heads_1/pallas_call | solution.py:1272
  650.0 25.4 %attend_back.3 = (bf16[2048,256]{1,0:T(8,128)(2,1)}, bf16[2048,256]{1,0:T(8,128)(2,1)}, bf16[2048,256]{1,0:T(8,128)(2,1)}) custom-call(s32[4,8]{1,0:T(4,128)} %stack.120.ranges, bf16[2048,256]{1,0:T(8,128)(2,1)} %get-tuple-element.161.refs_0_, bf16[2048,256]{1,0:T(8,128)(2,1)} %get-tuple-element.255.refs_1_, ...), custom_call_target="tpu_custom_call" | custom-call | tf_op jit(solution)/shard_map/attend_back/pallas_call | solution.py:1580
  675.4 38.0 %back_to_rows_1.1.grad_qkv = bf16[512,3072]{1,0:T(8,128)(2,1)} custom-call(bf16[2048,256]{1,0:T(8,128)(2,1)} %get-tuple-element.257.refs_0_, bf16[2048,256]{1,0:T(8,128)(2,1)} %get-tuple-element.258.refs_1_, bf16[2048,256]{1,0:T(8,128)(2,1)} %get-tuple-element.259.refs_2_), custom_call_target="tpu_custom_call" | custom-call | tf_op jit(solution)/shard_map/back_to_rows_1/pallas_call | solution.py:1272
  714.2 3.7 add_convert_fusion
  721.6 15.0 %projections_back.3 = (bf16[1024,3072]{1,0:T(8,128)(2,1)}, f32[512,1024]{1,0:T(8,128)}, f32[1,1024]{1,0:T(1,128)}) custom-call(f32[512,1024]{1,0:T(8,128)} %get-tuple-element.237.grad_mixed, f32[512,1024]{1,0:T(8,128)} %convert_element_type.178.stream, f32[1,1024]{1,0:T(1,128)} %bitcast.113, bf16[512,1024]{1,0:T(8,128)(2,1)} %get-tuple-element.238.normed, ...), custom_call_target="tpu_custom_call" | custom-call | tf_op jit(solution)/shard_map/projections_back/pallas_call | solution.py:1825
  742.1 5.2 collective-permute-done.28.refs_3_
  748.8 78.1 %back_to_owners.1 = (bf16[2,256,1024]{2,1,0:T(8,128)(2,1)}, f32[32,2816]{1,0:T(8,128)}, f32[32,2816]{1,0:T(8,128)}, f32[32,1024]{1,0:T(8,128)}, f32[176,512]{1,0...) custom-call(bf16[512,1024]{1,0:T(8,128)(2,1)} %convert_element_type.211.refs_0_, ...), custom_call_target="tpu_custom_call" | custom-call | tf_op jit(solution)/shard_map/back_to_owners/pallas_call | solution.py:1272
  (262 shorter events, 83.4 us)
Async XLA Ops:
  2.0 7.3 collective-permute-start
  174.6 13.5 %collective-permute-start.4 = (bf16[176,512]{1,0:T(8,128)(2,1)S(1)}, bf16[176,512]{1,0:T(8,128)(2,1)S(1)}, u32[]{:S(2)}, u32[]{:S(2)}) collective-permute-start(bf16[176,512]{1,0:T(8,128)(2,1)S(1)} %constant_dynamic-slice_fusion.2), channel_id=1, source_target_pairs={{0,2},{1,3},{2,0},{3,1},{4,6},{5,7},{6,4},{7,5},{8,10},{9,11},{10,... | collective-permute-start | bytes 540680 | tf_op jit(solution)/shard_map/ppermute | solution.py:1302
  178.4 77.8 %collective-permute-start.5 = (bf16[176,512]{1,0:T(8,128)(2,1)S(1)}, bf16[176,512]{1,0:T(8,128)(2,1)S(1)}, u32[]{:S(2)}, u32[]{:S(2)}) collective-permute-start(bf16[176,512]{1,0:T(8,128)(2,1)S(1)} %constant_dynamic-slice_fusion.2), channel_id=1, source_target_pairs={{0,4},{1,5},{2,6},{3,7},{4,0},{5,1},{6,2},{7,3},{8,12},{9,13},{10,... | collective-permute-start | bytes 540680 | tf_op jit(solution)/shard_map/ppermute | solution.py:1302
  181.2 74.9 %collective-permute-start.6 = (bf16[176,512]{1,0:T(8,128)(2,1)S(1)}, bf16[176,512]{1,0:T(8,128)(2,1)S(1)}, u32[]{:S(2)}, u32[]{:S(2)}) collective-permute-start(bf16[176,512]{1,0:T(8,128)(2,1)S(1)} %constant_dynamic-slice_fusion.2), channel_id=1, source_target_pairs={{0,6},{1,7},{2,4},{3,5},{4,2},{5,3},{6,0},{7,1},{8,14},{9,15},{10,... | collective-permute-start | bytes 540680 | tf_op jit(solution)/shard_map/ppermute | solution.py:1302
  182.3 73.9 %collective-permute-start.1 = (bf16[32,6656]{1,0:T(8,128)(2,1)S(1)}, bf16[32,6656]{1,0:T(8,128)(2,1)S(1)}, u32[]{:S(2)}, u32[]{:S(2)}) collective-permute-start(bf16[32,6656]{1,0:T(8,128)(2,1)S(1)} %pad_maximum_fusion.3), channel_id=1, source_target_pairs={{0,2},{1,3},{2,0},{3,1},{4,6},{5,7},{6,4},{7,5},{8,10},{9,11},{10,... | collective-permute-start | bytes 1277960 | tf_op jit(solution)/shard_map/ppermute | solution.py:1302
  182.6 73.6 %collective-permute-start.2 = (bf16[32,6656]{1,0:T(8,128)(2,1)S(1)}, bf16[32,6656]{1,0:T(8,128)(2,1)S(1)}, u32[]{:S(2)}, u32[]{:S(2)}) collective-permute-start(bf16[32,6656]{1,0:T(8,128)(2,1)S(1)} %pad_maximum_fusion.3), channel_id=1, source_target_pairs={{0,4},{1,5},{2,6},{3,7},{4,0},{5,1},{6,2},{7,3},{8,12},{9,13},{10,... | collective-permute-start | bytes 1277960 | tf_op jit(solution)/shard_map/ppermute | solution.py:1302
  188.1 68.1 %collective-permute-start.3 = (bf16[32,6656]{1,0:T(8,128)(2,1)S(1)}, bf16[32,6656]{1,0:T(8,128)(2,1)S(1)}, u32[]{:S(2)}, u32[]{:S(2)}) collective-permute-start(bf16[32,6656]{1,0:T(8,128)(2,1)S(1)} %pad_maximum_fusion.3), channel_id=1, source_target_pairs={{0,6},{1,7},{2,4},{3,5},{4,2},{5,3},{6,0},{7,1},{8,14},{9,15},{10,... | collective-permute-start | bytes 1277960 | tf_op jit(solution)/shard_map/ppermute | solution.py:1302
  256.2 59.8 %copy-start.4 = (bf16[4,176,512]{2,1,0:T(8,128)(2,1)}, bf16[4,176,512]{2,1,0:T(8,128)(2,1)S(1)}, u32[]{:S(2)}) copy-start(bf16[4,176,512]{2,1,0:T(8,128)(2,1)S(1)} %pad_maximum_fusion.2.refs_5_) | copy-start | bytes 2162692
  258.7 57.3 %collective-permute-start.7 = (bf16[4,32,6656]{2,1,0:T(8,128)(2,1)S(1)}, bf16[4,32,6656]{2,1,0:T(8,128)(2,1)}, u32[]{:S(2)}, u32[]{:S(2)}) collective-permute-start(bf16[4,32,6656]{2,1,0:T(8,128)(2,1)S(1)} %pad_maximum_fusion.refs_1_), channel_id=1, source_target_pairs={{0,8},{1,17},{2,10},{3,19},{4,12},{5,21},{6,14},{7,23},{8,0},{9,25... | collective-permute-start | bytes 5111816 | tf_op jit(solution)/shard_map/ppermute | solution.py:1302
  263.9 81.1 %collective-permute-start.9 = (bf16[4,32,6656]{2,1,0:T(8,128)(2,1)S(1)}, bf16[4,32,6656]{2,1,0:T(8,128)(2,1)}, u32[]{:S(2)}, u32[]{:S(2)}) collective-permute-start(bf16[4,32,6656]{2,1,0:T(8,128)(2,1)S(1)} %pad_maximum_fusion.refs_1_), channel_id=1, source_target_pairs={{0,16},{1,9},{2,18},{3,11},{4,20},{5,13},{6,22},{7,15},{8,24},{9,1... | collective-permute-start | bytes 5111816 | tf_op jit(solution)/shard_map/ppermute | solution.py:1302
  263.9 52.1 %collective-permute-start.8 = (bf16[4,176,512]{2,1,0:T(8,128)(2,1)S(1)}, bf16[4,176,512]{2,1,0:T(8,128)(2,1)}, u32[]{:S(2)}, u32[]{:S(2)}) collective-permute-start(bf16[4,176,512]{2,1,0:T(8,128)(2,1)S(1)} %pad_maximum_fusion.2.refs_5_), channel_id=1, source_target_pairs={{0,8},{1,17},{2,10},{3,19},{4,12},{5,21},{6,14},{7,23},{8,0},{9,25... | collective-permute-start | bytes 2162696 | tf_op jit(solution)/shard_map/ppermute | solution.py:1302
  316.0 36.8 %collective-permute-start.10 = (bf16[4,32,6656]{2,1,0:T(8,128)(2,1)}, bf16[4,32,6656]{2,1,0:T(8,128)(2,1)}, u32[]{:S(2)}, u32[]{:S(2)}) collective-permute-start(bf16[4,32,6656]{2,1,0:T(8,128)(2,1)} %collective-permute-done.7.refs_2_), channel_id=1, source_target_pairs={{0,16},{1,9},{2,18},{3,11},{4,20},{5,13},{6,22},{7,15},{8,24},{9,1... | collective-permute-start | bytes 5111816 | tf_op jit(solution)/shard_map/ppermute | solution.py:1302
  316.0 28.9 %collective-permute-start.11 = (bf16[4,176,512]{2,1,0:T(8,128)(2,1)S(1)}, bf16[4,176,512]{2,1,0:T(8,128)(2,1)S(1)}, u32[]{:S(2)}, u32[]{:S(2)}) collective-permute-start(bf16[4,176,512]{2,1,0:T(8,128)(2,1)S(1)} %pad_maximum_fusion.2.refs_5_), channel_id=1, source_target_pairs={{0,16},{1,9},{2,18},{3,11},{4,20},{5,13},{6,22},{7,15},{8,24},{9,1... | collective-permute-start | bytes 2162696 | tf_op jit(solution)/shard_map/ppermute | solution.py:1302
  317.5 35.3 %collective-permute-start.12 = (bf16[4,176,512]{2,1,0:T(8,128)(2,1)}, bf16[4,176,512]{2,1,0:T(8,128)(2,1)}, u32[]{:S(2)}, u32[]{:S(2)}) collective-permute-start(bf16[4,176,512]{2,1,0:T(8,128)(2,1)} %collective-permute-done.8.refs_6_), channel_id=1, source_target_pairs={{0,16},{1,9},{2,18},{3,11},{4,20},{5,13},{6,22},{7,15},{8,24},{9,1... | collective-permute-start | bytes 2162696 | tf_op jit(solution)/shard_map/ppermute | solution.py:1302
  372.8 25.0 %collective-permute-start.13 = (bf16[256,1024]{1,0:T(8,128)(2,1)S(1)}, bf16[256,1024]{1,0:T(8,128)(2,1)S(1)}, u32[]{:S(2)}, u32[]{:S(2)}) collective-permute-start(bf16[256,1024]{1,0:T(8,128)(2,1)S(1)} %get-tuple-element.340), channel_id=1, source_target_pairs={{0,4},{1,0},{2,5},{3,1},{4,6},{5,2},{6,7},{7,3},{8,12},{9,8},{10,1... | collective-permute-start | bytes 1572872 | tf_op jit(solution)/shard_map/ppermute | solution.py:1308
  373.0 24.8 %collective-permute-start.14 = (bf16[256,1024]{1,0:T(8,128)(2,1)S(1)}, bf16[256,1024]{1,0:T(8,128)(2,1)S(1)}, u32[]{:S(2)}, u32[]{:S(2)}) collective-permute-start(bf16[256,1024]{1,0:T(8,128)(2,1)S(1)} %get-tuple-element.341), channel_id=1, source_target_pairs={{0,0},{1,4},{2,1},{3,5},{4,2},{5,6},{6,3},{7,7},{8,8},{9,12},{10,9... | collective-permute-start | bytes 1572872 | tf_op jit(solution)/shard_map/ppermute | solution.py:1308
  453.8 74.7 %collective-permute-start.15 = (bf16[8,16,18944]{2,1,0:T(8,128)(2,1)}, bf16[8,16,18944]{2,1,0:T(8,128)(2,1)}, u32[]{:S(2)}, u32[]{:S(2)}) collective-permute-start(bf16[8,16,18944]{2,1,0:T(8,128)(2,1)} %get-tuple-element.219), channel_id=1, source_target_pairs={{0,16},{1,9},{2,18},{3,11},{4,20},{5,13},{6,22},{7,15},{8,24},{9,1... | collective-permute-start | bytes 14549000 | tf_op jit(solution)/shard_map/ppermute | solution.py:1302
  455.6 71.8 %collective-permute-start.16 = (bf16[256,1024]{1,0:T(8,128)(2,1)S(1)}, bf16[256,1024]{1,0:T(8,128)(2,1)S(1)}, u32[]{:S(2)}, u32[]{:S(2)}) collective-permute-start(bf16[256,1024]{1,0:T(8,128)(2,1)S(1)} %get-tuple-element.336), channel_id=1, source_target_pairs={{4,0},{0,1},{5,2},{1,3},{6,4},{2,5},{7,6},{3,7},{12,8},{8,9},{13,1... | collective-permute-start | bytes 1572872 | tf_op jit(solution)/shard_map/ppermute | solution.py:1308
  457.5 69.9 %collective-permute-start.17 = (bf16[256,1024]{1,0:T(8,128)(2,1)S(1)}, bf16[256,1024]{1,0:T(8,128)(2,1)S(1)}, u32[]{:S(2)}, u32[]{:S(2)}) collective-permute-start(bf16[256,1024]{1,0:T(8,128)(2,1)S(1)} %get-tuple-element.337), channel_id=1, source_target_pairs={{0,0},{4,1},{1,2},{5,3},{2,4},{6,5},{3,6},{7,7},{8,8},{12,9},{9,10... | collective-permute-start | bytes 1572872 | tf_op jit(solution)/shard_map/ppermute | solution.py:1308
  533.1 32.3 %collective-permute-start.18 = (bf16[4,16,18944]{2,1,0:T(8,128)(2,1)}, bf16[4,16,18944]{2,1,0:T(8,128)(2,1)}, u32[]{:S(2)}, u32[]{:S(2)}) collective-permute-start(bf16[4,16,18944]{2,1,0:T(8,128)(2,1)} %add_convert_fusion.1), channel_id=1, source_target_pairs={{0,8},{1,17},{2,10},{3,19},{4,12},{5,21},{6,14},{7,23},{8,0},{9,25... | collective-permute-start | bytes 7274504 | tf_op jit(solution)/shard_map/ppermute | solution.py:1302
  565.4 48.8 %collective-permute-start.19 = (bf16[8,16,6144]{2,1,0:T(8,128)(2,1)}, bf16[8,16,6144]{2,1,0:T(8,128)(2,1)S(1)}, u32[]{:S(2)}, u32[]{:S(2)}) collective-permute-start(bf16[8,16,6144]{2,1,0:T(8,128)(2,1)} %get-tuple-element.242), channel_id=1, source_target_pairs={{0,16},{1,9},{2,18},{3,11},{4,20},{5,13},{6,22},{7,15},{8,24},{9,1... | collective-permute-start | bytes 4718600 | tf_op jit(solution)/shard_map/ppermute | solution.py:1302
  576.3 64.5 %collective-permute-start.20 = (bf16[16,18944]{1,0:T(8,128)(2,1)}, bf16[16,18944]{1,0:T(8,128)(2,1)}, u32[]{:S(2)}, u32[]{:S(2)}) collective-permute-start(bf16[16,18944]{1,0:T(8,128)(2,1)} %get-tuple-element.327), channel_id=1, source_target_pairs={{0,2},{1,3},{2,0},{3,1},{4,6},{5,7},{6,4},{7,5},{8,10},{9,11},{10,... | collective-permute-start | bytes 1818632 | tf_op jit(solution)/shard_map/ppermute | solution.py:1302
  577.5 63.3 %collective-permute-start.21 = (bf16[16,18944]{1,0:T(8,128)(2,1)}, bf16[16,18944]{1,0:T(8,128)(2,1)}, u32[]{:S(2)}, u32[]{:S(2)}) collective-permute-start(bf16[16,18944]{1,0:T(8,128)(2,1)} %get-tuple-element.326), channel_id=1, source_target_pairs={{0,4},{1,5},{2,6},{3,7},{4,0},{5,1},{6,2},{7,3},{8,12},{9,13},{10,... | collective-permute-start | bytes 1818632 | tf_op jit(solution)/shard_map/ppermute | solution.py:1302
  578.6 62.2 %collective-permute-start.22 = (bf16[16,18944]{1,0:T(8,128)(2,1)}, bf16[16,18944]{1,0:T(8,128)(2,1)}, u32[]{:S(2)}, u32[]{:S(2)}) collective-permute-start(bf16[16,18944]{1,0:T(8,128)(2,1)} %get-tuple-element.325), channel_id=1, source_target_pairs={{0,6},{1,7},{2,4},{3,5},{4,2},{5,3},{6,0},{7,1},{8,14},{9,15},{10,... | collective-permute-start | bytes 1818632 | tf_op jit(solution)/shard_map/ppermute | solution.py:1302
  615.3 25.5 %collective-permute-start.23 = (bf16[4,16,6144]{2,1,0:T(8,128)(2,1)}, bf16[4,16,6144]{2,1,0:T(8,128)(2,1)S(1)}, u32[]{:S(2)}, u32[]{:S(2)}) collective-permute-start(bf16[4,16,6144]{2,1,0:T(8,128)(2,1)} %add_convert_fusion.2), channel_id=1, source_target_pairs={{0,8},{1,17},{2,10},{3,19},{4,12},{5,21},{6,14},{7,23},{8,0},{9,25... | collective-permute-start | bytes 2359304 | tf_op jit(solution)/shard_map/ppermute | solution.py:1302
  640.4 73.8 %collective-permute-start.24 = (bf16[8,16,18944]{2,1,0:T(8,128)(2,1)}, bf16[8,16,18944]{2,1,0:T(8,128)(2,1)}, u32[]{:S(2)}, u32[]{:S(2)}) collective-permute-start(bf16[8,16,18944]{2,1,0:T(8,128)(2,1)} %get-tuple-element.262), channel_id=1, source_target_pairs={{0,16},{1,9},{2,18},{3,11},{4,20},{5,13},{6,22},{7,15},{8,24},{9,1... | collective-permute-start | bytes 14549000 | tf_op jit(solution)/shard_map/ppermute | solution.py:1302
  644.4 75.4 %collective-permute-start.30 = (f32[88,512]{1,0:T(8,128)}, f32[88,512]{1,0:T(8,128)}, u32[]{:S(2)}, u32[]{:S(2)}) collective-permute-start(f32[88,512]{1,0:T(8,128)} %get-tuple-element.351), channel_id=1, source_target_pairs={{0,1},{1,0},{2,3},{3,2},{4,5},{5,4},{6,7},{7,6},{8,9},{9,8},{10,11... | collective-permute-start | bytes 540680 | tf_op jit(solution)/shard_map/ppermute | solution.py:1302
  644.8 69.3 %collective-permute-start.25 = (bf16[16,6144]{1,0:T(8,128)(2,1)S(1)}, bf16[16,6144]{1,0:T(8,128)(2,1)S(1)}, u32[]{:S(2)}, u32[]{:S(2)}) collective-permute-start(bf16[16,6144]{1,0:T(8,128)(2,1)S(1)} %get-tuple-element.344), channel_id=1, source_target_pairs={{0,2},{1,3},{2,0},{3,1},{4,6},{5,7},{6,4},{7,5},{8,10},{9,11},{10,... | collective-permute-start | bytes 589832 | tf_op jit(solution)/shard_map/ppermute | solution.py:1302
  645.2 69.0 %collective-permute-start.26 = (bf16[16,6144]{1,0:T(8,128)(2,1)S(1)}, bf16[16,6144]{1,0:T(8,128)(2,1)S(1)}, u32[]{:S(2)}, u32[]{:S(2)}) collective-permute-start(bf16[16,6144]{1,0:T(8,128)(2,1)S(1)} %get-tuple-element.343), channel_id=1, source_target_pairs={{0,4},{1,5},{2,6},{3,7},{4,0},{5,1},{6,2},{7,3},{8,12},{9,13},{10,... | collective-permute-start | bytes 589832 | tf_op jit(solution)/shard_map/ppermute | solution.py:1302
  647.1 67.0 %collective-permute-start.27 = (bf16[16,6144]{1,0:T(8,128)(2,1)S(1)}, bf16[16,6144]{1,0:T(8,128)(2,1)}, u32[]{:S(2)}, u32[]{:S(2)}) collective-permute-start(bf16[16,6144]{1,0:T(8,128)(2,1)S(1)} %get-tuple-element.342), channel_id=1, source_target_pairs={{0,6},{1,7},{2,4},{3,5},{4,2},{5,3},{6,0},{7,1},{8,14},{9,15},{10,... | collective-permute-start | bytes 589832 | tf_op jit(solution)/shard_map/ppermute | solution.py:1302
  717.9 29.4 %collective-permute-start.28 = (bf16[4,16,18944]{2,1,0:T(8,128)(2,1)}, bf16[4,16,18944]{2,1,0:T(8,128)(2,1)S(1)}, u32[]{:S(2)}, u32[]{:S(2)}) collective-permute-start(bf16[4,16,18944]{2,1,0:T(8,128)(2,1)} %add_convert_fusion), channel_id=1, source_target_pairs={{0,8},{1,17},{2,10},{3,19},{4,12},{5,21},{6,14},{7,23},{8,0},{9,25... | collective-permute-start | bytes 7274504 | tf_op jit(solution)/shard_map/ppermute | solution.py:1302
  828.1 5.7 collective-permute-start.29
  (45 other events, 413.5 us)

commit v4 on v3

--- a/solution.py
+++ b/solution.py
@@ -652,17 +652,27 @@
 
 
 class Gather:
-    def __init__(self, shard, blocks):
-        self.arrays = [shard]
+    def __init__(self, shards, blocks):
+        self.arrays = list(shards)
         self.blocks = blocks
-        self.outs = [jax.ShapeDtypeStruct(blocks.whole(4 * LOCAL), shard.dtype)]
+        self.outs = [jax.ShapeDtypeStruct(blocks.whole(4 * LOCAL), BF)]
         self.out_specs = [ANY]
         self.scratch = [SEND((36,)), SEND((36,)), SEND(())]
+        self.scratch += [pltpu.VMEM(blocks.shape, BF), SEND((len(shards),))]
 
     def run(self, at, ins, outs, scratch):
-        (shard,), (whole,) = ins, outs
-        send, recv, here = scratch
+        (whole,) = outs
+        send, recv, here, shard, load = scratch
         core = at.core
+        copies, begin = [], 0
+        for index, src in enumerate(ins):
+            cut = pl.ds(begin, src.shape[1])
+            copies.append(local(src, shard.at[:, cut], load.at[index]))
+            begin += src.shape[1]
+        for copy_in in copies:
+            copy_in.start()
+        for copy_in in copies:
+            copy_in.wait()
 
         def spot(step, of=core):
             return self.blocks.at(whole, at.chip(*step, of), of)
@@ -770,15 +780,15 @@
 
 
 class Front:
-    def __init__(self, tokens, shard, blocks, gains, gain_blocks, rest):
+    def __init__(self, tokens, shards, blocks, gains, gain_blocks, rest):
         self.rest = rest
-        self.parts = [Gather(shard, blocks), Gather(gains, gain_blocks), Rows(tokens)]
+        self.parts = [Gather(shards, blocks), Gather([gains], gain_blocks), Rows(tokens)]
         (rows,) = self.parts[2].outs
         rows, width = rows.shape
         columns = blocks.shape[1]
         qkv = jax.ShapeDtypeStruct((rows, columns), BF)
         self.swap = Swap([qkv], True)
-        self.arrays = [part.arrays[0] for part in self.parts]
+        self.arrays = [array for part in self.parts for array in part.arrays]
         self.outs = [part.outs[0] for part in self.parts]
         self.outs += [jax.ShapeDtypeStruct((rows, width), BF)] + self.swap.outs
         self.out_specs = [ANY] * 3 + [VMEM] + self.swap.out_specs
@@ -792,10 +802,11 @@
         ]
 
     def run(self, at, ins, outs, scratch):
-        stages, rest = [], list(scratch)
+        stages, rest, given = [], list(scratch), list(ins)
         for index, part in enumerate(self.parts):
             held = [rest.pop(0) for _ in part.scratch]
-            stages.append(part.run(at, [ins[index]], [outs[index]], held))
+            taken = [given.pop(0) for _ in part.arrays]
+            stages.append(part.run(at, taken, [outs[index]], held))
         swap_scratch = [rest.pop(0) for _ in self.swap.scratch]
         weights, tokens, gains, qkv, load = rest
         normed, swapped = outs[3], outs[4:]
@@ -846,53 +857,95 @@
 
 
 class Assemble:
-    def __init__(self, groups, blocks):
+    def __init__(self, groups, blocks, pieces):
         self.arrays = list(groups)
         self.blocks = blocks
+        self.pieces = pieces
         self.outs = [jax.ShapeDtypeStruct(b.whole(4 * LOCAL), groups[0].dtype) for b in blocks]
         self.out_specs = [ANY] * len(blocks)
-        n = len(blocks)
+        n = len(pieces)
         self.scratch = [SEND((n, 16)), SEND((n, 16)), SEND((n, 16)), SEND((16,))]
         self.scratch += [pltpu.VMEM((16,) + groups[0].shape[1:], groups[0].dtype)]
 
     def run(self, at, ins, outs, scratch):
         send, recv, here, load, held = scratch
 
-        def fetch(slot):
-            return local(ins[slot // 4].at[slot % 4], held.at[slot], load.at[slot])
-
-        def each():
-            for slot in range(16):
-                begin = 0
-                for index, blocks in enumerate(self.blocks):
-                    yield index, slot, pl.ds(begin, blocks.shape[1])
-                    begin += blocks.shape[1]
-
-        def spot(index, slot, core):
-            return self.blocks[index].at(outs[index], at.chip(*STEPS[slot], core), core)
-
-        def copies(index, slot, cut):
-            src = held.at[slot, :, cut]
-            dst = spot(index, slot, at.core)
-            return remote(
-                src, dst, send.at[index, slot], recv.at[index, slot], at.sibling()
-            ), local(src, dst, here.at[index, slot])
-
-        for slot in range(16):
-            fetch(slot).start()
+        def fetch(group, dz):
+            slot = group * 4 + dz
+            return local(ins[group].at[dz], held.at[slot], load.at[slot])
+
+        def copies(group, dz, core):
+            slot = group * 4 + dz
+            chip = at.chip(group % 2, group // 2, dz, core)
+            for index, (matrix, row, rows, column, width, down, over) in enumerate(self.pieces):
+                block = self.blocks[matrix].at(outs[matrix], chip, core)
+                dst = block.at[pl.ds(row, rows), pl.ds(column, width)]
+                src = held.at[slot, pl.ds(down, rows), pl.ds(over, width)]
+                yield src, dst, index, slot
+
+        def across(src, dst, index, slot):
+            return remote(src, dst, send.at[index, slot], recv.at[index, slot], at.sibling())
+
+        def own(src, dst, index, slot):
+            return local(src, dst, here.at[index, slot])
+
+        def every(do):
+            for group in range(4):
+
+                @pl.loop(0, 4)
+                def _(dz):
+                    do(group, dz)
+
+        every(lambda group, dz: fetch(group, dz).start())
         yield
-        for index, slot, cut in each():
-            if index == 0:
-                fetch(slot).wait()
-            for copy in copies(index, slot, cut):
-                copy.start()
+
+        def give(group, dz):
+            fetch(group, dz).wait()
+            for copy in copies(group, dz, at.core):
+                across(*copy).start()
+                own(*copy).start()
+
+        every(give)
         yield "last"
-        for index, slot, cut in each():
-            across, own = copies(index, slot, cut)
-            across.wait_send()
-            own.wait()
-            dst = spot(index, slot, 1 - at.core)
-            remote(dst, dst, send.at[index, slot], recv.at[index, slot], at.sibling()).wait_recv()
+
+        def end(group, dz):
+            for copy in copies(group, dz, at.core):
+                across(*copy).wait_send()
+                own(*copy).wait()
+            for copy in copies(group, dz, 1 - at.core):
+                across(*copy).wait_recv()
+
+        every(end)
+
+
+class Sort:
+    def __init__(self, rank, *arrays):
+        self.arrays = [rank, *arrays]
+        self.outs = [jax.ShapeDtypeStruct(array.shape, array.dtype) for array in arrays]
+        self.out_specs = [VMEM] * len(arrays)
+        self.scratch = [pltpu.VMEM(array.shape, array.dtype) for array in self.arrays]
+        self.scratch += [SEND((len(self.arrays),))]
+
+    def run(self, at, ins, outs, scratch):
+        held, load = scratch[:-1], scratch[-1]
+        copies = [local(src, dst, load.at[i]) for i, (src, dst) in enumerate(zip(ins, held))]
+        for copy in copies:
+            copy.start()
+        yield
+        for copy in copies:
+            copy.wait()
+        rank = held[0]
+        entries = rank.shape[1]
+        tile = BLOCK
+
+        @pl.loop(0, entries // tile)
+        def _(t):
+            at_row = lax.broadcasted_iota(jnp.int32, (tile, entries), 0) + t * tile
+            moved = jnp.where(rank[...] == at_row, 1.0, 0.0).astype(BF)
+            for src, dst in zip(held[1:], outs):
+                dst[pl.ds(pl.multiple_of(t * tile, tile), tile), :] = dot_nn(moved, src[...]).astype(BF)
+
+        yield "last"
 
 
 PACK = 16
@@ -1633,8 +1686,8 @@
     def up(values):
         return (values + BLOCK - 1) // BLOCK
 
-    step = QUERIES // BLOCK
-    diagonal = jnp.arange(rows // QUERIES, dtype=jnp.int32) * step
+    place = jnp.arange(rows // QUERIES, dtype=jnp.int32) * QUERIES
+    diagonal, end = place // BLOCK, up(place + QUERIES)
     first = jnp.min(per_block(start), axis=1) // BLOCK
     full = jnp.clip(up(jnp.max(per_block(start), axis=1)), first, diagonal)
     some = mem_high > mem_low
@@ -1642,11 +1695,11 @@
     mem_end = jnp.maximum(up(jnp.max(per_block(mem_high), axis=1)), mem_first)
     mem_full = jnp.clip(up(jnp.max(per_block(mem_low), axis=1)), mem_first, mem_end)
     mem_rest = jnp.clip(jnp.min(per_block(mem_high), axis=1) // BLOCK, mem_full, mem_end)
-    columns = (first, full, diagonal, diagonal + step, mem_first, mem_full, mem_rest, mem_end)
+    columns = (first, full, diagonal, end, mem_first, mem_full, mem_rest, mem_end)
     return bounds, jnp.stack(columns, axis=1)
 
 
-def sort_memory(memory, mem_docs):
+def memory_rank(mem_docs):
     entries = mem_docs.shape[0]
     which = members(mem_docs)
     lanes = which.reshape(-1, HEAD)
@@ -1657,10 +1710,7 @@
     first = before(jnp.sum(totals, axis=1))[:, None] + before(totals)
     rank = inside.reshape(NUMBERS, -1, HEAD) + first[:, :, None]
     rank = jnp.sum(which * rank.reshape(NUMBERS, entries), axis=0)
-    moved = (rank[None, :] == jnp.arange(entries, dtype=jnp.int32)[:, None]).astype(BF)
-    return tuple(
-        jnp.dot(moved, memory[index], preferred_element_type=F32).astype(BF) for index in range(2)
-    )
+    return rank[None]
 
 
 def columns(matrix, sizes):
@@ -1695,7 +1745,7 @@
 
     @pl.when(step == 0)
     def _():
-        both = stream[...] + dot_nn(att[...], out_w[...])
+        both = stream[...].astype(F32) + dot_nn(att[...], out_w[...])
         mixed[...] = both
         normed[...] = (both * inverse_rms(both) * gain[...]).astype(BF)
         result[...] = both
@@ -1714,6 +1764,7 @@
     steps = ff // FEED
     part = pl.BlockSpec((rows, FEED), lambda f: (0, f))
     whole = jax.ShapeDtypeStruct((rows, width), F32)
+    narrow = jax.ShapeDtypeStruct((rows, width), BF)
     wide = jax.ShapeDtypeStruct((rows, ff), F32)
     return pl.pallas_call(
         feed_kernel,
@@ -1726,7 +1777,7 @@
             pl.BlockSpec((FEED, width), lambda f: (f, 0)),
         ],
         out_specs=(VMEM, VMEM, VMEM, part, part),
-        out_shape=(whole, whole, jax.ShapeDtypeStruct((rows, width), BF), wide, wide),
+        out_shape=(whole, whole, narrow, wide, wide),
         compiler_params=pltpu.CompilerParams(vmem_limit_bytes=ROOM),
     )(attended, stream, out_w, gain, gate_up_w, gate_up_w, down_w)
 
@@ -1757,7 +1808,7 @@
     @pl.when(step == pl.num_programs(0) - 1)
     def _():
         back, grad_gain = norm_back(mixed[...], gain[...], total[...])
-        both = grad_new[...] + back
+        both = grad_new[...].astype(F32) + back
         grad_mixed[...] = both
         gain_g[...] = grad_gain
         low = both.astype(BF)
@@ -1811,16 +1862,16 @@
 
     @pl.when(step == pl.num_programs(0) - 1)
     def _():
-        back, grad_gain = norm_back(stream[...], gain[...], total[...])
-        grad_stream[...] = grad_mixed[...] + back
+        back, grad_gain = norm_back(stream[...].astype(F32), gain[...], total[...])
+        grad_stream[...] = (grad_mixed[...] + back).astype(grad_stream.dtype)
         gain_g[...] = grad_gain
 
 
-def projections_back(grad_mixed, grad_qkv, weights, kept):
+def projections_back(grad_mixed, grad_qkv, weights, kept, kind):
     gain, qkv_w = weights[:2]
     stream, normed = kept[:2]
     rows, width = stream.shape
-    size = 512
+    size = 1024
     part = pl.BlockSpec((width, size), lambda f: (0, f))
     grad_qkv_w, grad_stream, grad_gain = pl.pallas_call(
         project_kernel,
@@ -1830,7 +1881,7 @@
         out_specs=(part, VMEM, VMEM),
         out_shape=(
             jax.ShapeDtypeStruct(qkv_w.shape, BF),
-            jax.ShapeDtypeStruct((rows, width), F32),
+            jax.ShapeDtypeStruct((rows, width), kind),
             jax.ShapeDtypeStruct((1, width), F32),
         ),
         scratch_shapes=[pltpu.VMEM((width, rows), BF), pltpu.VMEM((rows, width), F32)],
@@ -1874,30 +1925,40 @@
     core = lax.rem(lax.axis_index("key"), 2)
     seg = lax.axis_index("key") // LOCAL
     gains = gain_columns((attn_gain1, ffn_gain1, attn_gain2, ffn_gain2))
-    qkv1 = jnp.concatenate((query_weight1, key_weight1, value_weight1), axis=1)
-    qkv2 = jnp.concatenate((second_query_weight, key_weight2, value_weight2), axis=1)
-    gate_up1 = jnp.concatenate((gate_weight1, up_weight1), axis=1)
-    gate_up2 = jnp.concatenate((gate_weight2, up_weight2), axis=1)
     downs = jnp.concatenate((down_weight1, down_weight2), axis=0)
     docs = jnp.concatenate((token_docs, memory_docs), axis=0)
     pairs = PairBlocks(2 * each, width // 2)
 
-    def own(matrix):
-        return RowBlocks(count, matrix.shape[1])
-
-    def gather(matrix):
-        return Gather(matrix, own(matrix))
+    def own(*matrices):
+        return RowBlocks(count, sum(matrix.shape[1] for matrix in matrices))
+
+    def gather(*matrices):
+        return Gather(matrices, own(*matrices))
 
     other = hop(downs, "core")
     down1 = pair_rows(down_weight1, other[:each], core)
     down2 = pair_rows(down_weight2, other[each:], core)
-    rest2 = jnp.concatenate((gate_up2, out_weight2), axis=1)
+    groups = 2 * each // count
+    tail = down2[groups * count :]
+    half = width // 4
+    rest2 = jnp.concatenate(
+        [gate_weight2, up_weight2, out_weight2]
+        + [down2[g * count : (g + 1) * count] for g in range(groups)]
+        + [jnp.concatenate((tail[:, :half], tail[:, half:]))],
+        axis=1,
+    )
+    over = 2 * ff + width
+    pieces = [(0, 0, count, 0, 2 * ff, 0, 0), (1, 0, count, 0, width, 0, 2 * ff)]
+    pieces += [(2, g * count, count, 0, 2 * half, 0, over + 2 * g * half) for g in range(groups)]
+    over += 2 * groups * half
+    pieces += [(2, groups * count, count // 2, p * half, half, p * count // 2, over) for p in range(2)]
+    first1 = (query_weight1, key_weight1, value_weight1)
     front, (docs,), (mk,), (mv,), (gu1_w,), (down1_w,), (out1_w,), (qkv2_w,) = exchange(
         "front", 1,
-        [Front(tokens, qkv1, own(qkv1), gains, own(gains), 3), Docs(docs),
+        [Front(tokens, first1, own(*first1), gains, own(gains), 3), Docs(docs),
          later(Memory(memory_keys), 1), later(Memory(memory_values), 7),
-         later(gather(gate_up1), 2), later(Gather(down1, pairs), 2),
-         later(gather(out_weight1), 2), later(gather(qkv2), 2)],
+         later(gather(gate_weight1, up_weight1), 2), later(Gather([down1], pairs), 2),
+         later(gather(out_weight1), 2), later(gather(second_query_weight, key_weight2, value_weight2), 2)],
     )
     qkv1_w, gains, rows, normed1, *heads1 = front
     own_docs = lax.dynamic_index_in_dim(docs, seg, 0, keepdims=False)
@@ -1906,37 +1967,35 @@
     bounds, ranges = mask_ranges(own_docs, own_mem_docs, reset)
     gains = [gains[:, i].astype(F32)[None] for i in range(4)]
     hops = {}
-    heads1, shards = join(heads1, (rest2, down2))
-    hops["rest"] = [gather_column(shard) for shard in shards]
+    heads1, rest2 = join(heads1, rest2)
+    hops["rest"] = gather_column(rest2)
 
     def rows1(out):
         ((attended,),) = exchange("to_rows_1", 3, [Swap([out], False)])
+        attended, rest = join(attended, hops["rest"])
+        hops["rest"] = rest, hop(rest, "a")
         return attended, out1_w, gu1_w, down1_w
 
     def rows2(out):
-        out, (rest, down) = join(out, hops["rest"])
-        (attended,), (gate_up_w, out_w), (down_w,) = exchange(
-            "to_rows_2", 5,
-            [Swap([out], False), Assemble(rest, [RowBlocks(count, 2 * ff), RowBlocks(count, width)]),
-             Assemble(down, [pairs])],
+        out, rest = join(out, hops["rest"])
+        blocks = (RowBlocks(count, 2 * ff), RowBlocks(count, width), pairs)
+        (attended,), (gate_up_w, out_w, down_w) = exchange(
+            "to_rows_2", 5, [Swap([out], False), Assemble(rest, blocks, pieces)]
         )
         attended, cot = join(attended, cotangent)
         hops["cot"] = rows_hops(cot)
         return attended, out_w, gate_up_w, down_w
 
     middle, weights1, kept1 = layer(
-        rows.astype(F32), normed1, heads1, qkv1_w, (gains[0], gains[1]), rows1, None, bounds, ranges
-    )
-    middle, rest = join(middle, hops["rest"])
-    hops["rest"] = [(column, hop(column, "a"), hop(column, "b")) for column in rest]
+        rows, normed1, heads1, qkv1_w, (gains[0], gains[1]), rows1, None, bounds, ranges
+    )
     normed2 = (middle * inverse_rms(middle) * gains[2]).astype(BF)
     qkv = jnp.dot(normed2, qkv2_w, preferred_element_type=F32).astype(BF)
-    (heads2,) = exchange("to_heads_2", 4, [Swap([qkv], True)])
-    heads2, firsts = join(heads2, [group[1] for group in hops["rest"]])
-    hops["rest"] = [
-        (group[0], first, group[2], hop(first, "b")) for group, first in zip(hops["rest"], firsts)
-    ]
-    memory = sort_memory((mk, mv), own_mem_docs)
+    qkv, (column, first) = join(qkv, hops["rest"])
+    hops["rest"] = column, first, hop(column, "b"), hop(first, "b")
+    heads2, memory = exchange(
+        "to_heads_2", 4, [Swap([qkv], True), Sort(memory_rank(own_mem_docs), mk, mv)]
+    )
     result, weights2, kept2 = layer(
         middle, normed2, heads2, qkv2_w, (gains[2], gains[3]), rows2, memory, bounds, ranges
     )
@@ -1956,7 +2015,7 @@
         return CoreSums((gate_g, own(gate_g)), (up_g, own(up_g)), (out_g, own(out_g)), (down_g, pairs))
 
     gate_g2, up_g2, down_g2, grad_mixed, grad_att, out_g2, gain_b2 = feed_back(
-        cot.astype(F32), weights2, kept2
+        cot, weights2, kept2
     )
     (grad_out,), sums2 = exchange(
         "back_to_heads_2", 6,
@@ -1968,7 +2027,7 @@
     ((grad_qkv,),) = exchange("back_to_rows_2", 7, [Swap(list(grads), False)])
     grad_qkv, (sums2, output) = join(grad_qkv, (sums2, output))
     sums2 = scatter_first(sums2)
-    grad_middle, gain_a2, qkv_g2 = projections_back(grad_mixed, grad_qkv, weights2, kept2)
+    grad_middle, gain_a2, qkv_g2 = projections_back(grad_mixed, grad_qkv, weights2, kept2, F32)
     (qkv_s2,) = exchange("projection_sums_2", 12, [CoreSums((qkv_g2, own(qkv_g2)))])
     grad_middle, (sums2, qkv_s2) = join(grad_middle, (sums2, qkv_s2))
     sums2 = scatter_z(sums2)
@@ -1979,27 +2038,31 @@
     )
     grad_att, qkv_s2 = join(grad_att, qkv_s2)
     qkv_s2 = scatter_first(qkv_s2)
-    (grad_out,), sums1 = exchange(
+    (grad_out,), wide1, rest1 = exchange(
         "back_to_heads_1", 8,
-        [Swap([grad_att], True), feed_sums(gate_g1, up_g1, down_g1, out_g1)],
+        [Swap([grad_att], True), CoreSums((gate_g1, own(gate_g1)), (up_g1, own(up_g1))),
+         CoreSums((out_g1, own(out_g1)), (down_g1, pairs))],
     )
     grad_out, (sums2, qkv_s2) = join(grad_out, (sums2, qkv_s2))
     qkv_s2 = scatter_z(qkv_s2)
-    sums1 = scatter_second(sums1)
+    wide1, rest1 = scatter_second(wide1), scatter_second(rest1)
     q, k, v, out, stat = kept1[2:7]
     grads = attend_back(q, k, v, None, bounds, ranges, out, stat, grad_out)
+    grads, wide1 = join(grads, wide1)
+    wide1 = scatter_first(wide1)
     ((grad_qkv,),) = exchange("back_to_rows_1", 9, [Swap(list(grads), False)])
-    grad_qkv, (sums1, qkv_s2) = join(grad_qkv, (sums1, qkv_s2))
-    sums1 = scatter_first(sums1)
-    grad_rows, gain_a1, qkv_g1 = projections_back(grad_mixed, grad_qkv, weights1, kept1)
+    grad_qkv, (wide1, rest1, qkv_s2) = join(grad_qkv, (wide1, rest1, qkv_s2))
+    rest1 = scatter_first(rest1)
+    wide1 = scatter_z(wide1)
+    grad_rows, gain_a1, qkv_g1 = projections_back(grad_mixed, grad_qkv, weights1, kept1, BF)
     gain_grads = gain_columns([g[0] for g in (gain_a1, gain_b1, gain_a2, gain_b2)]).astype(BF)
-    here, second, first = sums1
-    (grad_tokens,), (gate_s1, up_s1, out_s1, down_s1), (q_s1,), (k_s1,), (v_s1,), (gain_s,) = exchange(
+    (grad_tokens,), (out_s1, down_s1), (q_s1,), (k_s1,), (v_s1,), (gain_s,) = exchange(
         "back_to_owners", 10,
-        [Chunks(grad_rows.astype(BF)), LineSums((here, second, first), shapes, ((0,), (1,), (2, 3)))]
+        [Chunks(grad_rows), LineSums(rest1, shapes[2:], ((0,), (1,)))]
         + [Scatter(qkv_g1, ColumnBlocks(count, width, i), i) for i in range(3)]
         + [Scatter(gain_grads, own(gain_grads))],
     )
+    gate_s1, up_s1 = unpack(scatter_end(wide1), shapes[:2])
     gate_s2, up_s2, out_s2, down_s2 = unpack(scatter_end(sums2), shapes)
     (qkv_s2,) = unpack(scatter_end(qkv_s2), ((count, 3 * width),))
     q_s2, k_s2, v_s2 = columns(qkv_s2, (width,) * 3)

time: 841 us -> 825 us (0.981)
  Pallas kernels: 692 us -> 681 us
  matrix products: 17.7 us -> 8.04 us
  starting transfers between devices: 49.2 us -> 40.6 us
    pallas_call x10, Pallas kernels: 469 us -> 453 us  [exchange(): pl.pallas_call(kernel, name=name, out_shape=[o for p in parts for o in p....]
    dot_general x3 -> x1, matrix products: 9.74 us -> 0.14 us  [memory_rank(): jnp.dot(lanes.astype(BF), earlier, preferred_element_type=F32)]
    ppermute x27 -> x26, starting transfers between devices: 40.8 us -> 32.3 us  [hop(): return lax.ppermute(values, ('grp', 'key'), pairs)]
    ppermute x27 -> x26, waiting for transfers between devices: 14.2 us -> 17.2 us  [hop(): return lax.ppermute(values, ('grp', 'key'), pairs)]
  transfers between devices with their start and end apart: 31 -> 30, of which waited for: 3 -> 4; matrix products, arithmetic and copies ran while one was open for 7% -> 7% of each run, Pallas kernels for 45% -> 46%
where the time goes in v4:
time: 825 us; the launch traced here: 817 us
  Pallas kernels  681 us (83%)
  other arithmetic  47.2 us (6%)
  starting transfers between devices  40.6 us (5%)
  local copies, waits for them, and re-layouts  20.8 us (3%)
  waiting for transfers between devices  17.2 us (2%)
    pallas_call x10, Pallas kernels, exchange(): pl.pallas_call(kernel, name=name, out_shape=[o for p in parts for o in p....  453 us
    pallas_call x2, Pallas kernels, feed_back(): pl.pallas_call(feed_back_kernel, name='feed_back', grid=(steps,), in_spec...  68.4 us
    pallas_call x2, Pallas kernels, attend_back(): pl.pallas_call(functools.partial(attend_back_kernel, memory is not None),...  54.2 us
    pallas_call x2, Pallas kernels, feed(): pl.pallas_call(feed_kernel, name='feed', grid=(steps,), in_specs=[VMEM, V...  39.6 us
    pallas_call x2, Pallas kernels, attend(): pl.pallas_call(functools.partial(attend_kernel, memory is not None), name...  36.7 us
    ppermute x26, starting transfers between devices, hop(): return lax.ppermute(values, ('grp', 'key'), pairs)  32.3 us
    pallas_call x2, Pallas kernels, projections_back(): pl.pallas_call(project_kernel, name='projections_back', grid=(grad_qkv.sh...  28.7 us
    ppermute x26, waiting for transfers between devices, hop(): return lax.ppermute(values, ('grp', 'key'), pairs)  17.2 us
  transfers between devices with their start and end apart: 30, of which 4 were waited for; matrix products, arithmetic and copies ran while one was open for 7% of the time, Pallas kernels for 46%

profile of v4, /device:TPU:1, one launch (start us, length us, event | category | flops | bytes accessed | tf_op | source)
XLA Modules:
  0.0 817.2 jit_solution(11751962379381490187)
XLA Ops:
  10.3 166.5 %front.1 = (bf16[1024,3072]{1,0:T(8,128)(2,1)}, bf16[1024,128]{1,0:T(8,128)(2,1)}, bf16[512,1024]{1,0:T(8,128)(2,1)}, bf16[512,1024]{1,0:T(8,128)(2,1)}, bf16[20...) custom-call(bf16[32,1024]{1,0:T(8,128)(2,1)} %refs_0_.1, ...), custom_call_target="tpu_custom_call" | custom-call | tf_op jit(solution)/shard_map/front/pallas_call | solution.py:1325
  176.8 6.0 collective-permute-start.1
  182.8 3.4 collective-permute-start.2
  192.7 12.8 %attend.2 = (bf16[2048,256]{1,0:T(8,128)(2,1)}, f32[8,2048]{1,0:T(8,128)}) custom-call(s32[4,8]{1,0:T(4,128)} %stack.105.ranges, bf16[2048,256]{1,0:T(8,128)(2,1)} %get-tuple-element.165.refs_0_, bf16[2048,256]{1,0:T(8,128)(2,1)} %get-tuple-element.166.refs_1_.refs_5_, bf16[2048,256]{1,0:T(8,128)(2,1)} %get-tuple-element.167.refs_2_.refs_6_, ...), custom_call_target="tpu_custom_call" | custom-call | tf_op jit(solution)/shard_map/attend/pallas_call | solution.py:1543
  205.5 31.0 %to_rows_1.1.att = bf16[512,1024]{1,0:T(8,128)(2,1)} custom-call(bf16[2048,256]{1,0:T(8,128)(2,1)} %get-tuple-element.168.refs_0_.refs_2_), custom_call_target="tpu_custom_call" | custom-call | tf_op jit(solution)/shard_map/to_rows_1/pallas_call | solution.py:1325
  240.8 19.5 %feed.2 = (f32[512,1024]{1,0:T(8,128)}, f32[512,1024]{1,0:T(8,128)}, bf16[512,1024]{1,0:T(8,128)(2,1)}, f32[512,2816]{1,0:T(8,128)}, f32[512,2816]{1,0:T(8,128)}) custom-call(bf16[512,1024]{1,0:T(8,128)(2,1)} %to_rows_1.1.att, bf16[512,1024]{1,0:T(8,128)(2,1)} %get-tuple-element.171.stream, bf16[1024,1024]{1,0:T(8,128)(2,1)} %get-tuple-element.172.out_w, ...), custom_call_target="tpu_custom_call" | custom-call | tf_op jit(solution)/shard_map/feed/pallas_call | solution.py:1769
  262.8 7.9 convolution_convert_fusion.refs_0_
  272.2 42.7 %to_heads_2.1 = (bf16[2048,256]{1,0:T(8,128)(2,1)}, bf16[2048,256]{1,0:T(8,128)(2,1)}, bf16[2048,256]{1,0:T(8,128)(2,1)}, bf16[2048,256]{1,0:T(8,128)(2,1)}, bf16[2048,256]{1,0:T(8,128)(2,1)}) custom-call(bf16[512,3072]{1,0:T(8,128)(2,1)} %convolution_convert_fusion.refs_0_, s32[1,2048]{1,0:T(1,128)} %bitcast.123, ...), custom_call_target="tpu_custom_call" | custom-call | tf_op jit(solution)/shard_map/to_heads_2/pallas_call | solution.py:1325
  315.0 23.9 %attend.3 = (bf16[2048,256]{1,0:T(8,128)(2,1)}, f32[8,2048]{1,0:T(8,128)}) custom-call(s32[4,8]{1,0:T(4,128)} %stack.105.ranges, bf16[2048,256]{1,0:T(8,128)(2,1)} %get-tuple-element.182.refs_0_, bf16[2048,256]{1,0:T(8,128)(2,1)} %get-tuple-element.183.refs_1_.refs_5_, bf16[2048,256]{1,0:T(8,128)(2,1)} %get-tuple-element.184.refs_2_.refs_6_, ...), custom_call_target="tpu_custom_call" | custom-call | tf_op jit(solution)/shard_map/attend/pallas_call | solution.py:1543
  338.9 21.5 %to_rows_2.1 = (bf16[512,1024]{1,0:T(8,128)(2,1)}, bf16[1024,5632]{1,0:T(8,128)(2,1)}, bf16[1024,1024]{1,0:T(8,128)(2,1)}, bf16[2816,1024]{1,0:T(8,128)(2,1)}) custom-call(bf16[2048,256]{1,0:T(8,128)(2,1)} %get-tuple-element.190.refs_0_.refs_2_, bf16[4,32,9472]{2,1,0:T(8,128)(2,1)} %pad_maximum_fusion.refs_1_, bf16[4,32,9472]{2,1,0:T(8,128)(2,1)} %copy-done.5, ...), custom_call_target="tpu_custom_call" | custom-call | tf_op jit(solution)/shard_map/to_rows_2/pallas_call | solution.py:1325
  360.7 4.4 collective-permute-start.8
  365.2 20.0 %feed.3 = (f32[512,1024]{1,0:T(8,128)}, f32[512,1024]{1,0:T(8,128)}, bf16[512,1024]{1,0:T(8,128)(2,1)}, f32[512,2816]{1,0:T(8,128)}, f32[512,2816]{1,0:T(8,128)}) custom-call(bf16[512,1024]{1,0:T(8,128)(2,1)} %get-tuple-element.197.att, f32[512,1024]{1,0:T(8,128)} %get-tuple-element.176.stream, bf16[1024,1024]{1,0:T(8,128)(2,1)} %get-tuple-element.198.out_w, ...), custom_call_target="tpu_custom_call" | custom-call | tf_op jit(solution)/shard_map/feed/pallas_call | solution.py:1769
  386.3 34.1 %feed_back.2 = (bf16[1024,2816]{1,0:T(8,128)(2,1)}, bf16[1024,2816]{1,0:T(8,128)(2,1)}, bf16[2816,1024]{1,0:T(8,128)(2,1)}, f32[512,1024]{1,0:T(8,128)}, bf16[51...) custom-call(bf16[512,1024]{1,0:T(8,128)(2,1)} %pad_maximum_fusion.1.grad_new, ...), custom_call_target="tpu_custom_call" | custom-call | tf_op jit(solution)/shard_map/feed_back/pallas_call | solution.py:1832
  420.4 20.4 %back_to_heads_2.1 = (bf16[2048,256]{1,0:T(8,128)(2,1)}, bf16[4,16,18944]{2,1,0:T(8,128)(2,1)}, bf16[4,16,18944]{2,1,0:T(8,128)(2,1)}, bf16[8,16,18944]{2,1,0:T(8,128)(2,1)}) custom-call(bf16[512,1024]{1,0:T(8,128)(2,1)} %get-tuple-element.205.refs_0_, bf16[1024,2816]{1,0:T(8,128)(2,1)} %get-tuple-element.206.refs_1_, ...), custom_call_target="tpu_custom_call" | custom-call | tf_op jit(solution)/shard_map/back_to_heads_2/pallas_call | solution.py:1325
  441.8 3.3 collective-permute-start.11
  445.2 33.1 %attend_back.2 = (bf16[2048,256]{1,0:T(8,128)(2,1)}, bf16[2048,256]{1,0:T(8,128)(2,1)}, bf16[2048,256]{1,0:T(8,128)(2,1)}) custom-call(s32[4,8]{1,0:T(4,128)} %stack.105.ranges, bf16[2048,256]{1,0:T(8,128)(2,1)} %get-tuple-element.182.refs_0_, bf16[2048,256]{1,0:T(8,128)(2,1)} %get-tuple-element.210.refs_1_, ...), custom_call_target="tpu_custom_call" | custom-call | tf_op jit(solution)/shard_map/attend_back/pallas_call | solution.py:1633
  478.3 37.2 %back_to_rows_2.1.grad_qkv = bf16[512,3072]{1,0:T(8,128)(2,1)} custom-call(bf16[2048,256]{1,0:T(8,128)(2,1)} %get-tuple-element.212.refs_0_, bf16[2048,256]{1,0:T(8,128)(2,1)} %get-tuple-element.213.refs_1_, bf16[2048,256]{1,0:T(8,128)(2,1)} %get-tuple-element.214.refs_2_), custom_call_target="tpu_custom_call" | custom-call | tf_op jit(solution)/shard_map/back_to_rows_2/pallas_call | solution.py:1325
  517.5 3.7 add_convert_fusion
  523.0 14.6 %projections_back.2 = (bf16[1024,3072]{1,0:T(8,128)(2,1)}, f32[512,1024]{1,0:T(8,128)}, f32[1,1024]{1,0:T(1,128)}) custom-call(f32[512,1024]{1,0:T(8,128)} %get-tuple-element.220.grad_mixed, f32[512,1024]{1,0:T(8,128)} %get-tuple-element.176.stream, f32[1,1024]{1,0:T(1,128)} %bitcast.122, bf16[512,1024]{1,0:T(8,128)(2,1)} %copy-done.2, ...), custom_call_target="tpu_custom_call" | custom-call | tf_op jit(solution)/shard_map/projections_back/pallas_call | solution.py:1876
  537.6 8.5 %projection_sums_2.1 = (bf16[4,16,6144]{2,1,0:T(8,128)(2,1)}, bf16[4,16,6144]{2,1,0:T(8,128)(2,1)}, bf16[8,16,6144]{2,1,0:T(8,128)(2,1)}) custom-call(bf16[1024,3072]{1,0:T(8,128)(2,1)} %get-tuple-element.226.refs_0_), custom_call_target="tpu_custom_call" | custom-call | tf_op jit(solution)/shard_map/projection_sums_2/pallas_call | solution.py:1325
  546.7 3.6 collective-permute-done.12
  551.4 5.5 fusion.37
  561.7 34.3 %feed_back.3 = (bf16[1024,2816]{1,0:T(8,128)(2,1)}, bf16[1024,2816]{1,0:T(8,128)(2,1)}, bf16[2816,1024]{1,0:T(8,128)(2,1)}, f32[512,1024]{1,0:T(8,128)}, bf16[51...) custom-call(f32[512,1024]{1,0:T(8,128)} %get-tuple-element.230.grad_new, ...), custom_call_target="tpu_custom_call" | custom-call | tf_op jit(solution)/shard_map/feed_back/pallas_call | solution.py:1832
  599.3 23.0 %back_to_heads_1.1 = (bf16[2048,256]{1,0:T(8,128)(2,1)}, bf16[4,16,11264]{2,1,0:T(8,128)(2,1)}, bf16[4,16,11264]{2,1,0:T(8,128)(2,1)}, bf16[8,16,11264]{2,1,0:T(...) custom-call(bf16[512,1024]{1,0:T(8,128)(2,1)} %get-tuple-element.241.refs_0_, ...), custom_call_target="tpu_custom_call" | custom-call | tf_op jit(solution)/shard_map/back_to_heads_1/pallas_call | solution.py:1325
  629.6 21.1 %attend_back.3 = (bf16[2048,256]{1,0:T(8,128)(2,1)}, bf16[2048,256]{1,0:T(8,128)(2,1)}, bf16[2048,256]{1,0:T(8,128)(2,1)}) custom-call(s32[4,8]{1,0:T(4,128)} %stack.105.ranges, bf16[2048,256]{1,0:T(8,128)(2,1)} %get-tuple-element.165.refs_0_, bf16[2048,256]{1,0:T(8,128)(2,1)} %get-tuple-element.253.refs_1_, ...), custom_call_target="tpu_custom_call" | custom-call | tf_op jit(solution)/shard_map/attend_back/pallas_call | solution.py:1633
  652.3 4.0 collective-permute-done.18
  656.3 2.8 add_convert_fusion.1
  663.3 39.3 %back_to_rows_1.1.grad_qkv = bf16[512,3072]{1,0:T(8,128)(2,1)} custom-call(bf16[2048,256]{1,0:T(8,128)(2,1)} %get-tuple-element.261.refs_0_, bf16[2048,256]{1,0:T(8,128)(2,1)} %get-tuple-element.262.refs_1_, bf16[2048,256]{1,0:T(8,128)(2,1)} %get-tuple-element.263.refs_2_), custom_call_target="tpu_custom_call" | custom-call | tf_op jit(solution)/shard_map/back_to_rows_1/pallas_call | solution.py:1325
  713.5 14.1 %projections_back.3 = (bf16[1024,3072]{1,0:T(8,128)(2,1)}, bf16[512,1024]{1,0:T(8,128)(2,1)}, f32[1,1024]{1,0:T(1,128)}) custom-call(f32[512,1024]{1,0:T(8,128)} %get-tuple-element.235.grad_mixed, bf16[512,1024]{1,0:T(8,128)(2,1)} %get-tuple-element.171.stream, f32[1,1024]{1,0:T(1,128)} %bitcast.124, bf16[512,1024]{1,0:T(8,128)(2,1)} %get-tuple-element.236.normed, ...), custom_call_target="tpu_custom_call" | custom-call | tf_op jit(solution)/shard_map/projections_back/pallas_call | solution.py:1876
  736.1 6.9 collective-permute-done.24.refs_3_
  742.9 63.2 %back_to_owners.1 = (bf16[2,256,1024]{2,1,0:T(8,128)(2,1)}, f32[32,1024]{1,0:T(8,128)}, f32[176,512]{1,0:T(8,128)}, f32[32,1024]{1,0:T(8,128)}, f32[32,1024]{1,0...) custom-call(bf16[512,1024]{1,0:T(8,128)(2,1)} %get-tuple-element.275.refs_0_, ...), custom_call_target="tpu_custom_call" | custom-call | tf_op jit(solution)/shard_map/back_to_owners/pallas_call | solution.py:1325
  810.0 2.8 convert_element_type.225
  (235 shorter events, 79.5 us)
Async XLA Ops:
  1.8 7.6 collective-permute-start
  176.8 59.6 %collective-permute-start.1 = (bf16[32,9472]{1,0:T(8,128)(2,1)S(1)}, bf16[32,9472]{1,0:T(8,128)(2,1)S(1)}, u32[]{:S(2)}, u32[]{:S(2)}) collective-permute-start(bf16[32,9472]{1,0:T(8,128)(2,1)S(1)} %constant_dynamic-update-slice_fusion), channel_id=1, source_target_pairs={{0,2},{1,3},{2,0},{3,1},{4,6},{5,7},{6,4},{7,5},{8,10},{9,11},{10,... | collective-permute-start | bytes 1818632 | tf_op jit(solution)/shard_map/ppermute | solution.py:1355
  182.8 53.7 %collective-permute-start.2 = (bf16[32,9472]{1,0:T(8,128)(2,1)S(1)}, bf16[32,9472]{1,0:T(8,128)(2,1)S(1)}, u32[]{:S(2)}, u32[]{:S(2)}) collective-permute-start(bf16[32,9472]{1,0:T(8,128)(2,1)S(1)} %constant_dynamic-update-slice_fusion), channel_id=1, source_target_pairs={{0,4},{1,5},{2,6},{3,7},{4,0},{5,1},{6,2},{7,3},{8,12},{9,13},{10,... | collective-permute-start | bytes 1818632 | tf_op jit(solution)/shard_map/ppermute | solution.py:1355
  186.2 50.3 %collective-permute-start.3 = (bf16[32,9472]{1,0:T(8,128)(2,1)S(1)}, bf16[32,9472]{1,0:T(8,128)(2,1)S(1)}, u32[]{:S(2)}, u32[]{:S(2)}) collective-permute-start(bf16[32,9472]{1,0:T(8,128)(2,1)S(1)} %constant_dynamic-update-slice_fusion), channel_id=1, source_target_pairs={{0,6},{1,7},{2,4},{3,5},{4,2},{5,3},{6,0},{7,1},{8,14},{9,15},{10,... | collective-permute-start | bytes 1818632 | tf_op jit(solution)/shard_map/ppermute | solution.py:1355
  238.3 32.4 %collective-permute-start.4 = (bf16[4,32,9472]{2,1,0:T(8,128)(2,1)}, bf16[4,32,9472]{2,1,0:T(8,128)(2,1)S(1)}, u32[]{:S(2)}, u32[]{:S(2)}) collective-permute-start(bf16[4,32,9472]{2,1,0:T(8,128)(2,1)} %pad_maximum_fusion.refs_1_), channel_id=1, source_target_pairs={{0,8},{1,17},{2,10},{3,19},{4,12},{5,21},{6,14},{7,23},{8,0},{9,25... | collective-permute-start | bytes 7274504 | tf_op jit(solution)/shard_map/ppermute | solution.py:1355
  270.7 44.3 %copy-start.5 = (bf16[4,32,9472]{2,1,0:T(8,128)(2,1)}, bf16[4,32,9472]{2,1,0:T(8,128)(2,1)S(1)}, u32[]{:S(2)}) copy-start(bf16[4,32,9472]{2,1,0:T(8,128)(2,1)S(1)} %collective-permute-done.4.refs_2_) | copy-start | bytes 7274500
  270.7 68.2 %collective-permute-start.5 = (bf16[4,32,9472]{2,1,0:T(8,128)(2,1)}, bf16[4,32,9472]{2,1,0:T(8,128)(2,1)}, u32[]{:S(2)}, u32[]{:S(2)}) collective-permute-start(bf16[4,32,9472]{2,1,0:T(8,128)(2,1)} %pad_maximum_fusion.refs_1_), channel_id=1, source_target_pairs={{0,16},{1,9},{2,18},{3,11},{4,20},{5,13},{6,22},{7,15},{8,24},{9,1... | collective-permute-start | bytes 7274504 | tf_op jit(solution)/shard_map/ppermute | solution.py:1355
  270.8 68.1 %collective-permute-start.6 = (bf16[4,32,9472]{2,1,0:T(8,128)(2,1)S(1)}, bf16[4,32,9472]{2,1,0:T(8,128)(2,1)}, u32[]{:S(2)}, u32[]{:S(2)}) collective-permute-start(bf16[4,32,9472]{2,1,0:T(8,128)(2,1)S(1)} %collective-permute-done.4.refs_2_), channel_id=1, source_target_pairs={{0,16},{1,9},{2,18},{3,11},{4,20},{5,13},{6,22},{7,15},{8,24},{9,1... | collective-permute-start | bytes 7274504 | tf_op jit(solution)/shard_map/ppermute | solution.py:1355
  360.5 24.7 %collective-permute-start.7 = (bf16[256,1024]{1,0:T(8,128)(2,1)S(1)}, bf16[256,1024]{1,0:T(8,128)(2,1)S(1)}, u32[]{:S(2)}, u32[]{:S(2)}) collective-permute-start(bf16[256,1024]{1,0:T(8,128)(2,1)S(1)} %get-tuple-element.353), channel_id=1, source_target_pairs={{0,4},{1,0},{2,5},{3,1},{4,6},{5,2},{6,7},{7,3},{8,12},{9,8},{10,1... | collective-permute-start | bytes 1572872 | tf_op jit(solution)/shard_map/ppermute | solution.py:1361
  360.7 24.5 %collective-permute-start.8 = (bf16[256,1024]{1,0:T(8,128)(2,1)S(1)}, bf16[256,1024]{1,0:T(8,128)(2,1)S(1)}, u32[]{:S(2)}, u32[]{:S(2)}) collective-permute-start(bf16[256,1024]{1,0:T(8,128)(2,1)S(1)} %get-tuple-element.354), channel_id=1, source_target_pairs={{0,0},{1,4},{2,1},{3,5},{4,2},{5,6},{6,3},{7,7},{8,8},{9,12},{10,9... | collective-permute-start | bytes 1572872 | tf_op jit(solution)/shard_map/ppermute | solution.py:1361
  440.8 75.8 %collective-permute-start.9 = (bf16[8,16,18944]{2,1,0:T(8,128)(2,1)}, bf16[8,16,18944]{2,1,0:T(8,128)(2,1)}, u32[]{:S(2)}, u32[]{:S(2)}) collective-permute-start(bf16[8,16,18944]{2,1,0:T(8,128)(2,1)} %get-tuple-element.217), channel_id=1, source_target_pairs={{0,16},{1,9},{2,18},{3,11},{4,20},{5,13},{6,22},{7,15},{8,24},{9,1... | collective-permute-start | bytes 14549000 | tf_op jit(solution)/shard_map/ppermute | solution.py:1355
  441.5 74.0 %collective-permute-start.10 = (bf16[256,1024]{1,0:T(8,128)(2,1)S(1)}, bf16[256,1024]{1,0:T(8,128)(2,1)S(1)}, u32[]{:S(2)}, u32[]{:S(2)}) collective-permute-start(bf16[256,1024]{1,0:T(8,128)(2,1)S(1)} %get-tuple-element.349), channel_id=1, source_target_pairs={{4,0},{0,1},{5,2},{1,3},{6,4},{2,5},{7,6},{3,7},{12,8},{8,9},{13,1... | collective-permute-start | bytes 1572872 | tf_op jit(solution)/shard_map/ppermute | solution.py:1361
  441.8 73.7 %collective-permute-start.11 = (bf16[256,1024]{1,0:T(8,128)(2,1)S(1)}, bf16[256,1024]{1,0:T(8,128)(2,1)S(1)}, u32[]{:S(2)}, u32[]{:S(2)}) collective-permute-start(bf16[256,1024]{1,0:T(8,128)(2,1)S(1)} %get-tuple-element.350), channel_id=1, source_target_pairs={{0,0},{4,1},{1,2},{5,3},{2,4},{6,5},{3,6},{7,7},{8,8},{12,9},{9,10... | collective-permute-start | bytes 1572872 | tf_op jit(solution)/shard_map/ppermute | solution.py:1361
  521.3 29.0 %collective-permute-start.12 = (bf16[4,16,18944]{2,1,0:T(8,128)(2,1)}, bf16[4,16,18944]{2,1,0:T(8,128)(2,1)}, u32[]{:S(2)}, u32[]{:S(2)}) collective-permute-start(bf16[4,16,18944]{2,1,0:T(8,128)(2,1)} %add_convert_fusion), channel_id=1, source_target_pairs={{0,8},{1,17},{2,10},{3,19},{4,12},{5,21},{6,14},{7,23},{8,0},{9,25... | collective-permute-start | bytes 7274504 | tf_op jit(solution)/shard_map/ppermute | solution.py:1355
  550.3 45.8 %collective-permute-start.13 = (bf16[8,16,6144]{2,1,0:T(8,128)(2,1)}, bf16[8,16,6144]{2,1,0:T(8,128)(2,1)S(1)}, u32[]{:S(2)}, u32[]{:S(2)}) collective-permute-start(bf16[8,16,6144]{2,1,0:T(8,128)(2,1)} %get-tuple-element.240), channel_id=1, source_target_pairs={{0,16},{1,9},{2,18},{3,11},{4,20},{5,13},{6,22},{7,15},{8,24},{9,1... | collective-permute-start | bytes 4718600 | tf_op jit(solution)/shard_map/ppermute | solution.py:1355
  558.1 64.5 %collective-permute-start.14 = (bf16[16,18944]{1,0:T(8,128)(2,1)}, bf16[16,18944]{1,0:T(8,128)(2,1)}, u32[]{:S(2)}, u32[]{:S(2)}) collective-permute-start(bf16[16,18944]{1,0:T(8,128)(2,1)} %get-tuple-element.337), channel_id=1, source_target_pairs={{0,2},{1,3},{2,0},{3,1},{4,6},{5,7},{6,4},{7,5},{8,10},{9,11},{10,... | collective-permute-start | bytes 1818632 | tf_op jit(solution)/shard_map/ppermute | solution.py:1355
  558.5 65.4 %collective-permute-start.15 = (bf16[16,18944]{1,0:T(8,128)(2,1)}, bf16[16,18944]{1,0:T(8,128)(2,1)}, u32[]{:S(2)}, u32[]{:S(2)}) collective-permute-start(bf16[16,18944]{1,0:T(8,128)(2,1)} %get-tuple-element.336), channel_id=1, source_target_pairs={{0,4},{1,5},{2,6},{3,7},{4,0},{5,1},{6,2},{7,3},{8,12},{9,13},{10,... | collective-permute-start | bytes 1818632 | tf_op jit(solution)/shard_map/ppermute | solution.py:1355
  559.6 64.2 %collective-permute-start.16 = (bf16[16,18944]{1,0:T(8,128)(2,1)}, bf16[16,18944]{1,0:T(8,128)(2,1)}, u32[]{:S(2)}, u32[]{:S(2)}) collective-permute-start(bf16[16,18944]{1,0:T(8,128)(2,1)} %get-tuple-element.335), channel_id=1, source_target_pairs={{0,6},{1,7},{2,4},{3,5},{4,2},{5,3},{6,0},{7,1},{8,14},{9,15},{10,... | collective-permute-start | bytes 1818632 | tf_op jit(solution)/shard_map/ppermute | solution.py:1355
  561.7 34.4 %copy-start.16 = (bf16[4,16,6144]{2,1,0:T(8,128)(2,1)S(1)}, bf16[4,16,6144]{2,1,0:T(8,128)(2,1)}, u32[]{:S(2)}) copy-start(bf16[4,16,6144]{2,1,0:T(8,128)(2,1)} %get-tuple-element.252) | copy-start | bytes 2359300
  597.3 26.5 %collective-permute-start.17 = (bf16[4,16,6144]{2,1,0:T(8,128)(2,1)}, bf16[4,16,6144]{2,1,0:T(8,128)(2,1)S(1)}, u32[]{:S(2)}, u32[]{:S(2)}) collective-permute-start(bf16[4,16,6144]{2,1,0:T(8,128)(2,1)} %add_convert_fusion.3), channel_id=1, source_target_pairs={{0,8},{1,17},{2,10},{3,19},{4,12},{5,21},{6,14},{7,23},{8,0},{9,25... | collective-permute-start | bytes 2359304 | tf_op jit(solution)/shard_map/ppermute | solution.py:1355
  622.3 34.0 %collective-permute-start.18 = (bf16[8,16,11264]{2,1,0:T(8,128)(2,1)}, bf16[8,16,11264]{2,1,0:T(8,128)(2,1)}, u32[]{:S(2)}, u32[]{:S(2)}) collective-permute-start(bf16[8,16,11264]{2,1,0:T(8,128)(2,1)} %get-tuple-element.260), channel_id=1, source_target_pairs={{0,16},{1,9},{2,18},{3,11},{4,20},{5,13},{6,22},{7,15},{8,24},{9,1... | collective-permute-start | bytes 8650760 | tf_op jit(solution)/shard_map/ppermute | solution.py:1355
  622.6 80.0 %collective-permute-start.20 = (bf16[8,16,7680]{2,1,0:T(8,128)(2,1)}, bf16[8,16,7680]{2,1,0:T(8,128)(2,1)}, u32[]{:S(2)}, u32[]{:S(2)}) collective-permute-start(bf16[8,16,7680]{2,1,0:T(8,128)(2,1)} %get-tuple-element.269), channel_id=1, source_target_pairs={{0,16},{1,9},{2,18},{3,11},{4,20},{5,13},{6,22},{7,15},{8,24},{9,1... | collective-permute-start | bytes 5898248 | tf_op jit(solution)/shard_map/ppermute | solution.py:1355
  627.4 32.3 %collective-permute-start.29 = (f32[88,512]{1,0:T(8,128)}, f32[88,512]{1,0:T(8,128)S(1)}, u32[]{:S(2)}, u32[]{:S(2)}) collective-permute-start(f32[88,512]{1,0:T(8,128)} %get-tuple-element.368), channel_id=1, source_target_pairs={{0,1},{1,0},{2,3},{3,2},{4,5},{5,4},{6,7},{7,6},{8,9},{9,8},{10,11... | collective-permute-start | bytes 540680 | tf_op jit(solution)/shard_map/ppermute | solution.py:1355
  628.5 74.2 %collective-permute-start.21 = (bf16[16,6144]{1,0:T(8,128)(2,1)S(1)}, bf16[16,6144]{1,0:T(8,128)(2,1)}, u32[]{:S(2)}, u32[]{:S(2)}) collective-permute-start(bf16[16,6144]{1,0:T(8,128)(2,1)S(1)} %get-tuple-element.357), channel_id=1, source_target_pairs={{0,2},{1,3},{2,0},{3,1},{4,6},{5,7},{6,4},{7,5},{8,10},{9,11},{10,... | collective-permute-start | bytes 589832 | tf_op jit(solution)/shard_map/ppermute | solution.py:1355
  628.8 73.8 %collective-permute-start.22 = (bf16[16,6144]{1,0:T(8,128)(2,1)S(1)}, bf16[16,6144]{1,0:T(8,128)(2,1)}, u32[]{:S(2)}, u32[]{:S(2)}) collective-permute-start(bf16[16,6144]{1,0:T(8,128)(2,1)S(1)} %get-tuple-element.356), channel_id=1, source_target_pairs={{0,4},{1,5},{2,6},{3,7},{4,0},{5,1},{6,2},{7,3},{8,12},{9,13},{10,... | collective-permute-start | bytes 589832 | tf_op jit(solution)/shard_map/ppermute | solution.py:1355
  659.1 43.6 %collective-permute-start.19 = (bf16[4,16,11264]{2,1,0:T(8,128)(2,1)}, bf16[4,16,11264]{2,1,0:T(8,128)(2,1)}, u32[]{:S(2)}, u32[]{:S(2)}) collective-permute-start(bf16[4,16,11264]{2,1,0:T(8,128)(2,1)} %add_convert_fusion.1), channel_id=1, source_target_pairs={{0,8},{1,17},{2,10},{3,19},{4,12},{5,21},{6,14},{7,23},{8,0},{9,25... | collective-permute-start | bytes 4325384 | tf_op jit(solution)/shard_map/ppermute | solution.py:1355
  659.7 42.9 %collective-permute-start.23 = (bf16[16,6144]{1,0:T(8,128)(2,1)S(1)}, bf16[16,6144]{1,0:T(8,128)(2,1)S(1)}, u32[]{:S(2)}, u32[]{:S(2)}) collective-permute-start(bf16[16,6144]{1,0:T(8,128)(2,1)S(1)} %get-tuple-element.355), channel_id=1, source_target_pairs={{0,6},{1,7},{2,4},{3,5},{4,2},{5,3},{6,0},{7,1},{8,14},{9,15},{10,... | collective-permute-start | bytes 589832 | tf_op jit(solution)/shard_map/ppermute | solution.py:1355
  707.5 23.7 %collective-permute-start.25 = (bf16[16,11264]{1,0:T(8,128)(2,1)}, bf16[16,11264]{1,0:T(8,128)(2,1)}, u32[]{:S(2)}, u32[]{:S(2)}) collective-permute-start(bf16[16,11264]{1,0:T(8,128)(2,1)} %get-tuple-element.338), channel_id=1, source_target_pairs={{0,2},{1,3},{2,0},{3,1},{4,6},{5,7},{6,4},{7,5},{8,10},{9,11},{10,... | collective-permute-start | bytes 1081352 | tf_op jit(solution)/shard_map/ppermute | solution.py:1355
  707.9 23.3 %collective-permute-start.26 = (bf16[16,11264]{1,0:T(8,128)(2,1)}, bf16[16,11264]{1,0:T(8,128)(2,1)}, u32[]{:S(2)}, u32[]{:S(2)}) collective-permute-start(bf16[16,11264]{1,0:T(8,128)(2,1)} %get-tuple-element.340), channel_id=1, source_target_pairs={{0,4},{1,5},{2,6},{3,7},{4,0},{5,1},{6,2},{7,3},{8,12},{9,13},{10,... | collective-permute-start | bytes 1081352 | tf_op jit(solution)/shard_map/ppermute | solution.py:1355
  709.9 24.0 %collective-permute-start.27 = (bf16[16,11264]{1,0:T(8,128)(2,1)}, bf16[16,11264]{1,0:T(8,128)(2,1)}, u32[]{:S(2)}, u32[]{:S(2)}) collective-permute-start(bf16[16,11264]{1,0:T(8,128)(2,1)} %get-tuple-element.339), channel_id=1, source_target_pairs={{0,6},{1,7},{2,4},{3,5},{4,2},{5,3},{6,0},{7,1},{8,14},{9,15},{10,... | collective-permute-start | bytes 1081352 | tf_op jit(solution)/shard_map/ppermute | solution.py:1355
  729.4 13.6 %collective-permute-start.24 = (bf16[4,16,7680]{2,1,0:T(8,128)(2,1)}, bf16[4,16,7680]{2,1,0:T(8,128)(2,1)}, u32[]{:S(2)}, u32[]{:S(2)}) collective-permute-start(bf16[4,16,7680]{2,1,0:T(8,128)(2,1)} %add_convert_fusion.2), channel_id=1, source_target_pairs={{0,8},{1,17},{2,10},{3,19},{4,12},{5,21},{6,14},{7,23},{8,0},{9,25... | collective-permute-start | bytes 2949128 | tf_op jit(solution)/shard_map/ppermute | solution.py:1355
  807.2 6.3 collective-permute-start.28
  (29 other events, 252.2 us)

commit v5 on v4

--- a/solution.py
+++ b/solution.py
@@ -1885,6 +1885,11 @@
             jax.ShapeDtypeStruct((1, width), F32),
         ),
         scratch_shapes=[pltpu.VMEM((width, rows), BF), pltpu.VMEM((rows, width), F32)],
+        cost_estimate=pl.CostEstimate(
+            flops=4 * rows * width * grad_qkv.shape[1],
+            bytes_accessed=4 * width * grad_qkv.shape[1],
+            transcendentals=0,
+        ),
         compiler_params=pltpu.CompilerParams(vmem_limit_bytes=ROOM),
     )(grad_mixed, stream, gain, normed, grad_qkv, qkv_w)
     return grad_stream, grad_gain, grad_qkv_w
@@ -2062,6 +2067,7 @@
         + [Scatter(qkv_g1, ColumnBlocks(count, width, i), i) for i in range(3)]
         + [Scatter(gain_grads, own(gain_grads))],
     )
+    grad_tokens, wide1 = join(grad_tokens, wide1)
     gate_s1, up_s1 = unpack(scatter_end(wide1), shapes[:2])
     gate_s2, up_s2, out_s2, down_s2 = unpack(scatter_end(sums2), shapes)
     (qkv_s2,) = unpack(scatter_end(qkv_s2), ((count, 3 * width),))

time: 825 us -> 824 us (level)
  waiting for transfers between devices: 17.2 us -> 0.08 us
  Pallas kernels: 681 us -> 693 us
    pallas_call x10, Pallas kernels: 453 us -> 474 us  [exchange(): pl.pallas_call(kernel, name=name, out_shape=[o for p in parts for o in p....]
    ppermute x26, waiting for transfers between devices: 17.2 us -> 0.07 us  [hop(): return lax.ppermute(values, ('grp', 'key'), pairs)]
  transfers between devices with their start and end apart: 30 -> 30, of which waited for: 4 -> 0; matrix products, arithmetic and copies ran while one was open for 7% -> 7% of each run, Pallas kernels for 46% -> 54%
where the time goes in v5:
time: 824 us; the launch traced here: 818 us
  Pallas kernels  693 us (84%)
  starting transfers between devices  47.7 us (6%)
  other arithmetic  45.1 us (5%)
  local copies, waits for them, and re-layouts  21.6 us (3%)
    pallas_call x10, Pallas kernels, exchange(): pl.pallas_call(kernel, name=name, out_shape=[o for p in parts for o in p....  474 us
    pallas_call x2, Pallas kernels, feed_back(): pl.pallas_call(feed_back_kernel, name='feed_back', grid=(steps,), in_spec...  68.4 us
    pallas_call x2, Pallas kernels, attend_back(): pl.pallas_call(functools.partial(attend_back_kernel, memory is not None),...  51.5 us
    pallas_call x2, Pallas kernels, feed(): pl.pallas_call(feed_kernel, name='feed', grid=(steps,), in_specs=[VMEM, V...  39.6 us
    ppermute x26, starting transfers between devices, hop(): return lax.ppermute(values, ('grp', 'key'), pairs)  36.1 us
    pallas_call x2, Pallas kernels, attend(): pl.pallas_call(functools.partial(attend_kernel, memory is not None), name...  31.5 us
    pallas_call x2, Pallas kernels, projections_back(): pl.pallas_call(project_kernel, name='projections_back', grid=(grad_qkv.sh...  28.8 us
  transfers between devices with their start and end apart: 30, of which 0 were waited for; matrix products, arithmetic and copies ran while one was open for 7% of the time, Pallas kernels for 54%

profile of v5, /device:TPU:1, one launch (start us, length us, event | category | flops | bytes accessed | tf_op | source)
XLA Modules:
  0.0 818.5 jit_solution(9501352526754326948)
XLA Ops:
  10.4 166.5 %front.1 = (bf16[1024,3072]{1,0:T(8,128)(2,1)}, bf16[1024,128]{1,0:T(8,128)(2,1)}, bf16[512,1024]{1,0:T(8,128)(2,1)}, bf16[512,1024]{1,0:T(8,128)(2,1)}, bf16[20...) custom-call(bf16[32,1024]{1,0:T(8,128)(2,1)} %refs_0_.1, ...), custom_call_target="tpu_custom_call" | custom-call | tf_op jit(solution)/shard_map/front/pallas_call | solution.py:1325
  176.9 6.0 collective-permute-start.1
  182.8 3.4 collective-permute-start.2
  192.7 15.1 %attend.2 = (bf16[2048,256]{1,0:T(8,128)(2,1)}, f32[8,2048]{1,0:T(8,128)}) custom-call(s32[4,8]{1,0:T(4,128)} %stack.105.ranges, bf16[2048,256]{1,0:T(8,128)(2,1)} %get-tuple-element.170.refs_0_, bf16[2048,256]{1,0:T(8,128)(2,1)} %get-tuple-element.171.refs_1_.refs_5_, bf16[2048,256]{1,0:T(8,128)(2,1)} %get-tuple-element.172.refs_2_.refs_6_, ...), custom_call_target="tpu_custom_call" | custom-call | tf_op jit(solution)/shard_map/attend/pallas_call | solution.py:1543
  207.8 27.5 %to_rows_1.1.att = bf16[512,1024]{1,0:T(8,128)(2,1)} custom-call(bf16[2048,256]{1,0:T(8,128)(2,1)} %get-tuple-element.173.refs_0_.refs_2_), custom_call_target="tpu_custom_call" | custom-call | tf_op jit(solution)/shard_map/to_rows_1/pallas_call | solution.py:1325
  239.2 19.5 %feed.2 = (f32[512,1024]{1,0:T(8,128)}, f32[512,1024]{1,0:T(8,128)}, bf16[512,1024]{1,0:T(8,128)(2,1)}, f32[512,2816]{1,0:T(8,128)}, f32[512,2816]{1,0:T(8,128)}) custom-call(bf16[512,1024]{1,0:T(8,128)(2,1)} %to_rows_1.1.att, bf16[512,1024]{1,0:T(8,128)(2,1)} %get-tuple-element.176.stream, bf16[1024,1024]{1,0:T(8,128)(2,1)} %get-tuple-element.177.out_w, ...), custom_call_target="tpu_custom_call" | custom-call | tf_op jit(solution)/shard_map/feed/pallas_call | solution.py:1769
  261.2 7.9 convolution_convert_fusion.refs_0_
  270.7 44.3 %to_heads_2.1 = (bf16[2048,256]{1,0:T(8,128)(2,1)}, bf16[2048,256]{1,0:T(8,128)(2,1)}, bf16[2048,256]{1,0:T(8,128)(2,1)}, bf16[2048,256]{1,0:T(8,128)(2,1)}, bf16[2048,256]{1,0:T(8,128)(2,1)}) custom-call(bf16[512,3072]{1,0:T(8,128)(2,1)} %convolution_convert_fusion.refs_0_, s32[1,2048]{1,0:T(1,128)} %bitcast.116, ...), custom_call_target="tpu_custom_call" | custom-call | tf_op jit(solution)/shard_map/to_heads_2/pallas_call | solution.py:1325
  315.0 16.4 %attend.3 = (bf16[2048,256]{1,0:T(8,128)(2,1)}, f32[8,2048]{1,0:T(8,128)}) custom-call(s32[4,8]{1,0:T(4,128)} %stack.105.ranges, bf16[2048,256]{1,0:T(8,128)(2,1)} %get-tuple-element.187.refs_0_, bf16[2048,256]{1,0:T(8,128)(2,1)} %get-tuple-element.188.refs_1_.refs_5_, bf16[2048,256]{1,0:T(8,128)(2,1)} %get-tuple-element.189.refs_2_.refs_6_, ...), custom_call_target="tpu_custom_call" | custom-call | tf_op jit(solution)/shard_map/attend/pallas_call | solution.py:1543
  331.4 26.2 %to_rows_2.1 = (bf16[512,1024]{1,0:T(8,128)(2,1)}, bf16[1024,5632]{1,0:T(8,128)(2,1)}, bf16[1024,1024]{1,0:T(8,128)(2,1)}, bf16[2816,1024]{1,0:T(8,128)(2,1)}) custom-call(bf16[2048,256]{1,0:T(8,128)(2,1)} %get-tuple-element.195.refs_0_.refs_2_, bf16[4,32,9472]{2,1,0:T(8,128)(2,1)} %pad_maximum_fusion.refs_1_, bf16[4,32,9472]{2,1,0:T(8,128)(2,1)} %copy-done.4, ...), custom_call_target="tpu_custom_call" | custom-call | tf_op jit(solution)/shard_map/to_rows_2/pallas_call | solution.py:1325
  358.1 7.6 collective-permute-start.8
  365.7 20.0 %feed.3 = (f32[512,1024]{1,0:T(8,128)}, f32[512,1024]{1,0:T(8,128)}, bf16[512,1024]{1,0:T(8,128)(2,1)}, f32[512,2816]{1,0:T(8,128)}, f32[512,2816]{1,0:T(8,128)}) custom-call(bf16[512,1024]{1,0:T(8,128)(2,1)} %get-tuple-element.202.att, f32[512,1024]{1,0:T(8,128)} %get-tuple-element.181.stream, bf16[1024,1024]{1,0:T(8,128)(2,1)} %get-tuple-element.203.out_w, ...), custom_call_target="tpu_custom_call" | custom-call | tf_op jit(solution)/shard_map/feed/pallas_call | solution.py:1769
  386.9 34.0 %feed_back.2 = (bf16[1024,2816]{1,0:T(8,128)(2,1)}, bf16[1024,2816]{1,0:T(8,128)(2,1)}, bf16[2816,1024]{1,0:T(8,128)(2,1)}, f32[512,1024]{1,0:T(8,128)}, bf16[51...) custom-call(bf16[512,1024]{1,0:T(8,128)(2,1)} %pad_maximum_fusion.1.grad_new, ...), custom_call_target="tpu_custom_call" | custom-call | tf_op jit(solution)/shard_map/feed_back/pallas_call | solution.py:1832
  421.0 21.3 %back_to_heads_2.1 = (bf16[2048,256]{1,0:T(8,128)(2,1)}, bf16[4,16,18944]{2,1,0:T(8,128)(2,1)}, bf16[4,16,18944]{2,1,0:T(8,128)(2,1)}, bf16[8,16,18944]{2,1,0:T(8,128)(2,1)}) custom-call(bf16[512,1024]{1,0:T(8,128)(2,1)} %get-tuple-element.210.refs_0_, bf16[1024,2816]{1,0:T(8,128)(2,1)} %get-tuple-element.211.refs_1_, ...), custom_call_target="tpu_custom_call" | custom-call | tf_op jit(solution)/shard_map/back_to_heads_2/pallas_call | solution.py:1325
  443.4 3.3 collective-permute-start.11
  446.8 26.6 %attend_back.2 = (bf16[2048,256]{1,0:T(8,128)(2,1)}, bf16[2048,256]{1,0:T(8,128)(2,1)}, bf16[2048,256]{1,0:T(8,128)(2,1)}) custom-call(s32[4,8]{1,0:T(4,128)} %stack.105.ranges, bf16[2048,256]{1,0:T(8,128)(2,1)} %get-tuple-element.187.refs_0_, bf16[2048,256]{1,0:T(8,128)(2,1)} %get-tuple-element.215.refs_1_, ...), custom_call_target="tpu_custom_call" | custom-call | tf_op jit(solution)/shard_map/attend_back/pallas_call | solution.py:1633
  473.3 42.2 %back_to_rows_2.1.grad_qkv = bf16[512,3072]{1,0:T(8,128)(2,1)} custom-call(bf16[2048,256]{1,0:T(8,128)(2,1)} %get-tuple-element.217.refs_0_, bf16[2048,256]{1,0:T(8,128)(2,1)} %get-tuple-element.218.refs_1_, bf16[2048,256]{1,0:T(8,128)(2,1)} %get-tuple-element.219.refs_2_), custom_call_target="tpu_custom_call" | custom-call | tf_op jit(solution)/shard_map/back_to_rows_2/pallas_call | solution.py:1325
  517.6 3.7 add_convert_fusion
  523.2 14.7 %projections_back.2 = (bf16[1024,3072]{1,0:T(8,128)(2,1)}, f32[512,1024]{1,0:T(8,128)}, f32[1,1024]{1,0:T(1,128)}) custom-call(f32[512,1024]{1,0:T(8,128)} %get-tuple-element.225.grad_mixed, f32[512,1024]{1,0:T(8,128)} %get-tuple-element.181.stream, f32[1,1024]{1,0:T(1,128)} %bitcast.117, bf16[512,1024]{1,0:T(8,128)(2,1)} %copy-done.12, ...), custom_call_target="tpu_custom_call" | custom-call | flops 6442450944 | bytes 12582912 | tf_op jit(solution)/shard_map/projections_back/pallas_call | solution.py:1876
  537.9 12.9 %projection_sums_2.1 = (bf16[4,16,6144]{2,1,0:T(8,128)(2,1)}, bf16[4,16,6144]{2,1,0:T(8,128)(2,1)}, bf16[8,16,6144]{2,1,0:T(8,128)(2,1)}) custom-call(bf16[1024,3072]{1,0:T(8,128)(2,1)} %get-tuple-element.231.refs_0_), custom_call_target="tpu_custom_call" | custom-call | tf_op jit(solution)/shard_map/projection_sums_2/pallas_call | solution.py:1325
  551.5 4.4 collective-permute-start.13
  555.9 5.5 fusion.34
  566.1 34.3 %feed_back.3 = (bf16[1024,2816]{1,0:T(8,128)(2,1)}, bf16[1024,2816]{1,0:T(8,128)(2,1)}, bf16[2816,1024]{1,0:T(8,128)(2,1)}, f32[512,1024]{1,0:T(8,128)}, bf16[51...) custom-call(f32[512,1024]{1,0:T(8,128)} %get-tuple-element.235.grad_new, ...), custom_call_target="tpu_custom_call" | custom-call | tf_op jit(solution)/shard_map/feed_back/pallas_call | solution.py:1832
  603.8 22.4 %back_to_heads_1.1 = (bf16[2048,256]{1,0:T(8,128)(2,1)}, bf16[4,16,11264]{2,1,0:T(8,128)(2,1)}, bf16[4,16,11264]{2,1,0:T(8,128)(2,1)}, bf16[8,16,11264]{2,1,0:T(...) custom-call(bf16[512,1024]{1,0:T(8,128)(2,1)} %get-tuple-element.246.refs_0_, ...), custom_call_target="tpu_custom_call" | custom-call | tf_op jit(solution)/shard_map/back_to_heads_1/pallas_call | solution.py:1325
  634.3 25.0 %attend_back.3 = (bf16[2048,256]{1,0:T(8,128)(2,1)}, bf16[2048,256]{1,0:T(8,128)(2,1)}, bf16[2048,256]{1,0:T(8,128)(2,1)}) custom-call(s32[4,8]{1,0:T(4,128)} %stack.105.ranges, bf16[2048,256]{1,0:T(8,128)(2,1)} %get-tuple-element.170.refs_0_, bf16[2048,256]{1,0:T(8,128)(2,1)} %get-tuple-element.258.refs_1_, ...), custom_call_target="tpu_custom_call" | custom-call | tf_op jit(solution)/shard_map/attend_back/pallas_call | solution.py:1633
  660.9 2.8 add_convert_fusion.1
  667.8 39.9 %back_to_rows_1.1.grad_qkv = bf16[512,3072]{1,0:T(8,128)(2,1)} custom-call(bf16[2048,256]{1,0:T(8,128)(2,1)} %get-tuple-element.266.refs_0_, bf16[2048,256]{1,0:T(8,128)(2,1)} %get-tuple-element.267.refs_1_, bf16[2048,256]{1,0:T(8,128)(2,1)} %get-tuple-element.268.refs_2_), custom_call_target="tpu_custom_call" | custom-call | tf_op jit(solution)/shard_map/back_to_rows_1/pallas_call | solution.py:1325
  711.2 2.3 fusion.32
  715.7 2.4 collective-permute-start.27
  718.1 14.1 %projections_back.3 = (bf16[1024,3072]{1,0:T(8,128)(2,1)}, bf16[512,1024]{1,0:T(8,128)(2,1)}, f32[1,1024]{1,0:T(1,128)}) custom-call(f32[512,1024]{1,0:T(8,128)} %get-tuple-element.240.grad_mixed, bf16[512,1024]{1,0:T(8,128)(2,1)} %get-tuple-element.176.stream, f32[1,1024]{1,0:T(1,128)} %bitcast.118, bf16[512,1024]{1,0:T(8,128)(2,1)} %get-tuple-element.241.normed, ...), custom_call_target="tpu_custom_call" | custom-call | flops 6442450944 | bytes 12582912 | tf_op jit(solution)/shard_map/projections_back/pallas_call | solution.py:1876
  735.7 70.4 %back_to_owners.1 = (bf16[2,256,1024]{2,1,0:T(8,128)(2,1)}, f32[32,1024]{1,0:T(8,128)}, f32[176,512]{1,0:T(8,128)}, f32[32,1024]{1,0:T(8,128)}, f32[32,1024]{1,0...) custom-call(bf16[512,1024]{1,0:T(8,128)(2,1)} %get-tuple-element.280.refs_0_, ...), custom_call_target="tpu_custom_call" | custom-call | tf_op jit(solution)/shard_map/back_to_owners/pallas_call | solution.py:1325
  807.2 2.2 collective-permute-start.28
  (240 shorter events, 71.0 us)
Async XLA Ops:
  1.8 7.6 collective-permute-start
  176.9 58.5 %collective-permute-start.1 = (bf16[32,9472]{1,0:T(8,128)(2,1)S(1)}, bf16[32,9472]{1,0:T(8,128)(2,1)S(1)}, u32[]{:S(2)}, u32[]{:S(2)}) collective-permute-start(bf16[32,9472]{1,0:T(8,128)(2,1)S(1)} %constant_dynamic-update-slice_fusion), channel_id=1, source_target_pairs={{0,2},{1,3},{2,0},{3,1},{4,6},{5,7},{6,4},{7,5},{8,10},{9,11},{10,... | collective-permute-start | bytes 1818632 | tf_op jit(solution)/shard_map/ppermute | solution.py:1355
  182.8 52.5 %collective-permute-start.2 = (bf16[32,9472]{1,0:T(8,128)(2,1)S(1)}, bf16[32,9472]{1,0:T(8,128)(2,1)S(1)}, u32[]{:S(2)}, u32[]{:S(2)}) collective-permute-start(bf16[32,9472]{1,0:T(8,128)(2,1)S(1)} %constant_dynamic-update-slice_fusion), channel_id=1, source_target_pairs={{0,4},{1,5},{2,6},{3,7},{4,0},{5,1},{6,2},{7,3},{8,12},{9,13},{10,... | collective-permute-start | bytes 1818632 | tf_op jit(solution)/shard_map/ppermute | solution.py:1355
  186.2 49.1 %collective-permute-start.3 = (bf16[32,9472]{1,0:T(8,128)(2,1)S(1)}, bf16[32,9472]{1,0:T(8,128)(2,1)S(1)}, u32[]{:S(2)}, u32[]{:S(2)}) collective-permute-start(bf16[32,9472]{1,0:T(8,128)(2,1)S(1)} %constant_dynamic-update-slice_fusion), channel_id=1, source_target_pairs={{0,6},{1,7},{2,4},{3,5},{4,2},{5,3},{6,0},{7,1},{8,14},{9,15},{10,... | collective-permute-start | bytes 1818632 | tf_op jit(solution)/shard_map/ppermute | solution.py:1355
  237.1 32.0 %collective-permute-start.4 = (bf16[4,32,9472]{2,1,0:T(8,128)(2,1)}, bf16[4,32,9472]{2,1,0:T(8,128)(2,1)S(1)}, u32[]{:S(2)}, u32[]{:S(2)}) collective-permute-start(bf16[4,32,9472]{2,1,0:T(8,128)(2,1)} %pad_maximum_fusion.refs_1_), channel_id=1, source_target_pairs={{0,8},{1,17},{2,10},{3,19},{4,12},{5,21},{6,14},{7,23},{8,0},{9,25... | collective-permute-start | bytes 7274504 | tf_op jit(solution)/shard_map/ppermute | solution.py:1355
  269.1 45.8 %copy-start.4 = (bf16[4,32,9472]{2,1,0:T(8,128)(2,1)}, bf16[4,32,9472]{2,1,0:T(8,128)(2,1)S(1)}, u32[]{:S(2)}) copy-start(bf16[4,32,9472]{2,1,0:T(8,128)(2,1)S(1)} %collective-permute-done.4.refs_2_) | copy-start | bytes 7274500
  269.1 62.2 %collective-permute-start.5 = (bf16[4,32,9472]{2,1,0:T(8,128)(2,1)}, bf16[4,32,9472]{2,1,0:T(8,128)(2,1)}, u32[]{:S(2)}, u32[]{:S(2)}) collective-permute-start(bf16[4,32,9472]{2,1,0:T(8,128)(2,1)} %pad_maximum_fusion.refs_1_), channel_id=1, source_target_pairs={{0,16},{1,9},{2,18},{3,11},{4,20},{5,13},{6,22},{7,15},{8,24},{9,1... | collective-permute-start | bytes 7274504 | tf_op jit(solution)/shard_map/ppermute | solution.py:1355
  269.5 61.9 %collective-permute-start.6 = (bf16[4,32,9472]{2,1,0:T(8,128)(2,1)S(1)}, bf16[4,32,9472]{2,1,0:T(8,128)(2,1)}, u32[]{:S(2)}, u32[]{:S(2)}) collective-permute-start(bf16[4,32,9472]{2,1,0:T(8,128)(2,1)S(1)} %collective-permute-done.4.refs_2_), channel_id=1, source_target_pairs={{0,16},{1,9},{2,18},{3,11},{4,20},{5,13},{6,22},{7,15},{8,24},{9,1... | collective-permute-start | bytes 7274504 | tf_op jit(solution)/shard_map/ppermute | solution.py:1355
  357.7 28.1 %collective-permute-start.7 = (bf16[256,1024]{1,0:T(8,128)(2,1)S(1)}, bf16[256,1024]{1,0:T(8,128)(2,1)S(1)}, u32[]{:S(2)}, u32[]{:S(2)}) collective-permute-start(bf16[256,1024]{1,0:T(8,128)(2,1)S(1)} %get-tuple-element.363), channel_id=1, source_target_pairs={{0,4},{1,0},{2,5},{3,1},{4,6},{5,2},{6,7},{7,3},{8,12},{9,8},{10,1... | collective-permute-start | bytes 1572872 | tf_op jit(solution)/shard_map/ppermute | solution.py:1361
  358.1 27.7 %collective-permute-start.8 = (bf16[256,1024]{1,0:T(8,128)(2,1)S(1)}, bf16[256,1024]{1,0:T(8,128)(2,1)S(1)}, u32[]{:S(2)}, u32[]{:S(2)}) collective-permute-start(bf16[256,1024]{1,0:T(8,128)(2,1)S(1)} %get-tuple-element.364), channel_id=1, source_target_pairs={{0,0},{1,4},{2,1},{3,5},{4,2},{5,6},{6,3},{7,7},{8,8},{9,12},{10,9... | collective-permute-start | bytes 1572872 | tf_op jit(solution)/shard_map/ppermute | solution.py:1361
  442.3 74.4 %collective-permute-start.9 = (bf16[8,16,18944]{2,1,0:T(8,128)(2,1)}, bf16[8,16,18944]{2,1,0:T(8,128)(2,1)}, u32[]{:S(2)}, u32[]{:S(2)}) collective-permute-start(bf16[8,16,18944]{2,1,0:T(8,128)(2,1)} %get-tuple-element.222), channel_id=1, source_target_pairs={{0,16},{1,9},{2,18},{3,11},{4,20},{5,13},{6,22},{7,15},{8,24},{9,1... | collective-permute-start | bytes 14549000 | tf_op jit(solution)/shard_map/ppermute | solution.py:1355
  443.1 72.4 %collective-permute-start.10 = (bf16[256,1024]{1,0:T(8,128)(2,1)S(1)}, bf16[256,1024]{1,0:T(8,128)(2,1)S(1)}, u32[]{:S(2)}, u32[]{:S(2)}) collective-permute-start(bf16[256,1024]{1,0:T(8,128)(2,1)S(1)} %get-tuple-element.359), channel_id=1, source_target_pairs={{4,0},{0,1},{5,2},{1,3},{6,4},{2,5},{7,6},{3,7},{12,8},{8,9},{13,1... | collective-permute-start | bytes 1572872 | tf_op jit(solution)/shard_map/ppermute | solution.py:1361
  443.4 72.1 %collective-permute-start.11 = (bf16[256,1024]{1,0:T(8,128)(2,1)S(1)}, bf16[256,1024]{1,0:T(8,128)(2,1)S(1)}, u32[]{:S(2)}, u32[]{:S(2)}) collective-permute-start(bf16[256,1024]{1,0:T(8,128)(2,1)S(1)} %get-tuple-element.360), channel_id=1, source_target_pairs={{0,0},{4,1},{1,2},{5,3},{2,4},{6,5},{3,6},{7,7},{8,8},{12,9},{9,10... | collective-permute-start | bytes 1572872 | tf_op jit(solution)/shard_map/ppermute | solution.py:1361
  521.3 30.2 %collective-permute-start.12 = (bf16[4,16,18944]{2,1,0:T(8,128)(2,1)}, bf16[4,16,18944]{2,1,0:T(8,128)(2,1)}, u32[]{:S(2)}, u32[]{:S(2)}) collective-permute-start(bf16[4,16,18944]{2,1,0:T(8,128)(2,1)} %add_convert_fusion), channel_id=1, source_target_pairs={{0,8},{1,17},{2,10},{3,19},{4,12},{5,21},{6,14},{7,23},{8,0},{9,25... | collective-permute-start | bytes 7274504 | tf_op jit(solution)/shard_map/ppermute | solution.py:1355
  551.5 49.0 %collective-permute-start.13 = (bf16[8,16,6144]{2,1,0:T(8,128)(2,1)}, bf16[8,16,6144]{2,1,0:T(8,128)(2,1)S(1)}, u32[]{:S(2)}, u32[]{:S(2)}) collective-permute-start(bf16[8,16,6144]{2,1,0:T(8,128)(2,1)} %get-tuple-element.245), channel_id=1, source_target_pairs={{0,16},{1,9},{2,18},{3,11},{4,20},{5,13},{6,22},{7,15},{8,24},{9,1... | collective-permute-start | bytes 4718600 | tf_op jit(solution)/shard_map/ppermute | solution.py:1355
  562.6 63.6 %collective-permute-start.14 = (bf16[16,18944]{1,0:T(8,128)(2,1)}, bf16[16,18944]{1,0:T(8,128)(2,1)}, u32[]{:S(2)}, u32[]{:S(2)}) collective-permute-start(bf16[16,18944]{1,0:T(8,128)(2,1)} %get-tuple-element.347), channel_id=1, source_target_pairs={{0,2},{1,3},{2,0},{3,1},{4,6},{5,7},{6,4},{7,5},{8,10},{9,11},{10,... | collective-permute-start | bytes 1818632 | tf_op jit(solution)/shard_map/ppermute | solution.py:1355
  563.8 63.9 %collective-permute-start.15 = (bf16[16,18944]{1,0:T(8,128)(2,1)}, bf16[16,18944]{1,0:T(8,128)(2,1)}, u32[]{:S(2)}, u32[]{:S(2)}) collective-permute-start(bf16[16,18944]{1,0:T(8,128)(2,1)} %get-tuple-element.346), channel_id=1, source_target_pairs={{0,4},{1,5},{2,6},{3,7},{4,0},{5,1},{6,2},{7,3},{8,12},{9,13},{10,... | collective-permute-start | bytes 1818632 | tf_op jit(solution)/shard_map/ppermute | solution.py:1355
  564.1 63.6 %collective-permute-start.16 = (bf16[16,18944]{1,0:T(8,128)(2,1)}, bf16[16,18944]{1,0:T(8,128)(2,1)}, u32[]{:S(2)}, u32[]{:S(2)}) collective-permute-start(bf16[16,18944]{1,0:T(8,128)(2,1)} %get-tuple-element.345), channel_id=1, source_target_pairs={{0,6},{1,7},{2,4},{3,5},{4,2},{5,3},{6,0},{7,1},{8,14},{9,15},{10,... | collective-permute-start | bytes 1818632 | tf_op jit(solution)/shard_map/ppermute | solution.py:1355
  566.1 34.4 %copy-start.18 = (bf16[4,16,6144]{2,1,0:T(8,128)(2,1)S(1)}, bf16[4,16,6144]{2,1,0:T(8,128)(2,1)}, u32[]{:S(2)}) copy-start(bf16[4,16,6144]{2,1,0:T(8,128)(2,1)} %get-tuple-element.257) | copy-start | bytes 2359300
  601.8 25.9 %collective-permute-start.17 = (bf16[4,16,6144]{2,1,0:T(8,128)(2,1)}, bf16[4,16,6144]{2,1,0:T(8,128)(2,1)S(1)}, u32[]{:S(2)}, u32[]{:S(2)}) collective-permute-start(bf16[4,16,6144]{2,1,0:T(8,128)(2,1)} %add_convert_fusion.3), channel_id=1, source_target_pairs={{0,8},{1,17},{2,10},{3,19},{4,12},{5,21},{6,14},{7,23},{8,0},{9,25... | collective-permute-start | bytes 2359304 | tf_op jit(solution)/shard_map/ppermute | solution.py:1355
  626.1 34.7 %collective-permute-start.18 = (bf16[8,16,11264]{2,1,0:T(8,128)(2,1)}, bf16[8,16,11264]{2,1,0:T(8,128)(2,1)}, u32[]{:S(2)}, u32[]{:S(2)}) collective-permute-start(bf16[8,16,11264]{2,1,0:T(8,128)(2,1)} %get-tuple-element.265), channel_id=1, source_target_pairs={{0,16},{1,9},{2,18},{3,11},{4,20},{5,13},{6,22},{7,15},{8,24},{9,1... | collective-permute-start | bytes 8650760 | tf_op jit(solution)/shard_map/ppermute | solution.py:1355
  626.2 81.5 %collective-permute-start.20 = (bf16[8,16,7680]{2,1,0:T(8,128)(2,1)}, bf16[8,16,7680]{2,1,0:T(8,128)(2,1)}, u32[]{:S(2)}, u32[]{:S(2)}) collective-permute-start(bf16[8,16,7680]{2,1,0:T(8,128)(2,1)} %get-tuple-element.274), channel_id=1, source_target_pairs={{0,16},{1,9},{2,18},{3,11},{4,20},{5,13},{6,22},{7,15},{8,24},{9,1... | collective-permute-start | bytes 5898248 | tf_op jit(solution)/shard_map/ppermute | solution.py:1355
  631.3 34.1 %collective-permute-start.29 = (f32[88,512]{1,0:T(8,128)}, f32[88,512]{1,0:T(8,128)S(1)}, u32[]{:S(2)}, u32[]{:S(2)}) collective-permute-start(f32[88,512]{1,0:T(8,128)} %get-tuple-element.378), channel_id=1, source_target_pairs={{0,1},{1,0},{2,3},{3,2},{4,5},{5,4},{6,7},{7,6},{8,9},{9,8},{10,11... | collective-permute-start | bytes 540680 | tf_op jit(solution)/shard_map/ppermute | solution.py:1355
  631.9 75.8 %collective-permute-start.21 = (bf16[16,6144]{1,0:T(8,128)(2,1)S(1)}, bf16[16,6144]{1,0:T(8,128)(2,1)}, u32[]{:S(2)}, u32[]{:S(2)}) collective-permute-start(bf16[16,6144]{1,0:T(8,128)(2,1)S(1)} %get-tuple-element.367), channel_id=1, source_target_pairs={{0,2},{1,3},{2,0},{3,1},{4,6},{5,7},{6,4},{7,5},{8,10},{9,11},{10,... | collective-permute-start | bytes 589832 | tf_op jit(solution)/shard_map/ppermute | solution.py:1355
  632.3 75.4 %collective-permute-start.22 = (bf16[16,6144]{1,0:T(8,128)(2,1)S(1)}, bf16[16,6144]{1,0:T(8,128)(2,1)}, u32[]{:S(2)}, u32[]{:S(2)}) collective-permute-start(bf16[16,6144]{1,0:T(8,128)(2,1)S(1)} %get-tuple-element.366), channel_id=1, source_target_pairs={{0,4},{1,5},{2,6},{3,7},{4,0},{5,1},{6,2},{7,3},{8,12},{9,13},{10,... | collective-permute-start | bytes 589832 | tf_op jit(solution)/shard_map/ppermute | solution.py:1355
  663.7 44.1 %collective-permute-start.19 = (bf16[4,16,11264]{2,1,0:T(8,128)(2,1)}, bf16[4,16,11264]{2,1,0:T(8,128)(2,1)}, u32[]{:S(2)}, u32[]{:S(2)}) collective-permute-start(bf16[4,16,11264]{2,1,0:T(8,128)(2,1)} %add_convert_fusion.1), channel_id=1, source_target_pairs={{0,8},{1,17},{2,10},{3,19},{4,12},{5,21},{6,14},{7,23},{8,0},{9,25... | collective-permute-start | bytes 4325384 | tf_op jit(solution)/shard_map/ppermute | solution.py:1355
  665.4 42.3 %collective-permute-start.23 = (bf16[16,6144]{1,0:T(8,128)(2,1)S(1)}, bf16[16,6144]{1,0:T(8,128)(2,1)S(1)}, u32[]{:S(2)}, u32[]{:S(2)}) collective-permute-start(bf16[16,6144]{1,0:T(8,128)(2,1)S(1)} %get-tuple-element.365), channel_id=1, source_target_pairs={{0,6},{1,7},{2,4},{3,5},{4,2},{5,3},{6,0},{7,1},{8,14},{9,15},{10,... | collective-permute-start | bytes 589832 | tf_op jit(solution)/shard_map/ppermute | solution.py:1355
  710.5 24.3 %collective-permute-start.24 = (bf16[4,16,7680]{2,1,0:T(8,128)(2,1)S(1)}, bf16[4,16,7680]{2,1,0:T(8,128)(2,1)S(1)}, u32[]{:S(2)}, u32[]{:S(2)}) collective-permute-start(bf16[4,16,7680]{2,1,0:T(8,128)(2,1)S(1)} %add_convert_fusion.2), channel_id=1, source_target_pairs={{0,8},{1,17},{2,10},{3,19},{4,12},{5,21},{6,14},{7,23},{8,0},{9,25... | collective-permute-start | bytes 2949128 | tf_op jit(solution)/shard_map/ppermute | solution.py:1355
  714.5 95.0 %collective-permute-start.25 = (bf16[16,11264]{1,0:T(8,128)(2,1)}, bf16[16,11264]{1,0:T(8,128)(2,1)}, u32[]{:S(2)}, u32[]{:S(2)}) collective-permute-start(bf16[16,11264]{1,0:T(8,128)(2,1)} %get-tuple-element.350), channel_id=1, source_target_pairs={{0,2},{1,3},{2,0},{3,1},{4,6},{5,7},{6,4},{7,5},{8,10},{9,11},{10,... | collective-permute-start | bytes 1081352 | tf_op jit(solution)/shard_map/ppermute | solution.py:1355
  714.5 95.0 %collective-permute-start.26 = (bf16[16,11264]{1,0:T(8,128)(2,1)}, bf16[16,11264]{1,0:T(8,128)(2,1)}, u32[]{:S(2)}, u32[]{:S(2)}) collective-permute-start(bf16[16,11264]{1,0:T(8,128)(2,1)} %get-tuple-element.349), channel_id=1, source_target_pairs={{0,4},{1,5},{2,6},{3,7},{4,0},{5,1},{6,2},{7,3},{8,12},{9,13},{10,... | collective-permute-start | bytes 1081352 | tf_op jit(solution)/shard_map/ppermute | solution.py:1355
  715.7 93.8 %collective-permute-start.27 = (bf16[16,11264]{1,0:T(8,128)(2,1)}, bf16[16,11264]{1,0:T(8,128)(2,1)}, u32[]{:S(2)}, u32[]{:S(2)}) collective-permute-start(bf16[16,11264]{1,0:T(8,128)(2,1)} %get-tuple-element.348), channel_id=1, source_target_pairs={{0,6},{1,7},{2,4},{3,5},{4,2},{5,3},{6,0},{7,1},{8,14},{9,15},{10,... | collective-permute-start | bytes 1081352 | tf_op jit(solution)/shard_map/ppermute | solution.py:1355
  807.2 7.6 collective-permute-start.28
  (31 other events, 252.8 us)
